TPU v7x, 32 devices: a whole 2x2x4 slice. The times are simulated.
32 devices in a mesh: ctx: 16 (over z, y, x), tp: 2 (over core).
Axes of the slice: x: 2, y: 2, z: 4, core: 2. Of those that a mesh axis runs over, the one named last changes fastest.
Arguments:
- hyena_in: bfloat16 [4096, 3, 4096], P('ctx', None, 'tp'), may hold values from -6 to 6
- filters: float32 [128, 4096], P(None, 'tp'), may hold values from -0.5 to 0.5
- attn_in: bfloat16 [4096, 3, 4096], P('ctx', None, 'tp'), may hold values from -18.5 to 18.5
- out_weight: bfloat16 [4096, 4096], P('tp', 'ctx'), may hold values from -0.125 to 0.125
- attn_weight: bfloat16 [4096, 4096], P('tp', 'ctx'), may hold values from -0.125 to 0.125
Outputs:
- block_out: bfloat16 [4096, 4096], P('ctx', 'tp')
- attn_block: bfloat16 [4096, 4096], P('ctx', 'tp')
All inputs are finite; a program needn't handle non-finite values.
Results may differ from a plain program's by a relative error of at most 0.014.
Values may be sent and summed in bfloat16 or wider, within the bound.
No kernel may reach another device: no remote copies, remote signals or barrier semaphores. Data moves between devices by JAX's collectives and lax.ppermute only.
A program may use at most 128 MiB of HBM per device.

v0:
```python
import math

import jax
import jax.numpy as jnp
from jax import lax
from jax.sharding import PartitionSpec as P

HEAD_DIM = 128
WINDOW = 2048


def from_behind(block, axis, distance):
    devices = range(lax.axis_size(axis))
    route = [(i - distance, i) for i in devices if i - distance in devices]
    return lax.ppermute(block, axis, route)


def depthwise(padded, filters):
    taps = filters.shape[0]
    length = padded.shape[0] - taps + 1

    def add_tap(index, total):
        window_rows = lax.dynamic_slice_in_dim(
            padded, (taps - 1 - index).astype(jnp.int32), length, 0
        )
        return total + filters[index][None, :] * window_rows

    return lax.fori_loop(0, taps, add_tap, jnp.zeros((length, padded.shape[1]), jnp.float32))


def head_attention(queries, keys_all, values_all, first_query, first_key):
    scores = lax.dot_general(
        queries, keys_all, (((1,), (1,)), ((), ())), preferred_element_type=jnp.float32
    )
    scores = scores * (1.0 / math.sqrt(HEAD_DIM))
    query_pos = first_query + lax.iota(jnp.int32, queries.shape[0])
    key_pos = first_key + lax.iota(jnp.int32, keys_all.shape[0])
    valid = (
        (key_pos[None, :] <= query_pos[:, None])
        & (key_pos[None, :] > query_pos[:, None] - WINDOW)
        & (key_pos[None, :] >= 0)
    )
    scores = jnp.where(valid, scores, -jnp.inf)
    top = jnp.max(scores, axis=1, keepdims=True)
    weights = jnp.exp(scores - top)
    total = jnp.sum(weights, axis=1, keepdims=True)
    probs = weights.astype(jnp.bfloat16)
    return jnp.dot(probs, values_all, preferred_element_type=jnp.float32) / total


def split_heads(array):
    return array.reshape(array.shape[0], -1, HEAD_DIM).transpose(1, 0, 2)


def per_device(hyena_in, filters, attn_in, out_weight, attn_weight):
    rows = hyena_in.shape[0]
    width = hyena_in.shape[2]
    taps = filters.shape[0]
    device_index = lax.axis_index("ctx")
    product = (hyena_in[:, 0].astype(jnp.float32) * hyena_in[:, 2].astype(jnp.float32)).astype(
        jnp.bfloat16
    )
    rim = from_behind(product[rows - taps + 1 :], "ctx", 1)
    inner = depthwise(product.astype(jnp.float32), filters)
    edge = depthwise(jnp.concatenate([rim, product[: taps - 1]], 0).astype(jnp.float32), filters)
    filtered = jnp.concatenate([edge, inner], 0)
    hyena_act = (hyena_in[:, 1].astype(jnp.float32) * filtered).astype(jnp.bfloat16)
    hyena_terms = jnp.dot(
        hyena_act,
        lax.all_gather(out_weight, "ctx", axis=1, tiled=True),
        preferred_element_type=jnp.float32,
    )
    queries = attn_in[:, 0]
    pairs = attn_in[:, 1:]
    blocks = WINDOW // rows

    def advance(carry, unused):
        moved = from_behind(carry, "ctx", 1)
        return (moved, moved)

    unused_last, earlier = lax.scan(advance, pairs, None, length=blocks)
    earlier = earlier[::-1].reshape(blocks * rows, 2, width)
    window_pairs = jnp.concatenate([earlier, pairs], 0)
    first_query = device_index * rows
    first_key = (device_index - blocks) * rows
    attended = lax.map(
        lambda operands: head_attention(
            operands[0], operands[1], operands[2], first_query, first_key
        ),
        (split_heads(queries), split_heads(window_pairs[:, 0]), split_heads(window_pairs[:, 1])),
    )
    attended = attended.transpose(1, 0, 2).reshape(rows, width).astype(jnp.bfloat16)
    attn_terms = jnp.dot(
        attended,
        lax.all_gather(attn_weight, "ctx", axis=1, tiled=True),
        preferred_element_type=jnp.float32,
    )
    hyena_sum, attn_sum = (
        lax.psum_scatter(
            hyena_terms.astype(jnp.bfloat16), "tp", scatter_dimension=1, tiled=True
        ).astype(jnp.float32),
        lax.psum_scatter(
            attn_terms.astype(jnp.bfloat16), "tp", scatter_dimension=1, tiled=True
        ).astype(jnp.float32),
    )
    return (hyena_sum.astype(jnp.bfloat16), attn_sum.astype(jnp.bfloat16))


def solution(mesh):
    in_specs = (
        P("ctx", None, "tp"),
        P(None, "tp"),
        P("ctx", None, "tp"),
        P("tp", "ctx"),
        P("tp", "ctx"),
    )
    out_specs = (P("ctx", "tp"), P("ctx", "tp"))
    return jax.shard_map(
        per_device, mesh=mesh, in_specs=in_specs, out_specs=out_specs, check_vma=False
    )
```

profile of v0, /device:TPU:0, one launch (start us, length us, event | category | flops | bytes accessed | tf_op | source)
XLA Modules:
  0.0 1344.4 jit_solution(12785828391453042803)
XLA Ops:
  11.1 5.6 collective-permute-start.1
  16.8 176.4 %while.59 = (s32[]{:T(128)}, f32[129,2048]{1,0:T(8,128)S(1)}, f32[128,2048]{1,0:T(8,128)}, f32[256,2048]{1,0:T(8,128)S(1)}, s32[]{:T(128)}, /*index=5*/s32[]{:T(128)}, s32[]{:T(128)}, s32[]{:T(128)}) while((s32[]{:T(128)}, f32[129,2048]{1,0:T(8,128)S(1)}, f32[128,2048]{1,0:T(8,128)}, f32[256,2048]{1,0:T(8,128)S(1)}, s32[]{:T(128)}, ...), condition=%wide.region_3.0_spmd.clone, body=%wide.region_2.0_spmd.clone.sunk | while | flops 792583 | bytes 3195029 | solution.py:28
  203.3 556.3 %while.56 = (s32[]{:T(128)}, bf16[256,2,2048]{2,1,0:T(2,128)(2,1)}, bf16[8,256,2,2048]{3,2,1,0:T(2,128)(2,1)}, s32[]{:T(128)}) while((s32[]{:T(128)}, bf16[256,2,2048]{2,1,0:T(2,128)(2,1)}, bf16[8,256,2,2048]{3,2,1,0:T(2,128)(2,1)}, s32[]{:T(128)}) %tuple.130), condition=%wide.region_6.7_spmd, body=%wide.region_5.6_spmd.sunk | while | flops 2 | bytes 16777320 | solution.py:81
  206.0 44.8 %collective-permute-done = bf16[256,2,2048]{2,1,0:T(2,128)(2,1)S(1)} collective-permute-done((bf16[256,2,2048]{2,1,0:T(2,128)(2,1)}, bf16[256,2,2048]{2,1,0:T(2,128)(2,1)S(1)}, u32[]{:S(2)}, u32[]{:S(2)}) %collective-permute-start) | collective-permute-done | bytes 2097184 | tf_op jit(solution)/shard_map/while/body/eval_jaxpr/ppermute | solution.py:15
  254.9 4.4 collective-permute-start
  259.3 44.0 %collective-permute-done = bf16[256,2,2048]{2,1,0:T(2,128)(2,1)S(1)} collective-permute-done((bf16[256,2,2048]{2,1,0:T(2,128)(2,1)}, bf16[256,2,2048]{2,1,0:T(2,128)(2,1)S(1)}, u32[]{:S(2)}, u32[]{:S(2)}) %collective-permute-start) | collective-permute-done | bytes 2097184 | tf_op jit(solution)/shard_map/while/body/eval_jaxpr/ppermute | solution.py:15
  311.8 52.0 %collective-permute-done = bf16[256,2,2048]{2,1,0:T(2,128)(2,1)S(1)} collective-permute-done((bf16[256,2,2048]{2,1,0:T(2,128)(2,1)}, bf16[256,2,2048]{2,1,0:T(2,128)(2,1)S(1)}, u32[]{:S(2)}, u32[]{:S(2)}) %collective-permute-start) | collective-permute-done | bytes 2097184 | tf_op jit(solution)/shard_map/while/body/eval_jaxpr/ppermute | solution.py:15
  367.9 71.2 %collective-permute-start = (bf16[256,2,2048]{2,1,0:T(2,128)(2,1)}, bf16[256,2,2048]{2,1,0:T(2,128)(2,1)S(1)}, u32[]{:S(2)}, u32[]{:S(2)}) collective-permute-start(bf16[256,2,2048]{2,1,0:T(2,128)(2,1)} %get-tuple-element.591), channel_id=1, source_target_pairs={{0,2},{2,4},{4,6},{6,8},{8,10},{10,12},{12,14},{14,16},{16,18},{18... | collective-permute-start | bytes 6291464 | tf_op jit(solution)/shard_map/while/body/eval_jaxpr/ppermute | solution.py:15
  439.2 89.5 %collective-permute-done = bf16[256,2,2048]{2,1,0:T(2,128)(2,1)S(1)} collective-permute-done((bf16[256,2,2048]{2,1,0:T(2,128)(2,1)}, bf16[256,2,2048]{2,1,0:T(2,128)(2,1)S(1)}, u32[]{:S(2)}, u32[]{:S(2)}) %collective-permute-start) | collective-permute-done | bytes 2097184 | tf_op jit(solution)/shard_map/while/body/eval_jaxpr/ppermute | solution.py:15
  537.2 44.3 %collective-permute-done = bf16[256,2,2048]{2,1,0:T(2,128)(2,1)S(1)} collective-permute-done((bf16[256,2,2048]{2,1,0:T(2,128)(2,1)}, bf16[256,2,2048]{2,1,0:T(2,128)(2,1)S(1)}, u32[]{:S(2)}, u32[]{:S(2)}) %collective-permute-start) | collective-permute-done | bytes 2097184 | tf_op jit(solution)/shard_map/while/body/eval_jaxpr/ppermute | solution.py:15
  585.7 5.4 collective-permute-start
  591.1 43.9 %collective-permute-done = bf16[256,2,2048]{2,1,0:T(2,128)(2,1)S(1)} collective-permute-done((bf16[256,2,2048]{2,1,0:T(2,128)(2,1)}, bf16[256,2,2048]{2,1,0:T(2,128)(2,1)S(1)}, u32[]{:S(2)}, u32[]{:S(2)}) %collective-permute-start) | collective-permute-done | bytes 2097184 | tf_op jit(solution)/shard_map/while/body/eval_jaxpr/ppermute | solution.py:15
  639.1 5.3 collective-permute-start
  644.4 42.1 %collective-permute-done = bf16[256,2,2048]{2,1,0:T(2,128)(2,1)S(1)} collective-permute-done((bf16[256,2,2048]{2,1,0:T(2,128)(2,1)}, bf16[256,2,2048]{2,1,0:T(2,128)(2,1)S(1)}, u32[]{:S(2)}, u32[]{:S(2)}) %collective-permute-start) | collective-permute-done | bytes 2097184 | tf_op jit(solution)/shard_map/while/body/eval_jaxpr/ppermute | solution.py:15
  690.6 40.0 %collective-permute-start = (bf16[256,2,2048]{2,1,0:T(2,128)(2,1)}, bf16[256,2,2048]{2,1,0:T(2,128)(2,1)S(1)}, u32[]{:S(2)}, u32[]{:S(2)}) collective-permute-start(bf16[256,2,2048]{2,1,0:T(2,128)(2,1)} %get-tuple-element.591), channel_id=1, source_target_pairs={{0,2},{2,4},{4,6},{6,8},{8,10},{10,12},{12,14},{14,16},{16,18},{18... | collective-permute-start | bytes 6291464 | tf_op jit(solution)/shard_map/while/body/eval_jaxpr/ppermute | solution.py:15
  730.6 24.9 %collective-permute-done = bf16[256,2,2048]{2,1,0:T(2,128)(2,1)S(1)} collective-permute-done((bf16[256,2,2048]{2,1,0:T(2,128)(2,1)}, bf16[256,2,2048]{2,1,0:T(2,128)(2,1)S(1)}, u32[]{:S(2)}, u32[]{:S(2)}) %collective-permute-start) | collective-permute-done | bytes 2097184 | tf_op jit(solution)/shard_map/while/body/eval_jaxpr/ppermute | solution.py:15
  759.6 14.3 %rev.3 = bf16[8,256,2,2048]{3,2,1,0:T(2,128)(2,1)} reverse(bf16[8,256,2,2048]{3,2,1,0:T(2,128)(2,1)} %get-tuple-element.330), dimensions={0} | reverse | bytes 33554432 | tf_op jit(solution)/shard_map/rev | solution.py:82
  773.9 41.1 %copy.16 = bf16[2048,2,2048]{0,2,1:T(8,128)(2,1)} copy(bf16[2048,2,2048]{2,1,0:T(2,128)(2,1)} %bitcast.65) | data formatting | bytes 33554432 | tf_op jit(solution)/shard_map/reshape | solution.py:82
  817.4 14.1 %pad_maximum_fusion = (bf16[2304,1,2048]{0,2,1:T(8,128)(2,1)}, bf16[2304,1,2048]{0,2,1:T(8,128)(2,1)}) fusion(bf16[256,2,2048]{0,2,1:T(8,128)(2,1)S(1)} %copy-done, bf16[2048,2,2048]{0,2,1:T(8,128)(2,1)} %copy.16), kind=kLoop, calls=%fused_computation.30 | loop fusion | flops 37748736 | bytes 37748736 | tf_op jit(solution)/shard_map/concatenate | solution.py:83
  831.5 78.6 %while.57 = (s32[]{:T(128)}, bf16[16,256,128]{1,2,0:T(8,128)(2,1)}, s32[]{:T(128)}, s32[]{:T(128)}, bf16[16,256,128]{1,2,0:T(8,128)(2,1)}, /*index=5*/bf16[16,23...) while((s32[]{:T(128)}, bf16[16,256,128]{1,2,0:T(8,128)(2,1)}, s32[]{:T(128)}, s32[]{:T(128)}, ...), condition=%wide.region_10.11_spmd, body=%wide.region_7.10_spmd.sunk | while | flops 308550400 | bytes 8685153 | solution.py:86
  912.8 12.0 convolution_convert_fusion
  924.9 332.0 %while.58 = (s32[]{:T(128)}, f32[127,2048]{1,0:T(8,128)S(1)}, f32[128,2048]{1,0:T(8,128)}, f32[254,2048]{1,0:T(8,128)}, s32[]{:T(128)}, /*index=5*/s32[]{:T(128)}, s32[]{:T(128)}, s32[]{:T(128)}) while((s32[]{:T(128)}, f32[127,2048]{1,0:T(8,128)S(1)}, f32[128,2048]{1,0:T(8,128)}, f32[254,2048]{1,0:T(8,128)}, s32[]{:T(128)}, ...), condition=%wide.region_1.0_spmd.clone, body=%wide.region_0.0_spmd.clone.sunk | while | flops 780295 | bytes 3145877 | solution.py:28
  1257.0 11.9 convolution_convert_fusion.1
  1268.9 68.9 %reduce-scatter.3.cloned.1.call-done = bf16[256,2048]{1,0:T(8,128)(2,1)} async-done(((bf16[256,4096]{1,0:T(8,128)(2,1)}), bf16[256,2048]{1,0:T(8,128)(2,1)}) %reduce-scatter.3.cloned.1.call-update) | async-done | bytes 1048592 | tf_op jit(solution)/shard_map/reduce_scatter | solution.py:99
  (687 shorter events, 644.2 us)
Async XLA Ops:
  7.2 905.6 %all-gather.5.cloned.1.call-start = ((), (), s32[]{:S(2)}) async-start(), calls=%async_computation.4 | async-start | bytes 17825792 | tf_op jit(solution)/shard_map/all_gather | solution.py:95
  7.9 1249.1 %all-gather.3.cloned.1.call-start = ((), (), s32[]{:S(2)}) async-start(), calls=%async_computation.2 | async-start | bytes 17825792 | tf_op jit(solution)/shard_map/all_gather | solution.py:70
  11.1 899.1 %collective-permute-start.1 = (bf16[127,2048]{1,0:T(8,128)(2,1)}, bf16[127,2048]{1,0:T(8,128)(2,1)}, u32[]{:S(2)}, u32[]{:S(2)}) collective-permute-start(bf16[127,2048]{1,0:T(8,128)(2,1)} %get-tuple-element.416), channel_id=1, source_target_pairs={{0,2},{2,4},{4,6},{6,8},{8,10},{10,12},{12,14},{14,16},{16,18},{18... | collective-permute-start | bytes 1560584 | tf_op jit(solution)/shard_map/ppermute | solution.py:15
  16.7 1252.2 %reduce-scatter.5.cloned.1.call-start = ((), (), s32[]{:S(2)}) async-start(), calls=%async_computation.5 | async-start | bytes 3145728 | tf_op jit(solution)/shard_map/reduce_scatter | solution.py:102
  203.3 47.5 %collective-permute-start = (bf16[256,2,2048]{2,1,0:T(2,128)(2,1)}, bf16[256,2,2048]{2,1,0:T(2,128)(2,1)S(1)}, u32[]{:S(2)}, u32[]{:S(2)}) collective-permute-start(bf16[256,2,2048]{2,1,0:T(2,128)(2,1)} %get-tuple-element.591), channel_id=1, source_target_pairs={{0,2},{2,4},{4,6},{6,8},{8,10},{10,12},{12,14},{14,16},{16,18},{18... | collective-permute-start | bytes 6291464 | tf_op jit(solution)/shard_map/while/body/eval_jaxpr/ppermute | solution.py:15
  254.9 48.4 %collective-permute-start = (bf16[256,2,2048]{2,1,0:T(2,128)(2,1)}, bf16[256,2,2048]{2,1,0:T(2,128)(2,1)S(1)}, u32[]{:S(2)}, u32[]{:S(2)}) collective-permute-start(bf16[256,2,2048]{2,1,0:T(2,128)(2,1)} %get-tuple-element.591), channel_id=1, source_target_pairs={{0,2},{2,4},{4,6},{6,8},{8,10},{10,12},{12,14},{14,16},{16,18},{18... | collective-permute-start | bytes 6291464 | tf_op jit(solution)/shard_map/while/body/eval_jaxpr/ppermute | solution.py:15
  307.4 56.4 %collective-permute-start = (bf16[256,2,2048]{2,1,0:T(2,128)(2,1)}, bf16[256,2,2048]{2,1,0:T(2,128)(2,1)S(1)}, u32[]{:S(2)}, u32[]{:S(2)}) collective-permute-start(bf16[256,2,2048]{2,1,0:T(2,128)(2,1)} %get-tuple-element.591), channel_id=1, source_target_pairs={{0,2},{2,4},{4,6},{6,8},{8,10},{10,12},{12,14},{14,16},{16,18},{18... | collective-permute-start | bytes 6291464 | tf_op jit(solution)/shard_map/while/body/eval_jaxpr/ppermute | solution.py:15
  367.9 160.8 %collective-permute-start = (bf16[256,2,2048]{2,1,0:T(2,128)(2,1)}, bf16[256,2,2048]{2,1,0:T(2,128)(2,1)S(1)}, u32[]{:S(2)}, u32[]{:S(2)}) collective-permute-start(bf16[256,2,2048]{2,1,0:T(2,128)(2,1)} %get-tuple-element.591), channel_id=1, source_target_pairs={{0,2},{2,4},{4,6},{6,8},{8,10},{10,12},{12,14},{14,16},{16,18},{18... | collective-permute-start | bytes 6291464 | tf_op jit(solution)/shard_map/while/body/eval_jaxpr/ppermute | solution.py:15
  532.8 48.8 %collective-permute-start = (bf16[256,2,2048]{2,1,0:T(2,128)(2,1)}, bf16[256,2,2048]{2,1,0:T(2,128)(2,1)S(1)}, u32[]{:S(2)}, u32[]{:S(2)}) collective-permute-start(bf16[256,2,2048]{2,1,0:T(2,128)(2,1)} %get-tuple-element.591), channel_id=1, source_target_pairs={{0,2},{2,4},{4,6},{6,8},{8,10},{10,12},{12,14},{14,16},{16,18},{18... | collective-permute-start | bytes 6291464 | tf_op jit(solution)/shard_map/while/body/eval_jaxpr/ppermute | solution.py:15
  585.7 49.3 %collective-permute-start = (bf16[256,2,2048]{2,1,0:T(2,128)(2,1)}, bf16[256,2,2048]{2,1,0:T(2,128)(2,1)S(1)}, u32[]{:S(2)}, u32[]{:S(2)}) collective-permute-start(bf16[256,2,2048]{2,1,0:T(2,128)(2,1)} %get-tuple-element.591), channel_id=1, source_target_pairs={{0,2},{2,4},{4,6},{6,8},{8,10},{10,12},{12,14},{14,16},{16,18},{18... | collective-permute-start | bytes 6291464 | tf_op jit(solution)/shard_map/while/body/eval_jaxpr/ppermute | solution.py:15
  639.1 47.4 %collective-permute-start = (bf16[256,2,2048]{2,1,0:T(2,128)(2,1)}, bf16[256,2,2048]{2,1,0:T(2,128)(2,1)S(1)}, u32[]{:S(2)}, u32[]{:S(2)}) collective-permute-start(bf16[256,2,2048]{2,1,0:T(2,128)(2,1)} %get-tuple-element.591), channel_id=1, source_target_pairs={{0,2},{2,4},{4,6},{6,8},{8,10},{10,12},{12,14},{14,16},{16,18},{18... | collective-permute-start | bytes 6291464 | tf_op jit(solution)/shard_map/while/body/eval_jaxpr/ppermute | solution.py:15
  690.6 64.9 %collective-permute-start = (bf16[256,2,2048]{2,1,0:T(2,128)(2,1)}, bf16[256,2,2048]{2,1,0:T(2,128)(2,1)S(1)}, u32[]{:S(2)}, u32[]{:S(2)}) collective-permute-start(bf16[256,2,2048]{2,1,0:T(2,128)(2,1)} %get-tuple-element.591), channel_id=1, source_target_pairs={{0,2},{2,4},{4,6},{6,8},{8,10},{10,12},{12,14},{14,16},{16,18},{18... | collective-permute-start | bytes 6291464 | tf_op jit(solution)/shard_map/while/body/eval_jaxpr/ppermute | solution.py:15
  815.0 2.4 copy-start
  831.5 78.6 %copy-start.1 = (bf16[127,2048]{1,0:T(8,128)(2,1)S(1)}, bf16[127,2048]{1,0:T(8,128)(2,1)}, u32[]{:S(2)}) copy-start(bf16[127,2048]{1,0:T(8,128)(2,1)} %get-tuple-element.417) | copy-start | bytes 1560580
  924.8 413.0 %reduce-scatter.3.cloned.1.call-start = ((), (), s32[]{:S(2)}) async-start(), calls=%async_computation.3 | async-start | bytes 3145728 | tf_op jit(solution)/shard_map/reduce_scatter | solution.py:99
Sparse Core Ops, SparseCore 0:
  10.7 243.9 all-gather.4
  257.4 320.8 all-gather.2
  925.0 68.6 reduce-scatter.4
  1269.0 68.7 reduce-scatter.2
where the time goes:
time: 1360 us; the launch traced here: 1340 us
  waiting for transfers between devices  455 us (33%)
  local copies, waits for them, and re-layouts  332 us (24%)
  other arithmetic  311 us (23%)
  starting transfers between devices  144 us (11%)
  matrix products  82.3 us (6%)
  between operations  13.8 us (1%)
    ppermute x9, waiting for transfers between devices, from_behind(): return lax.ppermute(block, axis, route)  386 us
    add x256, other arithmetic, add_tap(): return total + filters[index][None, :] * window_rows  284 us
    dynamic_slice x256, local copies, waits for them, and re-layouts, add_tap(): return total + filters[index][None, :] * window_rows  218 us
    ppermute x9, starting transfers between devices, from_behind(): return lax.ppermute(block, axis, route)  143 us
    reduce_scatter x1, waiting for transfers between devices, per_device(): lax.psum_scatter(hyena_terms.astype(jnp.bfloat16), 'tp', scatter_dimensio...  68.9 us
    reshape x1, local copies, waits for them, and re-layouts, per_device(): earlier = earlier[::-1].reshape(blocks * rows, 2, width)  41.1 us
    dot_general x16, matrix products, head_attention(): lax.dot_general(queries, keys_all, (((1,), (1,)), ((), ())), preferred_el...  32.8 us
  transfers between devices with their start and end apart: 13, of which 9 were waited for; matrix products, arithmetic and copies ran while one was open for 54% of the time, Pallas kernels for 0%

commit v1 on v0

v1 whole, which is shorter than its diff:
```python
import functools
import math

import jax
import jax.numpy as jnp
import ml_dtypes
import numpy as np
from jax import lax
from jax.experimental import pallas as pl
from jax.experimental.pallas import tpu as pltpu
from jax.sharding import PartitionSpec as P

HEAD_DIM = 128
WINDOW = 2048
PLANE = 4
MASKED = -1e30
VMEM = 56 * 1024 * 1024


def split_bf16(array):
    high = array.astype(jnp.bfloat16)
    return high, (array - high.astype(jnp.float32)).astype(jnp.bfloat16)


def mm(a, b):
    return jnp.dot(a, b, preferred_element_type=jnp.float32)


def dft_matrices(taps):
    size = 2 * taps
    n = np.arange(size)
    k = np.arange(taps)
    angle = 2 * np.pi * ((k[:, None] * n[None, :]) % size) / size
    cosine, sine = np.cos(angle), np.sin(angle)
    forward = np.concatenate([cosine, -sine], 0)
    forward[taps] = (-1.0) ** n
    weight = np.full(taps, 2.0 / size)
    weight[0] = 1.0 / size
    inverse = np.concatenate([cosine * weight[:, None], -sine * weight[:, None]], 0)
    inverse[taps] = (-1.0) ** n / size
    inverse = inverse.T[taps:]

    def halves(array):
        array = array.astype(np.float32)
        high = array.astype(ml_dtypes.bfloat16)
        return high, (array - high.astype(np.float32)).astype(ml_dtypes.bfloat16)

    return [jnp.asarray(m) for m in halves(forward) + halves(inverse)]


def fir_kernel(rim, product, gate, filters, f_hi, f_lo, g_hi, g_lo, out):
    taps = filters.shape[0]
    rows = product.shape[0]
    h_hi, h_lo = split_bf16(filters[...])
    spectrum = (
        mm(f_hi[:, :taps], h_hi) + mm(f_hi[:, :taps], h_lo) + mm(f_lo[:, :taps], h_hi)
    )
    first = lax.broadcasted_iota(jnp.int32, (taps, spectrum.shape[1]), 0) == 0
    h_re, h_im = spectrum[:taps], spectrum[taps:]
    h_re2 = jnp.where(first, h_im, h_re)
    h_im = jnp.where(first, 0.0, h_im)
    for start in range(0, rows, taps):
        before = rim[...] if start == 0 else product[start - taps : start]
        x = jnp.concatenate([before, product[start : start + taps]], 0)
        xs = mm(f_hi[...], x) + mm(f_lo[...], x)
        x_re, x_im = xs[:taps], xs[taps:]
        y = jnp.concatenate([x_re * h_re - x_im * h_im, x_re * h_im + x_im * h_re2], 0)
        y_hi, y_lo = split_bf16(y)
        filtered = mm(g_hi[...], y_hi) + mm(g_hi[...], y_lo) + mm(g_lo[...], y_hi)
        span = slice(start, start + taps)
        out[span] = (gate[span].astype(jnp.float32) * filtered).astype(out.dtype)


def fir(rim, product, gate, filters):
    taps, width = filters.shape
    rows = product.shape[0]
    tile = min(512, width)
    mats = dft_matrices(taps)
    column = lambda n: pl.BlockSpec((n, tile), lambda i: (0, i))
    return pl.pallas_call(
        fir_kernel,
        grid=(width // tile,),
        in_specs=[column(taps), column(rows), column(rows), column(taps)]
        + [pl.BlockSpec(m.shape, lambda i: (0, 0)) for m in mats],
        out_specs=column(rows),
        out_shape=jax.ShapeDtypeStruct((rows, width), jnp.bfloat16),
        compiler_params=pltpu.CompilerParams(vmem_limit_bytes=VMEM),
        cost_estimate=pl.CostEstimate(
            flops=2 * width * (10 * rows * taps + 6 * taps * taps),
            bytes_accessed=8 * rows * width,
            transcendentals=0,
        ),
    )(rim, product, gate, filters, *mats)


def attend_kernel(kind, first, last, info, q_ref, k_ref, v_ref, *refs):
    refs = list(refs)
    if not first:
        acc_in, stat_in = refs.pop(0), refs.pop(0)
    if last:
        (out,) = refs
    else:
        acc_out, stat_out = refs
    plane, rows = k_ref.shape[0], k_ref.shape[2]
    me = info[0]
    factor = math.log2(math.e) / math.sqrt(HEAD_DIM)
    lane = lax.broadcasted_iota(jnp.int32, (rows, HEAD_DIM), 1)

    def write(top, total, acc):
        if last:
            out[0] = (acc / total).astype(out.dtype)
        else:
            acc_out[0] = acc
            stat_out[0] = jnp.where(lane < HEAD_DIM // 2, top, total)

    def previous():
        stat = stat_in[0]
        half = HEAD_DIM // 2
        return stat[:, 0:1], stat[:, half : half + 1], acc_in[0]

    def attend(blocks, diagonal):
        q = q_ref[0]
        scores = []
        for j in blocks:
            s = lax.dot_general(
                q, k_ref[me ^ j, 0], (((1,), (1,)), ((), ())), preferred_element_type=jnp.float32
            ) * factor
            if j == diagonal:
                row = lax.broadcasted_iota(jnp.int32, s.shape, 0)
                col = lax.broadcasted_iota(jnp.int32, s.shape, 1)
                s = jnp.where(col <= row if kind == "causal" else col > row, s, MASKED)
            scores.append(s)
        top = functools.reduce(jnp.maximum, scores).max(axis=1, keepdims=True)
        if not first:
            old_top, old_total, old_acc = previous()
            top = jnp.maximum(top, old_top)
        acc, sums = None, None
        for j, s in zip(blocks, scores):
            w = jnp.exp2(s - top)
            sums = w if sums is None else sums + w
            term = mm(w.astype(jnp.bfloat16), v_ref[me ^ j, 0])
            acc = term if acc is None else acc + term
        total = sums.sum(axis=1, keepdims=True)
        if not first:
            shrink = jnp.exp2(old_top - top)
            total = total + shrink * old_total
            acc = acc + shrink * old_acc
        write(top, total, acc)

    def run():
        if kind == "full":
            attend(list(range(plane)), None)
            return
        here = pl.program_id(1)
        for i in range(plane):

            @pl.when(here == i)
            def _(i=i):
                attend(list(range(i + 1)) if kind == "causal" else list(range(i, plane)), i)

    if first:
        run()
    else:

        @pl.when(info[1] > 0)
        def _():
            run()

        @pl.when(info[1] == 0)
        def _():
            write(*previous())


def attend(kind, first, last, info, queries, pairs, carry):
    plane, rows, width = queries.shape
    heads = width // HEAD_DIM
    mine = pl.BlockSpec((1, rows, HEAD_DIM), lambda h, i, info: (info[0] ^ i, 0, h))
    keys = pl.BlockSpec((plane, 1, rows, HEAD_DIM), lambda h, i, info: (0, 0, 0, h))
    values = pl.BlockSpec((plane, 1, rows, HEAD_DIM), lambda h, i, info: (0, 1, 0, h))
    if last:
        out_specs, out_shape = mine, jax.ShapeDtypeStruct(queries.shape, jnp.bfloat16)
    else:
        out_specs = (mine, mine)
        out_shape = (jax.ShapeDtypeStruct(queries.shape, jnp.float32),) * 2
    scores = heads * (plane * rows) ** 2 // (1 if kind == "full" else 2)
    return pl.pallas_call(
        functools.partial(attend_kernel, kind, first, last),
        grid_spec=pltpu.PrefetchScalarGridSpec(
            num_scalar_prefetch=1,
            grid=(heads, plane),
            in_specs=[mine, keys, values] + [mine] * len(carry),
            out_specs=out_specs,
        ),
        out_shape=out_shape,
        compiler_params=pltpu.CompilerParams(vmem_limit_bytes=VMEM),
        cost_estimate=pl.CostEstimate(
            flops=4 * scores * HEAD_DIM, bytes_accessed=12 * queries.size, transcendentals=scores
        ),
    )(info, queries, pairs, pairs, *carry)


def project_kernel(levels, splits, info, *refs):
    parts, weights, out = refs[:splits], refs[splits:-1], refs[-1]
    level = info[0]
    depth = parts[0].shape[2]
    for index, w in enumerate(weights):
        target = level + (index - (levels - 1))

        @pl.when((target >= 0) & (target < levels))
        def _(w=w, target=target):
            total = None
            for s, part in enumerate(parts):
                term = mm(part[0], w[s * depth : (s + 1) * depth])
                total = term if total is None else total + term
            out[target, 0] = total.astype(out.dtype)


def project(levels, info, parts, weights):
    plane, rows, depth = parts[0].shape
    columns = weights[0].shape[1]

    def part_spec(s):
        return pl.BlockSpec((1, rows, depth), lambda r, info: (r ^ s, 0, 0))

    return pl.pallas_call(
        functools.partial(project_kernel, levels, len(parts)),
        grid_spec=pltpu.PrefetchScalarGridSpec(
            num_scalar_prefetch=1,
            grid=(plane,),
            in_specs=[part_spec(s) for s in range(len(parts))]
            + [pl.BlockSpec(w.shape, lambda r, info: (0, 0)) for w in weights],
            out_specs=pl.BlockSpec((levels, 1, rows, columns), lambda r, info: (0, r, 0, 0)),
        ),
        out_shape=jax.ShapeDtypeStruct((levels, plane, rows, columns), jnp.bfloat16),
        compiler_params=pltpu.CompilerParams(vmem_limit_bytes=VMEM),
        cost_estimate=pl.CostEstimate(
            flops=2 * plane * rows * depth * len(parts) * columns * levels,
            bytes_accessed=16 * 1024 * 1024,
            transcendentals=0,
        ),
    )(info, *parts, *weights)


def per_device(hyena_in, filters, attn_in, out_weight, attn_weight):
    rows, _, width = hyena_in.shape
    taps = filters.shape[0]
    n_ctx, n_tp = lax.axis_size("ctx"), lax.axis_size("tp")
    levels = n_ctx // PLANE
    device_index = lax.axis_index("ctx")
    group = lax.axis_index("tp")
    me, level = device_index % PLANE, device_index // PLANE
    chunk = width // PLANE

    def swap(block, relative):
        return lax.ppermute(block, "ctx", [(i, i ^ relative) for i in range(n_ctx)])

    def climb(block, direction, step):
        if direction > 0:
            sources = range((step - 1) * PLANE, n_ctx - PLANE)
        else:
            sources = range(PLANE, n_ctx - (step - 1) * PLANE)
        return lax.ppermute(block, "ctx", [(i, i + direction * PLANE) for i in sources])

    def by_relative(build):
        return [build(me ^ s) for s in range(PLANE)]

    def piece(first, count, index):
        block = lax.dynamic_slice(attn_in, (0, first, index * chunk), (rows, count, chunk))
        return block.transpose(1, 0, 2)

    pair_pieces = by_relative(lambda index: piece(1, 2, index))
    query_pieces = by_relative(lambda index: piece(0, 1, index)[0])
    pairs = jnp.stack([pair_pieces[0]] + [swap(pair_pieces[s], s) for s in range(1, PLANE)])
    queries = jnp.stack([query_pieces[0]] + [swap(query_pieces[s], s) for s in range(1, PLANE)])

    attn_rows = attn_weight.reshape(PLANE, chunk, -1)
    attn_weight = jnp.concatenate(
        by_relative(lambda index: lax.dynamic_index_in_dim(attn_rows, index, 0, False)), 0
    )

    def along_levels(weight):
        up, down = [weight], [weight]
        for step in range(1, levels):
            up.append(climb(up[-1], 1, step))
            down.append(climb(down[-1], -1, step))
        return up[:0:-1] + down

    product = (hyena_in[:, 0].astype(jnp.float32) * hyena_in[:, 2].astype(jnp.float32)).astype(
        jnp.bfloat16
    )
    rim = lax.ppermute(
        product[rows - taps :], "ctx", [(i, i + 1) for i in range(n_ctx - 1)]
    )
    hyena_act = fir(rim, product, hyena_in[:, 1], filters)

    def across_plane(block):
        one, two = swap(block, 1), swap(block, 2)
        half = block.shape[0] // 2
        three = jnp.concatenate([swap(one[:half], 2), swap(two[half:], 1)], 0)
        return [block, one, two, three]

    hyena_rows = jnp.stack(across_plane(hyena_act))

    back = WINDOW // (PLANE * rows)
    carry = ()
    for distance in range(back + 1):
        if distance:
            pairs = climb(pairs, 1, 1)
        kind = "causal" if distance == 0 else "full" if distance < back else "anti"
        info = jnp.stack([me, (level >= distance).astype(jnp.int32)]).astype(jnp.int32)
        carry = attend(kind, distance == 0, distance == back, info, queries, pairs, carry)
    attended = across_plane(carry)

    level_info = jnp.stack([level]).astype(jnp.int32)
    share = levels // n_tp

    def finish(parts, weight):
        partial = project(levels, level_info, parts, along_levels(weight))
        partial = partial.reshape((n_tp, share) + partial.shape[1:])
        total = lax.dynamic_index_in_dim(partial, group, 0, False).astype(jnp.float32)
        for shift in range(1, n_tp):
            sent = lax.dynamic_index_in_dim(partial, (group + shift) % n_tp, 0, False)
            got = lax.ppermute(sent, "tp", [(i, (i + shift) % n_tp) for i in range(n_tp)])
            total = total + got.astype(jnp.float32)
        total = total.astype(jnp.bfloat16)
        ours = [total[:, 0]] + [swap(total[:, s], s) for s in range(1, PLANE)]
        natural = [
            lax.select_n(me, *[ours[t ^ j] for t in range(PLANE)]) for j in range(PLANE)
        ]
        return jnp.stack(natural, 1).transpose(2, 0, 1, 3).reshape(rows, -1)

    return (finish([hyena_rows], out_weight), finish(attended, attn_weight))


def solution(mesh):
    in_specs = (
        P("ctx", None, "tp"),
        P(None, "tp"),
        P("ctx", None, "tp"),
        P("tp", "ctx"),
        P("tp", "ctx"),
    )
    out_specs = (P("ctx", "tp"), P("ctx", "tp"))
    return jax.shard_map(
        per_device, mesh=mesh, in_specs=in_specs, out_specs=out_specs, check_vma=False
    )
```

time: 1360 us -> 353 us (0.26); the launches traced: 1340 us -> 351 us
  local copies, waits for them, and re-layouts: 332 us -> 19.2 us
  other arithmetic: 311 us -> 14.2 us
  waiting for transfers between devices: 455 us -> 166 us
  matrix products: 82.3 us -> 0 us
  Pallas kernels: 0 us -> 70.1 us
  starting transfers between devices: 144 us -> 80.2 us
    add x288 -> x0, other arithmetic: 284 us -> none  [the longest x256 284 us: add_tap(): return total + filters[index][None, :] * window_rows]
    ppermute x9 -> x37, waiting for transfers between devices: 386 us -> 166 us  [the longest x14 119 us: climb(): lax.ppermute(block, 'ctx', [(i, i + direction * PLANE) for i in sources])]
    dynamic_slice x256 -> x2, local copies, waits for them, and re-layouts: 218 us -> 2.73 us  [the longest x1 1.69 us: finish(): lax.dynamic_index_in_dim(partial, group, 0, False).astype(jnp.float32)]
    dot_general x34 -> x0, matrix products: 82.3 us -> none  [the longest x16 32.8 us: head_attention(): lax.dot_general(queries, keys_all, (((1,), (1,)), ((), ())), preferred_el...]
    pallas_call x0 -> x6, Pallas kernels: none -> 70.1 us  [the longest x3 39.7 us: attend(): pl.pallas_call(functools.partial(attend_kernel, kind, first, last), grid_...]
    reduce_scatter x2 -> x0, waiting for transfers between devices: 68.9 us -> none  [the longest x1 68.9 us: per_device(): lax.psum_scatter(hyena_terms.astype(jnp.bfloat16), 'tp', scatter_dimensio...]
    ppermute x9 -> x37, starting transfers between devices: 143 us -> 80.2 us  [the longest x14 45.1 us: climb(): lax.ppermute(block, 'ctx', [(i, i + direction * PLANE) for i in sources])]
    reshape x1 -> x2, local copies, waits for them, and re-layouts: 41.1 us -> 3.17 us  [finish(): return jnp.stack(natural, 1).transpose(2, 0, 1, 3).reshape(rows, -1)]
  transfers between devices with their start and end apart: 13 -> 37, of which waited for: 9 -> 12; matrix products, arithmetic and copies ran while one was open for 54% -> 8% of each run, Pallas kernels for 0% -> 20%
where the time goes in v1:
time: 353 us; the launch traced here: 351 us
  waiting for transfers between devices  166 us (47%)
  starting transfers between devices  80.2 us (23%)
  Pallas kernels  70.1 us (20%)
  local copies, waits for them, and re-layouts  19.2 us (5%)
  other arithmetic  14.2 us (4%)
    ppermute x14, waiting for transfers between devices, climb(): lax.ppermute(block, 'ctx', [(i, i + direction * PLANE) for i in sources])  119 us
    ppermute x20, waiting for transfers between devices, swap(): return lax.ppermute(block, 'ctx', [(i, i ^ relative) for i in range(n_ctx)])  47.7 us
    ppermute x14, starting transfers between devices, climb(): lax.ppermute(block, 'ctx', [(i, i + direction * PLANE) for i in sources])  45.1 us
    pallas_call x3, Pallas kernels, attend(): pl.pallas_call(functools.partial(attend_kernel, kind, first, last), grid_...  39.7 us
    ppermute x20, starting transfers between devices, swap(): return lax.ppermute(block, 'ctx', [(i, i ^ relative) for i in range(n_ctx)])  31.5 us
    pallas_call x2, Pallas kernels, project(): pl.pallas_call(functools.partial(project_kernel, levels, len(parts)), gri...  23.1 us
    pallas_call x1, Pallas kernels, fir(): pl.pallas_call(fir_kernel, grid=(width // tile,), in_specs=[column(taps),...  7.21 us
  transfers between devices with their start and end apart: 37, of which 12 were waited for; matrix products, arithmetic and copies ran while one was open for 8% of the time, Pallas kernels for 20%

profile of v1, /device:TPU:0, one launch (start us, length us, event | category | flops | bytes accessed | tf_op | source)
XLA Modules:
  0.0 351.1 jit_solution(13981333754147836435)
XLA Ops:
  2.3 3.0 collective-permute-start.18
  6.9 11.2 %collective-permute-done.18 = bf16[2,256,512]{2,1,0:T(8,128)(2,1)S(1)} collective-permute-done((bf16[2,256,512]{2,1,0:T(8,128)(2,1)S(1)}, bf16[2,256,512]{2,1,0:T(8,128)(2,1)S(1)}, u32[]{:S(2)}, u32[]{:S(2)}) %collective-permute-start.18) | collective-permute-done | bytes 524320 | tf_op jit(solution)/shard_map/ppermute | solution.py:255
  18.1 11.9 %collective-permute-done.19 = bf16[2,256,512]{2,1,0:T(8,128)(2,1)S(1)} collective-permute-done((bf16[2,256,512]{2,1,0:T(8,128)(2,1)S(1)}, bf16[2,256,512]{2,1,0:T(8,128)(2,1)S(1)}, u32[]{:S(2)}, u32[]{:S(2)}) %collective-permute-start.19) | collective-permute-done | bytes 524320 | tf_op jit(solution)/shard_map/ppermute | solution.py:255
  30.3 5.1 %collective-permute-start.21 = (bf16[4,2,256,512]{3,2,1,0:T(8,128)(2,1)S(1)}, bf16[4,2,256,512]{3,2,1,0:T(8,128)(2,1)}, u32[]{:S(2)}, u32[]{:S(2)}) collective-permute-start(bf16[4,2,256,512]{3,2,1,0:T(8,128)(2,1)S(1)} %pad_maximum_fusion.1.k_ref.v_ref), channel_id=1, source_target_pairs={{0,8},{2,10},{4,12},{6,14},{8,16},{10,18},{12,20},{14,22},{16,24},... | collective-permute-start | bytes 6291464 | tf_op jit(solution)/shard_map/ppermute | solution.py:262
  40.0 3.5 collective-permute-start
  43.7 2.8 collective-permute-start.27
  50.6 9.6 %collective-permute-done.16 = bf16[256,512]{1,0:T(8,128)(2,1)S(1)} collective-permute-done((bf16[256,512]{1,0:T(8,128)(2,1)S(1)}, bf16[256,512]{1,0:T(8,128)(2,1)S(1)}, u32[]{:S(2)}, u32[]{:S(2)}) %collective-permute-start.16) | collective-permute-done | bytes 262176 | tf_op jit(solution)/shard_map/ppermute | solution.py:255
  61.5 18.6 %collective-permute-done.21.k_ref.v_ref = bf16[4,2,256,512]{3,2,1,0:T(8,128)(2,1)} collective-permute-done((bf16[4,2,256,512]{3,2,1,0:T(8,128)(2,1)S(1)}, bf16[4,2,256,512]{3,2,1,0:T(8,128)(2,1)}, u32[]{:S(2)}, u32[]{:S(2)}) %collective-permute-start.21) | collective-permute-done | bytes 2097184 | tf_op jit(solution)/shard_map/ppermute | solution.py:262
  80.1 18.7 %collective-permute-start.22 = (bf16[4,2,256,512]{3,2,1,0:T(8,128)(2,1)}, bf16[4,2,256,512]{3,2,1,0:T(8,128)(2,1)S(1)}, u32[]{:S(2)}, u32[]{:S(2)}) collective-permute-start(bf16[4,2,256,512]{3,2,1,0:T(8,128)(2,1)} %collective-permute-done.21.k_ref.v_ref), channel_id=1, source_target_pairs={{0,8},{2,10},{4,12},{6,14},{8,16},{10,18},{12,20},{14,22},{16,24},... | collective-permute-start | bytes 6291464 | tf_op jit(solution)/shard_map/ppermute | solution.py:262
  99.9 7.2 %shard_map.104 = bf16[256,2048]{1,0:T(8,128)(2,1)} custom-call(bf16[128,2048]{1,0:T(8,128)(2,1)} %collective-permute-done.rim, bf16[256,2048]{1,0:T(8,128)(2,1)} %fusion.2.product, bf16[256,2048]{1,0:T(8,128)(2,1)} %slice_bitcast_fusion.gate, f32[128,2048]{1,0:T(8,128)} %filters.1, bf16[256,256]{1,0:T(8,128)(2,1)} %constant.79.clone.f_hi, ...), custom_call_target="tpu_custom_call" | custom-call | flops 1744830464 | bytes 4194304 | tf_op jit(solution)/shard_map/pallas_call | solution.py:80
  107.1 4.8 %collective-permute-start.5 = (bf16[2048,256]{1,0:T(8,128)(2,1)}, bf16[2048,256]{1,0:T(8,128)(2,1)}, u32[]{:S(2)}, u32[]{:S(2)}) collective-permute-start(bf16[2048,256]{1,0:T(8,128)(2,1)} %refs_4_.1), channel_id=1, source_target_pairs={{0,8},{2,10},{4,12},{6,14},{8,16},{10,18},{12,20},{14,22},{16,24},... | collective-permute-start | bytes 3145736 | tf_op jit(solution)/shard_map/ppermute | solution.py:262
  112.0 3.8 %collective-permute-start.2 = (bf16[256,2048]{1,0:T(8,128)(2,1)}, bf16[256,2048]{1,0:T(8,128)(2,1)}, u32[]{:S(2)}, u32[]{:S(2)}) collective-permute-start(bf16[256,2048]{1,0:T(8,128)(2,1)} %shard_map.104), channel_id=1, source_target_pairs={{0,4},{2,6},{4,0},{6,2},{8,12},{10,14},{12,8},{14,10},{16,20},{18,... | collective-permute-start | bytes 3145736 | tf_op jit(solution)/shard_map/ppermute | solution.py:255
  118.1 49.6 %collective-permute-done.5.refs_3_ = bf16[2048,256]{1,0:T(8,128)(2,1)} collective-permute-done((bf16[2048,256]{1,0:T(8,128)(2,1)}, bf16[2048,256]{1,0:T(8,128)(2,1)}, u32[]{:S(2)}, u32[]{:S(2)}) %collective-permute-start.5) | collective-permute-done | bytes 1048608 | tf_op jit(solution)/shard_map/ppermute | solution.py:262
  174.9 15.0 %shard_map.106 = (f32[4,256,512]{2,1,0:T(8,128)}, f32[4,256,512]{2,1,0:T(8,128)}) custom-call(s32[2]{0:T(128)} %pad_add_fusion.2.info, bf16[4,256,512]{2,1,0:T(8,128)(2,1)} %pad_maximum_fusion.2.q_ref, bf16[4,2,256,512]{3,2,1,0:T(8,128)(2,1)} %copy-done, bf16[4,2,256,512]{3,2,1,0:T(8,128)(2,1)} %copy-done), custom_call_target="tpu_custom_call" | custom-call | flops 1073741824 | bytes 6291456 | tf_op jit(solution)/shard_map/pallas_call | solution.py:186
  191.0 12.8 %collective-permute-start.4 = (bf16[128,2048]{1,0:T(8,128)(2,1)S(1)}, bf16[128,2048]{1,0:T(8,128)(2,1)S(1)}, u32[]{:S(2)}, u32[]{:S(2)}) collective-permute-start(bf16[128,2048]{1,0:T(8,128)(2,1)S(1)} %slice.70), channel_id=1, source_target_pairs={{0,2},{2,0},{4,6},{6,4},{8,10},{10,8},{12,14},{14,12},{16,18},{18,... | collective-permute-start | bytes 1572872 | tf_op jit(solution)/shard_map/ppermute | solution.py:255
  203.8 12.8 %shard_map.107 = (f32[4,256,512]{2,1,0:T(8,128)}, f32[4,256,512]{2,1,0:T(8,128)}) custom-call(s32[2]{0:T(128)} %pad_add_fusion.1.info, bf16[4,256,512]{2,1,0:T(8,128)(2,1)} %pad_maximum_fusion.2.q_ref, bf16[4,2,256,512]{3,2,1,0:T(8,128)(2,1)} %collective-permute-done.21.k_ref.v_ref, bf16[4,2,256,512]{3,2,1,0:T(8,128)(2,1)} %collective-permute-done.21.k_ref.v_ref, ...), custom_call_target="tpu_custom_call" | custom-call | flops 2147483648 | bytes 6291456 | tf_op jit(solution)/shard_map/pallas_call | solution.py:186
  216.6 11.9 %shard_map.108.refs_0_ = bf16[4,256,512]{2,1,0:T(8,128)(2,1)} custom-call(s32[2]{0:T(128)} %pad_add_fusion.info, bf16[4,256,512]{2,1,0:T(8,128)(2,1)} %pad_maximum_fusion.2.q_ref, bf16[4,2,256,512]{3,2,1,0:T(8,128)(2,1)} %copy-done.3, bf16[4,2,256,512]{3,2,1,0:T(8,128)(2,1)} %copy-done.3, f32[4,256,512]{2,1,0:T(8,128)} %get-tuple-element.8.refs_0_, ...), custom_call_target="tpu_custom_call" | custom-call | flops 1073741824 | bytes 6291456 | tf_op jit(solution)/shard_map/pallas_call | solution.py:186
  235.8 33.0 %collective-permute-done.31.refs_9_ = bf16[2048,256]{1,0:T(8,128)(2,1)} collective-permute-done((bf16[2048,256]{1,0:T(8,128)(2,1)}, bf16[2048,256]{1,0:T(8,128)(2,1)}, u32[]{:S(2)}, u32[]{:S(2)}) %collective-permute-start.31) | collective-permute-done | bytes 1048608 | tf_op jit(solution)/shard_map/ppermute | solution.py:262
  271.0 3.3 pad_maximum_fusion.refs_0_
  275.5 15.7 %collective-permute-done.10.refs_7_ = bf16[2048,256]{1,0:T(8,128)(2,1)} collective-permute-done((bf16[2048,256]{1,0:T(8,128)(2,1)}, bf16[2048,256]{1,0:T(8,128)(2,1)}, u32[]{:S(2)}, u32[]{:S(2)}) %collective-permute-start.10) | collective-permute-done | bytes 1048608 | tf_op jit(solution)/shard_map/ppermute | solution.py:262
  291.3 11.5 %shard_map.105 = bf16[4,4,256,256]{3,2,1,0:T(8,128)(2,1)} custom-call(s32[1]{0:T(128)} %bitcast.info, bf16[4,256,2048]{2,1,0:T(8,128)(2,1)} %pad_maximum_fusion.refs_0_, bf16[2048,256]{1,0:T(8,128)(2,1)} %collective-permute-done.7.refs_1_, bf16[2048,256]{1,0:T(8,128)(2,1)} %collective-permute-done.6.refs_2_, ...), custom_call_target="tpu_custom_call" | custom-call | flops 4294967296 | bytes 16777216 | tf_op jit(solution)/shard_map/pallas_call | solution.py:225
  308.2 11.7 %shard_map.109 = bf16[4,4,256,256]{3,2,1,0:T(8,128)(2,1)} custom-call(s32[1]{0:T(128)} %bitcast.info, bf16[4,256,512]{2,1,0:T(8,128)(2,1)} %shard_map.108.refs_0_, bf16[4,256,512]{2,1,0:T(8,128)(2,1)} %copy-done.12, bf16[4,256,512]{2,1,0:T(8,128)(2,1)} %collective-permute-done.24.refs_2_, bf16[4,256,512]{2,1,0:T(8,128)(2,1)} %pad_maximum_fusion.3.refs_3_, ...), custom_call_target="tpu_custom_call" | custom-call | flops 4294967296 | bytes 16777216 | tf_op jit(solution)/shard_map/pallas_call | solution.py:225
  332.2 6.2 %collective-permute-done.13 = bf16[2,256,256]{2,1,0:T(8,128)(2,1)S(1)} collective-permute-done((bf16[2,256,256]{2,1,0:T(8,128)(2,1)S(1)}, bf16[2,256,256]{2,1,0:T(8,128)(2,1)S(1)}, u32[]{:S(2)}, u32[]{:S(2)}) %collective-permute-start.13) | collective-permute-done | bytes 262176 | tf_op jit(solution)/shard_map/ppermute | solution.py:255
  342.1 6.3 %collective-permute-done.35 = bf16[2,256,256]{2,1,0:T(8,128)(2,1)S(1)} collective-permute-done((bf16[2,256,256]{2,1,0:T(8,128)(2,1)S(1)}, bf16[2,256,256]{2,1,0:T(8,128)(2,1)S(1)}, u32[]{:S(2)}, u32[]{:S(2)}) %collective-permute-start.35) | collective-permute-done | bytes 262176 | tf_op jit(solution)/shard_map/ppermute | solution.py:255
  (123 shorter events, 59.9 us)
Async XLA Ops:
  5.4 24.6 %collective-permute-start.19 = (bf16[2,256,512]{2,1,0:T(8,128)(2,1)S(1)}, bf16[2,256,512]{2,1,0:T(8,128)(2,1)S(1)}, u32[]{:S(2)}, u32[]{:S(2)}) collective-permute-start(bf16[2,256,512]{2,1,0:T(8,128)(2,1)S(1)} %get-tuple-element.13), channel_id=1, source_target_pairs={{0,4},{2,6},{4,0},{6,2},{8,12},{10,14},{12,8},{14,10},{16,20},{18,... | collective-permute-start | bytes 1572872 | tf_op jit(solution)/shard_map/ppermute | solution.py:255
  6.9 23.1 %collective-permute-start.20 = (bf16[2,256,512]{2,1,0:T(8,128)(2,1)S(1)}, bf16[2,256,512]{2,1,0:T(8,128)(2,1)S(1)}, u32[]{:S(2)}, u32[]{:S(2)}) collective-permute-start(bf16[2,256,512]{2,1,0:T(8,128)(2,1)S(1)} %get-tuple-element.12), channel_id=1, source_target_pairs={{0,6},{2,4},{4,2},{6,0},{8,14},{10,12},{12,10},{14,8},{16,22},{18,... | collective-permute-start | bytes 1572872 | tf_op jit(solution)/shard_map/ppermute | solution.py:255
  30.3 49.8 %collective-permute-start.21 = (bf16[4,2,256,512]{3,2,1,0:T(8,128)(2,1)S(1)}, bf16[4,2,256,512]{3,2,1,0:T(8,128)(2,1)}, u32[]{:S(2)}, u32[]{:S(2)}) collective-permute-start(bf16[4,2,256,512]{3,2,1,0:T(8,128)(2,1)S(1)} %pad_maximum_fusion.1.k_ref.v_ref), channel_id=1, source_target_pairs={{0,8},{2,10},{4,12},{6,14},{8,16},{10,18},{12,20},{14,22},{16,24},... | collective-permute-start | bytes 6291464 | tf_op jit(solution)/shard_map/ppermute | solution.py:262
  43.7 68.2 %collective-permute-start.27 = (bf16[2048,256]{1,0:T(8,128)(2,1)S(1)}, bf16[2048,256]{1,0:T(8,128)(2,1)}, u32[]{:S(2)}, u32[]{:S(2)}) collective-permute-start(bf16[2048,256]{1,0:T(8,128)(2,1)S(1)} %pad_maximum_fusion.4.refs_7_), channel_id=1, source_target_pairs={{0,8},{2,10},{4,12},{6,14},{8,16},{10,18},{12,20},{14,22},{16,24},... | collective-permute-start | bytes 3145736 | tf_op jit(solution)/shard_map/ppermute | solution.py:262
  46.5 65.5 %collective-permute-start.30 = (bf16[2048,256]{1,0:T(8,128)(2,1)S(1)}, bf16[2048,256]{1,0:T(8,128)(2,1)}, u32[]{:S(2)}, u32[]{:S(2)}) collective-permute-start(bf16[2048,256]{1,0:T(8,128)(2,1)S(1)} %pad_maximum_fusion.4.refs_7_), channel_id=1, source_target_pairs={{8,0},{10,2},{12,4},{14,6},{16,8},{18,10},{20,12},{22,14},{24,16},... | collective-permute-start | bytes 3145736 | tf_op jit(solution)/shard_map/ppermute | solution.py:262
  60.2 46.9 %collective-permute-start.17 = (bf16[256,512]{1,0:T(8,128)(2,1)S(1)}, bf16[256,512]{1,0:T(8,128)(2,1)S(1)}, u32[]{:S(2)}, u32[]{:S(2)}) collective-permute-start(bf16[256,512]{1,0:T(8,128)(2,1)S(1)} %copy-done.10), channel_id=1, source_target_pairs={{0,6},{2,4},{4,2},{6,0},{8,14},{10,12},{12,10},{14,8},{16,22},{18,... | collective-permute-start | bytes 786440 | tf_op jit(solution)/shard_map/ppermute | solution.py:255
  60.2 55.6 %collective-permute-start.8 = (bf16[2048,256]{1,0:T(8,128)(2,1)}, bf16[2048,256]{1,0:T(8,128)(2,1)}, u32[]{:S(2)}, u32[]{:S(2)}) collective-permute-start(bf16[2048,256]{1,0:T(8,128)(2,1)} %refs_4_.1), channel_id=1, source_target_pairs={{8,0},{10,2},{12,4},{14,6},{16,8},{18,10},{20,12},{22,14},{24,16},... | collective-permute-start | bytes 3145736 | tf_op jit(solution)/shard_map/ppermute | solution.py:262
  80.1 110.9 %collective-permute-start.22 = (bf16[4,2,256,512]{3,2,1,0:T(8,128)(2,1)}, bf16[4,2,256,512]{3,2,1,0:T(8,128)(2,1)S(1)}, u32[]{:S(2)}, u32[]{:S(2)}) collective-permute-start(bf16[4,2,256,512]{3,2,1,0:T(8,128)(2,1)} %collective-permute-done.21.k_ref.v_ref), channel_id=1, source_target_pairs={{0,8},{2,10},{4,12},{6,14},{8,16},{10,18},{12,20},{14,22},{16,24},... | collective-permute-start | bytes 6291464 | tf_op jit(solution)/shard_map/ppermute | solution.py:262
  107.1 60.7 %collective-permute-start.5 = (bf16[2048,256]{1,0:T(8,128)(2,1)}, bf16[2048,256]{1,0:T(8,128)(2,1)}, u32[]{:S(2)}, u32[]{:S(2)}) collective-permute-start(bf16[2048,256]{1,0:T(8,128)(2,1)} %refs_4_.1), channel_id=1, source_target_pairs={{0,8},{2,10},{4,12},{6,14},{8,16},{10,18},{12,20},{14,22},{16,24},... | collective-permute-start | bytes 3145736 | tf_op jit(solution)/shard_map/ppermute | solution.py:262
  111.9 57.2 %collective-permute-start.1 = (bf16[256,2048]{1,0:T(8,128)(2,1)}, bf16[256,2048]{1,0:T(8,128)(2,1)S(1)}, u32[]{:S(2)}, u32[]{:S(2)}) collective-permute-start(bf16[256,2048]{1,0:T(8,128)(2,1)} %shard_map.104), channel_id=1, source_target_pairs={{0,2},{2,0},{4,6},{6,4},{8,10},{10,8},{12,14},{14,12},{16,18},{18,... | collective-permute-start | bytes 3145736 | tf_op jit(solution)/shard_map/ppermute | solution.py:255
  112.0 60.1 %collective-permute-start.2 = (bf16[256,2048]{1,0:T(8,128)(2,1)}, bf16[256,2048]{1,0:T(8,128)(2,1)}, u32[]{:S(2)}, u32[]{:S(2)}) collective-permute-start(bf16[256,2048]{1,0:T(8,128)(2,1)} %shard_map.104), channel_id=1, source_target_pairs={{0,4},{2,6},{4,0},{6,2},{8,12},{10,14},{12,8},{14,10},{16,20},{18,... | collective-permute-start | bytes 3145736 | tf_op jit(solution)/shard_map/ppermute | solution.py:255
  115.8 112.7 %collective-permute-start.28 = (bf16[2048,256]{1,0:T(8,128)(2,1)}, bf16[2048,256]{1,0:T(8,128)(2,1)}, u32[]{:S(2)}, u32[]{:S(2)}) collective-permute-start(bf16[2048,256]{1,0:T(8,128)(2,1)} %collective-permute-done.27.refs_6_), channel_id=1, source_target_pairs={{8,16},{10,18},{12,20},{14,22},{16,24},{18,26},{20,28},{22,30},{9,... | collective-permute-start | bytes 3145736 | tf_op jit(solution)/shard_map/ppermute | solution.py:262
  167.8 63.8 %collective-permute-start.9 = (bf16[2048,256]{1,0:T(8,128)(2,1)}, bf16[2048,256]{1,0:T(8,128)(2,1)}, u32[]{:S(2)}, u32[]{:S(2)}) collective-permute-start(bf16[2048,256]{1,0:T(8,128)(2,1)} %collective-permute-done.8.refs_5_), channel_id=1, source_target_pairs={{8,0},{10,2},{12,4},{14,6},{16,8},{18,10},{20,12},{22,14},{9,1},{1... | collective-permute-start | bytes 3145736 | tf_op jit(solution)/shard_map/ppermute | solution.py:262
  169.1 63.8 %collective-permute-start.6 = (bf16[2048,256]{1,0:T(8,128)(2,1)}, bf16[2048,256]{1,0:T(8,128)(2,1)}, u32[]{:S(2)}, u32[]{:S(2)}) collective-permute-start(bf16[2048,256]{1,0:T(8,128)(2,1)} %collective-permute-done.5.refs_3_), channel_id=1, source_target_pairs={{8,16},{10,18},{12,20},{14,22},{16,24},{18,26},{20,28},{22,30},{9,... | collective-permute-start | bytes 3145736 | tf_op jit(solution)/shard_map/ppermute | solution.py:262
  172.1 57.8 %collective-permute-start.3 = (bf16[128,2048]{1,0:T(8,128)(2,1)S(1)}, bf16[128,2048]{1,0:T(8,128)(2,1)S(1)}, u32[]{:S(2)}, u32[]{:S(2)}) collective-permute-start(bf16[128,2048]{1,0:T(8,128)(2,1)S(1)} %slice.69), channel_id=1, source_target_pairs={{0,4},{2,6},{4,0},{6,2},{8,12},{10,14},{12,8},{14,10},{16,20},{18,... | collective-permute-start | bytes 1572872 | tf_op jit(solution)/shard_map/ppermute | solution.py:255
  191.0 39.1 %collective-permute-start.4 = (bf16[128,2048]{1,0:T(8,128)(2,1)S(1)}, bf16[128,2048]{1,0:T(8,128)(2,1)S(1)}, u32[]{:S(2)}, u32[]{:S(2)}) collective-permute-start(bf16[128,2048]{1,0:T(8,128)(2,1)S(1)} %slice.70), channel_id=1, source_target_pairs={{0,2},{2,0},{4,6},{6,4},{8,10},{10,8},{12,14},{14,12},{16,18},{18,... | collective-permute-start | bytes 1572872 | tf_op jit(solution)/shard_map/ppermute | solution.py:255
  228.5 40.3 %collective-permute-start.31 = (bf16[2048,256]{1,0:T(8,128)(2,1)}, bf16[2048,256]{1,0:T(8,128)(2,1)}, u32[]{:S(2)}, u32[]{:S(2)}) collective-permute-start(bf16[2048,256]{1,0:T(8,128)(2,1)} %collective-permute-done.30.refs_8_), channel_id=1, source_target_pairs={{8,0},{10,2},{12,4},{14,6},{16,8},{18,10},{20,12},{22,14},{9,1},{1... | collective-permute-start | bytes 3145736 | tf_op jit(solution)/shard_map/ppermute | solution.py:262
  230.0 39.6 %collective-permute-start.23 = (bf16[4,256,512]{2,1,0:T(8,128)(2,1)}, bf16[4,256,512]{2,1,0:T(8,128)(2,1)S(1)}, u32[]{:S(2)}, u32[]{:S(2)}) collective-permute-start(bf16[4,256,512]{2,1,0:T(8,128)(2,1)} %shard_map.108.refs_0_), channel_id=1, source_target_pairs={{0,2},{2,0},{4,6},{6,4},{8,10},{10,8},{12,14},{14,12},{16,18},{18,... | collective-permute-start | bytes 3145736 | tf_op jit(solution)/shard_map/ppermute | solution.py:255
  230.8 43.6 %collective-permute-start.24 = (bf16[4,256,512]{2,1,0:T(8,128)(2,1)}, bf16[4,256,512]{2,1,0:T(8,128)(2,1)}, u32[]{:S(2)}, u32[]{:S(2)}) collective-permute-start(bf16[4,256,512]{2,1,0:T(8,128)(2,1)} %shard_map.108.refs_0_), channel_id=1, source_target_pairs={{0,4},{2,6},{4,0},{6,2},{8,12},{10,14},{12,8},{14,10},{16,20},{18,... | collective-permute-start | bytes 3145736 | tf_op jit(solution)/shard_map/ppermute | solution.py:255
  231.6 59.7 %collective-permute-start.10 = (bf16[2048,256]{1,0:T(8,128)(2,1)}, bf16[2048,256]{1,0:T(8,128)(2,1)}, u32[]{:S(2)}, u32[]{:S(2)}) collective-permute-start(bf16[2048,256]{1,0:T(8,128)(2,1)} %collective-permute-done.9.refs_6_), channel_id=1, source_target_pairs={{8,0},{10,2},{12,4},{14,6},{9,1},{11,3},{13,5},{15,7}} | collective-permute-start | bytes 3145736 | tf_op jit(solution)/shard_map/ppermute | solution.py:262
  232.9 58.4 %collective-permute-start.7 = (bf16[2048,256]{1,0:T(8,128)(2,1)}, bf16[2048,256]{1,0:T(8,128)(2,1)}, u32[]{:S(2)}, u32[]{:S(2)}) collective-permute-start(bf16[2048,256]{1,0:T(8,128)(2,1)} %collective-permute-done.6.refs_2_), channel_id=1, source_target_pairs={{16,24},{18,26},{20,28},{22,30},{17,25},{19,27},{21,29},{23,31}} | collective-permute-start | bytes 3145736 | tf_op jit(solution)/shard_map/ppermute | solution.py:262
  268.8 37.8 %collective-permute-start.29 = (bf16[2048,256]{1,0:T(8,128)(2,1)}, bf16[2048,256]{1,0:T(8,128)(2,1)S(1)}, u32[]{:S(2)}, u32[]{:S(2)}) collective-permute-start(bf16[2048,256]{1,0:T(8,128)(2,1)} %collective-permute-done.28.refs_5_), channel_id=1, source_target_pairs={{16,24},{18,26},{20,28},{22,30},{17,25},{19,27},{21,29},{23,31}} | collective-permute-start | bytes 3145736 | tf_op jit(solution)/shard_map/ppermute | solution.py:262
  269.5 38.7 %collective-permute-start.32 = (bf16[2048,256]{1,0:T(8,128)(2,1)}, bf16[2048,256]{1,0:T(8,128)(2,1)}, u32[]{:S(2)}, u32[]{:S(2)}) collective-permute-start(bf16[2048,256]{1,0:T(8,128)(2,1)} %collective-permute-done.31.refs_9_), channel_id=1, source_target_pairs={{8,0},{10,2},{12,4},{14,6},{9,1},{11,3},{13,5},{15,7}} | collective-permute-start | bytes 3145736 | tf_op jit(solution)/shard_map/ppermute | solution.py:262
  274.4 31.1 %collective-permute-start.25 = (bf16[2,256,512]{2,1,0:T(8,128)(2,1)S(1)}, bf16[2,256,512]{2,1,0:T(8,128)(2,1)S(1)}, u32[]{:S(2)}, u32[]{:S(2)}) collective-permute-start(bf16[2,256,512]{2,1,0:T(8,128)(2,1)S(1)} %slice.75), channel_id=1, source_target_pairs={{0,4},{2,6},{4,0},{6,2},{8,12},{10,14},{12,8},{14,10},{16,20},{18,... | collective-permute-start | bytes 1572872 | tf_op jit(solution)/shard_map/ppermute | solution.py:255
  (29 other events, 425.7 us)

commit v2 on v1

v2 whole, which is shorter than its diff:
```python
import functools
import math

import jax
import jax.numpy as jnp
import ml_dtypes
import numpy as np
from jax import lax
from jax.experimental import pallas as pl
from jax.experimental.pallas import tpu as pltpu
from jax.sharding import PartitionSpec as P

HEAD_DIM = 128
WINDOW = 2048
PLANE = 4
MASKED = -1e30
VMEM = 56 * 1024 * 1024


def split_bf16(array):
    high = array.astype(jnp.bfloat16)
    return high, (array - high.astype(jnp.float32)).astype(jnp.bfloat16)


def mm(a, b):
    return jnp.dot(a, b, preferred_element_type=jnp.float32)


def dft_matrices(taps):
    size = 2 * taps
    n = np.arange(size)
    k = np.arange(taps)
    angle = 2 * np.pi * ((k[:, None] * n[None, :]) % size) / size
    cosine, sine = np.cos(angle), np.sin(angle)
    forward = np.concatenate([cosine, -sine], 0)
    forward[taps] = (-1.0) ** n
    weight = np.full(taps, 2.0 / size)
    weight[0] = 1.0 / size
    inverse = np.concatenate([cosine * weight[:, None], -sine * weight[:, None]], 0)
    inverse[taps] = (-1.0) ** n / size
    inverse = inverse.T[taps:]

    def halves(array):
        array = array.astype(np.float32)
        high = array.astype(ml_dtypes.bfloat16)
        return high, (array - high.astype(np.float32)).astype(ml_dtypes.bfloat16)

    return [jnp.asarray(m) for m in halves(forward) + halves(inverse)]


def fir_kernel(rim, product, gate, filters, f_hi, f_lo, g_hi, g_lo, out):
    taps = filters.shape[0]
    rows = product.shape[0]
    h_hi, h_lo = split_bf16(filters[...])
    spectrum = (
        mm(f_hi[:, :taps], h_hi) + mm(f_hi[:, :taps], h_lo) + mm(f_lo[:, :taps], h_hi)
    )
    first = lax.broadcasted_iota(jnp.int32, (taps, spectrum.shape[1]), 0) == 0
    h_re, h_im = spectrum[:taps], spectrum[taps:]
    h_re2 = jnp.where(first, h_im, h_re)
    h_im = jnp.where(first, 0.0, h_im)
    for start in range(0, rows, taps):
        before = rim[...] if start == 0 else product[start - taps : start]
        x = jnp.concatenate([before, product[start : start + taps]], 0)
        xs = mm(f_hi[...], x) + mm(f_lo[...], x)
        x_re, x_im = xs[:taps], xs[taps:]
        y = jnp.concatenate([x_re * h_re - x_im * h_im, x_re * h_im + x_im * h_re2], 0)
        y_hi, y_lo = split_bf16(y)
        filtered = mm(g_hi[...], y_hi) + mm(g_hi[...], y_lo) + mm(g_lo[...], y_hi)
        span = slice(start, start + taps)
        out[span] = (gate[span].astype(jnp.float32) * filtered).astype(out.dtype)


def fir(rim, product, gate, filters):
    taps, width = filters.shape
    rows = product.shape[0]
    tile = min(512, width)
    mats = dft_matrices(taps)
    column = lambda n: pl.BlockSpec((n, tile), lambda i: (0, i))
    return pl.pallas_call(
        fir_kernel,
        grid=(width // tile,),
        in_specs=[column(taps), column(rows), column(rows), column(taps)]
        + [pl.BlockSpec(m.shape, lambda i: (0, 0)) for m in mats],
        out_specs=column(rows),
        out_shape=jax.ShapeDtypeStruct((rows, width), jnp.bfloat16),
        compiler_params=pltpu.CompilerParams(vmem_limit_bytes=VMEM),
        cost_estimate=pl.CostEstimate(
            flops=2 * width * (10 * rows * taps + 6 * taps * taps),
            bytes_accessed=8 * rows * width,
            transcendentals=0,
        ),
    )(rim, product, gate, filters, *mats)


def attend_kernel(kind, first, last, info, q_ref, k_ref, v_ref, *refs):
    refs = list(refs)
    if not first:
        acc_in, stat_in = refs.pop(0), refs.pop(0)
    out, stat_out = refs
    plane, rows = k_ref.shape[0], k_ref.shape[2]
    me = info[0]
    factor = math.log2(math.e) / math.sqrt(HEAD_DIM)
    half = HEAD_DIM // 2

    def write(i, top, total, acc):
        if last:
            out[me ^ i] = (acc * (1.0 / total)).astype(out.dtype)
            level = jnp.broadcast_to(top + jnp.log2(total), (rows, HEAD_DIM))
            stat_out[0, me ^ i] = level.T[0:8]
        else:
            out[me ^ i] = acc
            lane = lax.broadcasted_iota(jnp.int32, (rows, HEAD_DIM), 1)
            stat_out[me ^ i] = jnp.where(lane < half, top, total)

    def previous(i):
        stat = stat_in[me ^ i]
        return stat[:, 0:1], stat[:, half : half + 1], acc_in[me ^ i]

    def attend(i):
        blocks = range(plane)
        if kind != "full":
            blocks = range(i + 1) if kind == "causal" else range(i, plane)
        q = q_ref[me ^ i]
        scores = []
        for j in blocks:
            s = lax.dot_general(
                q, k_ref[me ^ j, 0], (((1,), (1,)), ((), ())), preferred_element_type=jnp.float32
            ) * factor
            if j == i and kind != "full":
                row = lax.broadcasted_iota(jnp.int32, s.shape, 0)
                col = lax.broadcasted_iota(jnp.int32, s.shape, 1)
                s = jnp.where(col <= row if kind == "causal" else col > row, s, MASKED)
            scores.append(s)
        top = functools.reduce(jnp.maximum, scores).max(axis=1, keepdims=True)
        if not first:
            old_top, old_total, old_acc = previous(i)
            top = jnp.maximum(top, old_top)
        acc, sums = None, None
        for j, s in zip(blocks, scores):
            w = jnp.exp2(s - top)
            sums = w if sums is None else sums + w
            term = mm(w.astype(jnp.bfloat16), v_ref[me ^ j, 0])
            acc = term if acc is None else acc + term
        total = sums.sum(axis=1, keepdims=True)
        if not first:
            shrink = jnp.exp2(old_top - top)
            total = total + shrink * old_total
            acc = acc + shrink * old_acc
        write(i, top, total, acc)

    def run():
        for i in range(plane):
            attend(i)

    if first:
        run()
    else:

        @pl.when(info[1] > 0)
        def _():
            run()

        @pl.when(info[1] == 0)
        def _():
            for i in range(plane):
                write(i, *previous(i))


def attend(kind, last, info, queries, pairs, carry=(), dtype=jnp.float32):
    plane, rows, width = queries.shape
    heads = width // HEAD_DIM
    mine = pl.BlockSpec((plane, rows, HEAD_DIM), lambda h, info: (0, 0, h))
    keys = pl.BlockSpec((plane, 1, rows, HEAD_DIM), lambda h, info: (0, 0, 0, h))
    values = pl.BlockSpec((plane, 1, rows, HEAD_DIM), lambda h, info: (0, 1, 0, h))
    state = jax.ShapeDtypeStruct(queries.shape, jnp.float32)
    if last:
        out_specs = (mine, pl.BlockSpec((1, plane, 8, rows), lambda h, info: (h, 0, 0, 0)))
        out_shape = (
            jax.ShapeDtypeStruct(queries.shape, dtype),
            jax.ShapeDtypeStruct((heads, plane, 8, rows), jnp.float32),
        )
    else:
        out_specs, out_shape = (mine, mine), (state, state)
    scores = heads * (plane * rows) ** 2 // (1 if kind == "full" else 2)
    return pl.pallas_call(
        functools.partial(attend_kernel, kind, not carry, last),
        grid_spec=pltpu.PrefetchScalarGridSpec(
            num_scalar_prefetch=1,
            grid=(heads,),
            in_specs=[mine, keys, values] + [mine] * len(carry),
            out_specs=out_specs,
        ),
        out_shape=out_shape,
        compiler_params=pltpu.CompilerParams(vmem_limit_bytes=VMEM),
        cost_estimate=pl.CostEstimate(
            flops=4 * scores * HEAD_DIM, bytes_accessed=12 * queries.size, transcendentals=scores
        ),
    )(info, queries, pairs, pairs, *carry)


def merge_kernel(info, one_ref, level_one, two_ref, level_two, out):
    rows = one_ref.shape[1]
    for h in range(one_ref.shape[2] // HEAD_DIM):
        span = slice(h * HEAD_DIM, (h + 1) * HEAD_DIM)
        one, two = level_one[h, 0, 0:1], level_two[h, 0, 0:1]
        two = jnp.where(info[0] > 0, two, MASKED)
        top = jnp.maximum(one, two)
        one, two = jnp.exp2(one - top), jnp.exp2(two - top)
        share = jnp.broadcast_to(two * (1.0 / (one + two)), (HEAD_DIM, rows)).T
        first, second = one_ref[0, :, span], two_ref[0, :, span].astype(jnp.float32)
        out[0, :, span] = (first + share * (second - first)).astype(out.dtype)


def merge(info, one, level_one, two, level_two):
    plane, rows, width = one.shape
    block = pl.BlockSpec((1, rows, width), lambda i, info: (i, 0, 0))
    level = pl.BlockSpec((level_one.shape[0], 1, 8, rows), lambda i, info: (0, i, 0, 0))
    return pl.pallas_call(
        merge_kernel,
        grid_spec=pltpu.PrefetchScalarGridSpec(
            num_scalar_prefetch=1,
            grid=(plane,),
            in_specs=[block, level, block, level],
            out_specs=block,
        ),
        out_shape=jax.ShapeDtypeStruct(one.shape, jnp.bfloat16),
        compiler_params=pltpu.CompilerParams(vmem_limit_bytes=VMEM),
        cost_estimate=pl.CostEstimate(
            flops=4 * one.size, bytes_accessed=8 * one.size, transcendentals=0
        ),
    )(info, one, level_one, two, level_two)


def project_kernel(levels, n_tp, splits, by_rows, info, *refs):
    parts, weights = refs[:splits], refs[splits:-4]
    mine, others, a, acc = refs[-4:]
    level, group, step = info[0], info[1], pl.program_id(0)
    plane = mine.shape[0]
    rows = a.shape[0] // plane
    share = levels // n_tp
    if by_rows:
        for r, part in enumerate(parts):
            a[r * rows : (r + 1) * rows] = part[...]
    else:
        for s, part in enumerate(parts):

            @pl.when(step == s)
            def _(s=s, part=part):
                for r in range(plane):
                    a[r * rows : (r + 1) * rows] = part[r ^ s]

    @pl.when(step == 0)
    def _():
        acc[...] = jnp.zeros_like(acc)

    for index, w in enumerate(weights):
        target = level + (index - (levels - 1))

        @pl.when((target >= 0) & (target < levels))
        def _(w=w, target=target):
            acc[target] += mm(a[...], w[...])

    @pl.when(step == pl.num_programs(0) - 1)
    def _():
        for t in range(levels):
            ahead = (t // share + n_tp - group) % n_tp

            @pl.when(ahead == 0)
            def _(t=t):
                for r in range(plane):
                    mine[r, t % share] = acc[t, r * rows : (r + 1) * rows].astype(mine.dtype)

            @pl.when(ahead > 0)
            def _(t=t, ahead=ahead):
                for r in range(plane):
                    others[ahead - 1, r, t % share] = acc[t, r * rows : (r + 1) * rows].astype(
                        others.dtype
                    )


def project(levels, n_tp, info, parts, weights):
    by_rows = parts[0].ndim == 2
    weights = [w if isinstance(w, tuple) else (w[None], 0) for w in weights]
    width, columns = weights[0][0].shape[1:]
    rows = parts[0].shape[-2]
    depth = width // PLANE
    share = levels // n_tp
    if by_rows:
        part_spec = pl.BlockSpec((rows, depth), lambda k, info: (0, k))
    else:
        part_spec = pl.BlockSpec((PLANE, rows, depth), lambda k, info: (0, 0, 0))
    block = (PLANE, share, rows, columns)
    return pl.pallas_call(
        functools.partial(project_kernel, levels, n_tp, len(parts), by_rows),
        grid_spec=pltpu.PrefetchScalarGridSpec(
            num_scalar_prefetch=1,
            grid=(PLANE,),
            in_specs=[part_spec] * len(parts)
            + [
                pl.BlockSpec((pl.squeezed, depth, columns), lambda k, info, i=i: (i, k, 0))
                for _, i in weights
            ],
            out_specs=(
                pl.BlockSpec(block, lambda k, info: (0,) * 4),
                pl.BlockSpec((n_tp - 1,) + block, lambda k, info: (0,) * 5),
            ),
            scratch_shapes=[
                pltpu.VMEM((PLANE * rows, depth), jnp.bfloat16),
                pltpu.VMEM((levels, PLANE * rows, columns), jnp.float32),
            ],
        ),
        out_shape=(
            jax.ShapeDtypeStruct(block, jnp.bfloat16),
            jax.ShapeDtypeStruct((n_tp - 1,) + block, jnp.bfloat16),
        ),
        compiler_params=pltpu.CompilerParams(vmem_limit_bytes=VMEM),
        cost_estimate=pl.CostEstimate(
            flops=2 * PLANE * rows * width * columns * levels,
            bytes_accessed=16 * 1024 * 1024,
            transcendentals=0,
        ),
    )(info, *parts, *[w for w, _ in weights])


def assemble_kernel(info, *refs):
    pieces, out = refs[:-1], refs[-1]
    share, rows, columns = pieces[0].shape
    for s, piece in enumerate(pieces):
        for t in range(share):
            start = pl.multiple_of((t * PLANE + (info[0] ^ s)) * columns, columns)
            out[:, pl.ds(start, columns)] = piece[t]


def assemble(info, pieces):
    share, rows, columns = pieces[0].shape
    if columns % 128:
        natural = [
            lax.select_n(info[0], *[pieces[t ^ j] for t in range(PLANE)]) for j in range(PLANE)
        ]
        return jnp.stack(natural, 1).transpose(2, 0, 1, 3).reshape(rows, -1)
    return pl.pallas_call(
        assemble_kernel,
        grid_spec=pltpu.PrefetchScalarGridSpec(
            num_scalar_prefetch=1,
            grid=(1,),
            in_specs=[pl.BlockSpec(p.shape, lambda i, info: (0, 0, 0)) for p in pieces],
            out_specs=pl.BlockSpec((rows, share * PLANE * columns), lambda i, info: (0, 0)),
        ),
        out_shape=jax.ShapeDtypeStruct((rows, share * PLANE * columns), jnp.bfloat16),
        compiler_params=pltpu.CompilerParams(vmem_limit_bytes=VMEM),
    )(info, *pieces)


def per_device(hyena_in, filters, attn_in, out_weight, attn_weight):
    rows, _, width = hyena_in.shape
    taps = filters.shape[0]
    n_ctx, n_tp = lax.axis_size("ctx"), lax.axis_size("tp")
    levels = n_ctx // PLANE
    device_index = lax.axis_index("ctx")
    group = lax.axis_index("tp")
    me, level = device_index % PLANE, device_index // PLANE
    chunk = width // PLANE
    assert WINDOW == 2 * PLANE * rows and levels > 2 and levels % n_tp == 0

    def flags(*values):
        return jnp.stack([jnp.asarray(v).astype(jnp.int32) for v in values])

    def after(value, *others):
        return lax.optimization_barrier((value, *others))[0]

    def swap(block, relative):
        return lax.ppermute(block, "ctx", [(i, i ^ relative) for i in range(n_ctx)])

    def move(block, direction, first, last):
        sources = range(first * PLANE, (last + 1) * PLANE)
        return lax.ppermute(block, "ctx", [(i, i + direction * PLANE) for i in sources])

    def climb(block, direction, step=1):
        if direction > 0:
            return move(block, 1, step - 1, levels - 2)
        return move(block, -1, 1, levels - step)

    def across_plane(block):
        one, two = swap(block, 1), swap(block, 2)
        half = block.shape[0] // 2
        three = jnp.concatenate([swap(one[:half], 2), swap(two[half:], 1)], 0)
        return [block, one, two, three]

    last_rows = hyena_in[rows - taps :]
    rim = (last_rows[:, 0].astype(jnp.float32) * last_rows[:, 2].astype(jnp.float32)).astype(
        jnp.bfloat16
    )
    rim = lax.ppermute(rim, "ctx", [(i, i + 1) for i in range(n_ctx - 1)])

    def piece(index):
        block = lax.dynamic_slice(attn_in, (0, 0, index * chunk), (rows, 3, chunk))
        return block.transpose(1, 0, 2)

    sent = [piece(me ^ s) for s in range(PLANE)]
    pieces = [sent[0]] + [swap(sent[s], s) for s in range(1, PLANE)]
    attn_rows = attn_weight.reshape(PLANE, chunk, -1)
    attn_weight = jnp.concatenate(
        [lax.dynamic_index_in_dim(attn_rows, me ^ s, 0, False) for s in range(PLANE)], 0
    )
    weights = jnp.stack([out_weight, attn_weight])
    both_up = climb(weights, 1)
    both_down = climb(after(weights, rim), -1)
    product = (hyena_in[:, 0].astype(jnp.float32) * hyena_in[:, 2].astype(jnp.float32)).astype(
        jnp.bfloat16
    )
    product, gate, *pieces = lax.optimization_barrier((product, hyena_in[:, 1], *pieces))

    queries = jnp.stack([p[0] for p in pieces])
    pairs = jnp.stack([p[1:] for p in pieces])
    lower_pairs = move(pairs, 1, 0, levels - 3)
    upper_queries = climb(queries, -1)
    own = attend("causal", True, flags(me, 1), queries, pairs)
    top = levels - 2
    both_up = after(both_up, own[0])
    both_top = move(both_up, 1, top, top)
    hyena_act = fir(after(rim, both_up), product, gate, filters)
    upper_queries = after(upper_queries, hyena_act)
    hyena_one, hyena_two = (swap(after(hyena_act, upper_queries), s) for s in (1, 2))
    carry = attend("full", False, flags(me, 1), upper_queries, pairs)
    both_down = after(both_down, carry[0])
    hyena_down2 = climb(both_down[0], -1, 2)
    lower_pairs = after(lower_pairs, carry[0])
    hyena_rest = move(after(both_up, lower_pairs)[0], 1, 1, top - 1)
    served, served_level = attend(
        "anti", True, flags(me, level > 0), upper_queries, lower_pairs, carry, jnp.bfloat16
    )
    hyena_one, hyena_two, both_top = lax.optimization_barrier(
        (hyena_one, hyena_two, after(both_top, served))
    )
    partial_up = climb(after(served, both_top), 1)
    level_up = climb(after(served_level, both_top), 1)
    half = rows // 2
    hyena_three = swap(hyena_one[:half], 2), swap(after(hyena_two, level_up)[half:], 1)
    hyena_down2 = after(hyena_down2, level_up)
    attn_down2 = climb(after(both_down, hyena_down2)[1], -1, 2)
    hyena_three = jnp.concatenate(lax.optimization_barrier(hyena_three), 0)
    hyena_parts = [hyena_act, hyena_one, hyena_two, hyena_three]
    hyena_up2 = both_top[0] + after(hyena_rest, hyena_three)
    hyena_ups, hyena_downs = [hyena_up2], [hyena_down2]
    attn_ups, attn_downs = [], [attn_down2]
    for step in range(3, levels):
        hyena_ups.append(climb(hyena_ups[-1], 1, step))
    partial_up = after(partial_up, hyena_up2)
    attn_rest = move(after(both_up, partial_up)[1], 1, 1, top - 1)
    attended = across_plane(merge(flags(level > 0), *own, partial_up, level_up))
    for step in range(3, levels):
        hyena_downs.append(climb(after(hyena_downs[-1], attn_downs[0], partial_up), -1, step))
    attn_ups.append(both_top[1] + attn_rest)
    for step in range(3, levels):
        attn_ups.append(climb(attn_ups[-1], 1, step))
        attn_downs.append(climb(after(attn_downs[-1], hyena_downs[-1]), -1, step))
    hyena_weights = hyena_ups[::-1] + [(both_up, 0), (weights, 0), (both_down, 0)] + hyena_downs
    attn_weights = attn_ups[::-1] + [(both_up, 1), (weights, 1), (both_down, 1)] + attn_downs

    def finish(parts, weights):
        mine, others = project(levels, n_tp, flags(level, group), parts, weights)
        total = mine.astype(jnp.float32)
        for shift in range(1, n_tp):
            got = lax.ppermute(
                others[shift - 1], "tp", [(i, (i + shift) % n_tp) for i in range(n_tp)]
            )
            total = total + got.astype(jnp.float32)
        total = total.astype(jnp.bfloat16)
        return assemble(flags(me), [total[0]] + [swap(total[s], s) for s in range(1, PLANE)])

    return (
        finish(hyena_parts, hyena_weights),
        finish(attended, attn_weights),
    )


def solution(mesh):
    in_specs = (
        P("ctx", None, "tp"),
        P(None, "tp"),
        P("ctx", None, "tp"),
        P("tp", "ctx"),
        P("tp", "ctx"),
    )
    out_specs = (P("ctx", "tp"), P("ctx", "tp"))
    return jax.shard_map(
        per_device, mesh=mesh, in_specs=in_specs, out_specs=out_specs, check_vma=False
    )
```

time: 353 us -> 278 us (0.79)
  waiting for transfers between devices: 166 us -> 110 us
  starting transfers between devices: 80.2 us -> 60.9 us
  local copies, waits for them, and re-layouts: 19.2 us -> 25.7 us
  other arithmetic: 14.2 us -> 8.65 us
    ppermute x17 -> x18, waiting for transfers between devices: 119 us -> 59.4 us  [the longest x15 59.4 us: move(): lax.ppermute(block, 'ctx', [(i, i + direction * PLANE) for i in sources])]
    ppermute x20 -> x17, starting transfers between devices: 31.5 us -> 19.4 us  [swap(): return lax.ppermute(block, 'ctx', [(i, i ^ relative) for i in range(n_ctx)])]
    ppermute x17 -> x18, starting transfers between devices: 48.7 us -> 41.5 us  [the longest x15 35.8 us: move(): lax.ppermute(block, 'ctx', [(i, i + direction * PLANE) for i in sources])]
    another operation x9 -> x6, other arithmetic: 9.23 us -> 3.24 us  [the longest x2 1.58 us: per_device(): weights = jnp.stack([out_weight, attn_weight])]
    squeeze x5 -> x8, local copies, waits for them, and re-layouts: 3.25 us -> 8.21 us  [the longest x1 1.67 us: per_device(): attn_rest = move(after(both_up, partial_up)[1], 1, 1, top - 1)]
    slice x1 -> x6, local copies, waits for them, and re-layouts: 0.83 us -> 5.12 us  [the longest x4 2.92 us: per_device(): queries = jnp.stack([p[0] for p in pieces])]
    unnamed x32 -> x45, local copies, waits for them, and re-layouts: 1.54 us -> 5.08 us
    ppermute x20 -> x17, waiting for transfers between devices: 47.7 us -> 50.9 us  [swap(): return lax.ppermute(block, 'ctx', [(i, i ^ relative) for i in range(n_ctx)])]
  transfers between devices with their start and end apart: 37 -> 35, of which waited for: 12 -> 13; matrix products, arithmetic and copies ran while one was open for 8% -> 10% of each run, Pallas kernels for 20% -> 24%
where the time goes in v2:
time: 278 us; the launch traced here: 276 us
  waiting for transfers between devices  110 us (40%)
  Pallas kernels  69 us (25%)
  starting transfers between devices  60.9 us (22%)
  local copies, waits for them, and re-layouts  25.7 us (9%)
  other arithmetic  8.65 us (3%)
    ppermute x15, waiting for transfers between devices, move(): lax.ppermute(block, 'ctx', [(i, i + direction * PLANE) for i in sources])  59.4 us
    ppermute x17, waiting for transfers between devices, swap(): return lax.ppermute(block, 'ctx', [(i, i ^ relative) for i in range(n_ctx)])  50.9 us
    ppermute x15, starting transfers between devices, move(): lax.ppermute(block, 'ctx', [(i, i + direction * PLANE) for i in sources])  35.8 us
    pallas_call x3, Pallas kernels, attend(): pl.pallas_call(functools.partial(attend_kernel, kind, not carry, last), g...  28.1 us
    pallas_call x2, Pallas kernels, project(): pl.pallas_call(functools.partial(project_kernel, levels, n_tp, len(parts)...  24.9 us
    ppermute x17, starting transfers between devices, swap(): return lax.ppermute(block, 'ctx', [(i, i ^ relative) for i in range(n_ctx)])  19.4 us
    pallas_call x1, Pallas kernels, fir(): pl.pallas_call(fir_kernel, grid=(width // tile,), in_specs=[column(taps),...  7.22 us
    ppermute x1, starting transfers between devices, per_device(): rim = lax.ppermute(rim, 'ctx', [(i, i + 1) for i in range(n_ctx - 1)])  5.68 us
  transfers between devices with their start and end apart: 35, of which 13 were waited for; matrix products, arithmetic and copies ran while one was open for 10% of the time, Pallas kernels for 24%

profile of v2, /device:TPU:0, one launch (start us, length us, event | category | flops | bytes accessed | tf_op | source)
XLA Modules:
  0.0 275.6 jit_solution(1427450087974104834)
XLA Ops:
  2.9 5.7 %collective-permute-start = (bf16[128,2048]{1,0:T(8,128)(2,1)}, bf16[128,2048]{1,0:T(8,128)(2,1)}, u32[]{:S(2)}, u32[]{:S(2)}) collective-permute-start(bf16[128,2048]{1,0:T(8,128)(2,1)} %fusion.1), channel_id=1, source_target_pairs={{0,2},{2,4},{4,6},{6,8},{8,10},{10,12},{12,14},{14,16},{16,18},{18... | collective-permute-start | bytes 1572872 | tf_op jit(solution)/shard_map/ppermute | solution.py:394
  11.3 4.0 %collective-permute-start.1 = (bf16[2,2048,256]{2,1,0:T(8,128)(2,1)}, bf16[2,2048,256]{2,1,0:T(8,128)(2,1)}, u32[]{:S(2)}, u32[]{:S(2)}) collective-permute-start(bf16[2,2048,256]{2,1,0:T(8,128)(2,1)} %pad_maximum_fusion.refs_7_), channel_id=1, source_target_pairs={{0,8},{2,10},{4,12},{6,14},{8,16},{10,18},{12,20},{14,22},{16,24},... | collective-permute-start | bytes 6291464 | tf_op jit(solution)/shard_map/ppermute | solution.py:377
  15.3 3.7 %dynamic-slice_bitcast_fusion = (bf16[3,256,512]{2,1,0:T(8,128)(2,1)}, bf16[3,256,512]{2,1,0:T(8,128)(2,1)}, bf16[3,256,512]{2,1,0:T(8,128)(2,1)}, bf16[3,256,512]{2,1,0:T(8,128)(2,1)}) fusion(bf16[256,3,2048]{2,0,1:T(8,128)(2,1)} %param.11, s32[]{:T(128)S(6)} %select_n.45, s32[]{:T(128)S(6)} %select_n.43, s32[]{:T(128)S(6)} %select_n.42, s32[]{:T(128)S(6)} %select_n.44), kind=kLoop, calls=%fused_computation.17 | loop fusion | bytes 6291472 | tf_op jit(solution)/shard_map/transpose | solution.py:398
  26.2 14.6 %collective-permute-done.4 = bf16[3,256,512]{2,1,0:T(8,128)(2,1)} collective-permute-done((bf16[3,256,512]{2,1,0:T(8,128)(2,1)}, bf16[3,256,512]{2,1,0:T(8,128)(2,1)}, u32[]{:S(2)}, u32[]{:S(2)}) %collective-permute-start.4) | collective-permute-done | bytes 786464 | tf_op jit(solution)/shard_map/ppermute | solution.py:373
  40.8 15.1 %collective-permute-done.2 = bf16[3,256,512]{2,1,0:T(8,128)(2,1)} collective-permute-done((bf16[3,256,512]{2,1,0:T(8,128)(2,1)}, bf16[3,256,512]{2,1,0:T(8,128)(2,1)}, u32[]{:S(2)}, u32[]{:S(2)}) %collective-permute-start.2) | collective-permute-done | bytes 786464 | tf_op jit(solution)/shard_map/ppermute | solution.py:373
  63.0 4.7 %collective-permute-start.9 = (bf16[4,2,256,512]{3,2,1,0:T(8,128)(2,1)S(1)}, bf16[4,2,256,512]{3,2,1,0:T(8,128)(2,1)S(1)}, u32[]{:S(2)}, u32[]{:S(2)}) collective-permute-start(bf16[4,2,256,512]{3,2,1,0:T(8,128)(2,1)S(1)} %pad_maximum_fusion.1.k_ref.v_ref), channel_id=1, source_target_pairs={{0,8},{2,10},{4,12},{6,14},{8,16},{10,18},{12,20},{14,22},{1,9},{3... | collective-permute-start | bytes 6291464 | tf_op jit(solution)/shard_map/ppermute | solution.py:377
  68.4 10.0 %shard_map.104 = (f32[4,256,512]{2,1,0:T(8,128)}, f32[4,4,8,256]{3,2,1,0:T(8,128)}) custom-call(s32[2]{0:T(128)} %get-tuple-element.98.info, bf16[4,256,512]{2,1,0:T(8,128)(2,1)} %copy-done.3, bf16[4,2,256,512]{3,2,1,0:T(8,128)(2,1)} %copy-done, bf16[4,2,256,512]{3,2,1,0:T(8,128)(2,1)} %copy-done), custom_call_target="tpu_custom_call" | custom-call | flops 1073741824 | bytes 6291456 | tf_op jit(solution)/shard_map/pallas_call | solution.py:186
  79.2 7.2 %shard_map.105.refs_0_ = bf16[256,2048]{1,0:T(8,128)(2,1)} custom-call(bf16[128,2048]{1,0:T(8,128)(2,1)} %collective-permute-done.rim, bf16[256,2048]{1,0:T(8,128)(2,1)} %fusion.product, bf16[256,2048]{1,0:T(8,128)(2,1)} %slice_bitcast_fusion.4.gate, f32[128,2048]{1,0:T(8,128)} %filters.1, bf16[256,256]{1,0:T(8,128)(2,1)} %constant.62.clone.f_hi, ...), custom_call_target="tpu_custom_call" | custom-call | flops 1744830464 | bytes 4194304 | tf_op jit(solution)/shard_map/pallas_call | solution.py:80
  86.4 9.2 %collective-permute-done.5.q_ref = bf16[4,256,512]{2,1,0:T(8,128)(2,1)} collective-permute-done((bf16[4,256,512]{2,1,0:T(8,128)(2,1)S(1)}, bf16[4,256,512]{2,1,0:T(8,128)(2,1)}, u32[]{:S(2)}, u32[]{:S(2)}) %collective-permute-start.5) | collective-permute-done | bytes 1048608 | tf_op jit(solution)/shard_map/ppermute | solution.py:377
  98.6 11.2 %shard_map.106 = (f32[4,256,512]{2,1,0:T(8,128)}, f32[4,256,512]{2,1,0:T(8,128)}) custom-call(s32[2]{0:T(128)} %get-tuple-element.98.info, bf16[4,256,512]{2,1,0:T(8,128)(2,1)} %collective-permute-done.5.q_ref, bf16[4,2,256,512]{3,2,1,0:T(8,128)(2,1)} %copy-done, bf16[4,2,256,512]{3,2,1,0:T(8,128)(2,1)} %copy-done), custom_call_target="tpu_custom_call" | custom-call | flops 2147483648 | bytes 6291456 | tf_op jit(solution)/shard_map/pallas_call | solution.py:186
  113.7 6.9 %shard_map.107 = (bf16[4,256,512]{2,1,0:T(8,128)(2,1)}, f32[4,4,8,256]{3,2,1,0:T(8,128)}) custom-call(s32[2]{0:T(128)} %get-tuple-element.99.info, bf16[4,256,512]{2,1,0:T(8,128)(2,1)} %collective-permute-done.5.q_ref, bf16[4,2,256,512]{3,2,1,0:T(8,128)(2,1)} %copy-done.1, bf16[4,2,256,512]{3,2,1,0:T(8,128)(2,1)} %copy-done.1, ...), custom_call_target="tpu_custom_call" | custom-call | flops 1073741824 | bytes 6291456 | tf_op jit(solution)/shard_map/pallas_call | solution.py:186
  120.6 9.5 %collective-permute-start.11 = (f32[4,4,8,256]{3,2,1,0:T(8,128)}, f32[4,4,8,256]{3,2,1,0:T(8,128)S(1)}, u32[]{:S(2)}, u32[]{:S(2)}) collective-permute-start(f32[4,4,8,256]{3,2,1,0:T(8,128)} %get-tuple-element.62), channel_id=1, source_target_pairs={{0,8},{2,10},{4,12},{6,14},{8,16},{10,18},{12,20},{14,22},{16,24},... | collective-permute-start | bytes 393224 | tf_op jit(solution)/shard_map/ppermute | solution.py:377
  137.2 4.0 %collective-permute-start.18 = (bf16[4,256,512]{2,1,0:T(8,128)(2,1)S(1)}, bf16[4,256,512]{2,1,0:T(8,128)(2,1)S(1)}, u32[]{:S(2)}, u32[]{:S(2)}) collective-permute-start(bf16[4,256,512]{2,1,0:T(8,128)(2,1)S(1)} %copy-done.21), channel_id=1, source_target_pairs={{0,8},{2,10},{4,12},{6,14},{8,16},{10,18},{12,20},{14,22},{16,24},... | collective-permute-start | bytes 3145736 | tf_op jit(solution)/shard_map/ppermute | solution.py:377
  145.4 2.6 collective-permute-done.12
  149.1 12.2 %collective-permute-done.18.two_ref = bf16[4,256,512]{2,1,0:T(8,128)(2,1)S(1)} collective-permute-done((bf16[4,256,512]{2,1,0:T(8,128)(2,1)S(1)}, bf16[4,256,512]{2,1,0:T(8,128)(2,1)S(1)}, u32[]{:S(2)}, u32[]{:S(2)}) %collective-permute-start.18) | collective-permute-done | bytes 1048608 | tf_op jit(solution)/shard_map/ppermute | solution.py:377
  163.9 3.0 %collective-permute-done.17 = bf16[2048,256]{1,0:T(8,128)(2,1)} collective-permute-done((bf16[2048,256]{1,0:T(8,128)(2,1)S(1)}, bf16[2048,256]{1,0:T(8,128)(2,1)}, u32[]{:S(2)}, u32[]{:S(2)}) %collective-permute-start.17) | collective-permute-done | bytes 1048608 | tf_op jit(solution)/shard_map/ppermute | solution.py:377
  168.2 4.2 %shard_map.110.refs_0_ = bf16[4,256,512]{2,1,0:T(8,128)(2,1)} custom-call(s32[1]{0:T(128)} %bitcast.21.info, f32[4,256,512]{2,1,0:T(8,128)} %get-tuple-element.46.one_ref, f32[4,4,8,256]{3,2,1,0:T(8,128)} %get-tuple-element.77.level_one, bf16[4,256,512]{2,1,0:T(8,128)(2,1)} %copy-done.8, f32[4,4,8,256]{3,2,1,0:T(8,128)} %copy-done.20), custom_call_target="tpu_custom_call" | custom-call | flops 2097152 | bytes 4194304 | tf_op jit(solution)/shard_map/pallas_call | solution.py:219
  178.9 28.9 %collective-permute-done.19 = bf16[2048,256]{1,0:T(8,128)(2,1)} collective-permute-done((bf16[2048,256]{1,0:T(8,128)(2,1)}, bf16[2048,256]{1,0:T(8,128)(2,1)}, u32[]{:S(2)}, u32[]{:S(2)}) %collective-permute-start.19) | collective-permute-done | bytes 1048608 | tf_op jit(solution)/shard_map/ppermute | solution.py:377
  212.8 11.8 %shard_map.108 = (bf16[4,2,256,256]{3,2,1,0:T(8,128)(2,1)}, bf16[1,4,2,256,256]{4,3,2,1,0:T(8,128)(2,1)}) custom-call(s32[2]{0:T(128)} %pad_add_fusion.info, bf16[256,2048]{1,0:T(8,128)(2,1)} %shard_map.105.refs_0_, bf16[256,2048]{1,0:T(8,128)(2,1)} %collective-permute-done.6.refs_1_, bf16[256,2048]{1,0:T(8,128)(2,1)} %collective-permute-done.7.refs_2_, ...), custom_call_target="tpu_custom_call" | custom-call | flops 4294967296 | bytes 16777216 | tf_op jit(solution)/shard_map/pallas_call | solution.py:294
  225.8 6.0 %collective-permute-done.30 = bf16[2048,256]{1,0:T(8,128)(2,1)} collective-permute-done((bf16[2048,256]{1,0:T(8,128)(2,1)}, bf16[2048,256]{1,0:T(8,128)(2,1)}, u32[]{:S(2)}, u32[]{:S(2)}) %collective-permute-start.30) | collective-permute-done | bytes 1048608 | tf_op jit(solution)/shard_map/ppermute | solution.py:377
  231.8 13.1 %shard_map.111 = (bf16[4,2,256,256]{3,2,1,0:T(8,128)(2,1)}, bf16[1,4,2,256,256]{4,3,2,1,0:T(8,128)(2,1)}) custom-call(s32[2]{0:T(128)} %pad_add_fusion.info, bf16[4,256,512]{2,1,0:T(8,128)(2,1)} %shard_map.110.refs_0_, bf16[4,256,512]{2,1,0:T(8,128)(2,1)} %collective-permute-done.24.refs_1_, bf16[4,256,512]{2,1,0:T(8,128)(2,1)} %copy-done.18, ...), custom_call_target="tpu_custom_call" | custom-call | flops 4294967296 | bytes 16777216 | tf_op jit(solution)/shard_map/pallas_call | solution.py:294
  252.2 3.9 %collective-permute-done.23.refs_3_ = bf16[2,256,256]{2,1,0:T(8,128)(2,1)S(1)} collective-permute-done((bf16[2,256,256]{2,1,0:T(8,128)(2,1)S(1)}, bf16[2,256,256]{2,1,0:T(8,128)(2,1)S(1)}, u32[]{:S(2)}, u32[]{:S(2)}) %collective-permute-start.23) | collective-permute-done | bytes 262176 | tf_op jit(solution)/shard_map/ppermute | solution.py:373
  256.2 5.5 %collective-permute-done.22.refs_2_ = bf16[2,256,256]{2,1,0:T(8,128)(2,1)S(1)} collective-permute-done((bf16[2,256,256]{2,1,0:T(8,128)(2,1)S(1)}, bf16[2,256,256]{2,1,0:T(8,128)(2,1)S(1)}, u32[]{:S(2)}, u32[]{:S(2)}) %collective-permute-start.22) | collective-permute-done | bytes 262176 | tf_op jit(solution)/shard_map/ppermute | solution.py:373
  267.4 5.1 %collective-permute-done.33.refs_2_ = bf16[2,256,256]{2,1,0:T(8,128)(2,1)S(1)} collective-permute-done((bf16[2,256,256]{2,1,0:T(8,128)(2,1)S(1)}, bf16[2,256,256]{2,1,0:T(8,128)(2,1)S(1)}, u32[]{:S(2)}, u32[]{:S(2)}) %collective-permute-start.33) | collective-permute-done | bytes 262176 | tf_op jit(solution)/shard_map/ppermute | solution.py:373
  (133 shorter events, 72.3 us)
Async XLA Ops:
  2.9 22.1 %collective-permute-start = (bf16[128,2048]{1,0:T(8,128)(2,1)}, bf16[128,2048]{1,0:T(8,128)(2,1)}, u32[]{:S(2)}, u32[]{:S(2)}) collective-permute-start(bf16[128,2048]{1,0:T(8,128)(2,1)} %fusion.1), channel_id=1, source_target_pairs={{0,2},{2,4},{4,6},{6,8},{8,10},{10,12},{12,14},{14,16},{16,18},{18... | collective-permute-start | bytes 1572872 | tf_op jit(solution)/shard_map/ppermute | solution.py:394
  11.3 67.1 %collective-permute-start.1 = (bf16[2,2048,256]{2,1,0:T(8,128)(2,1)}, bf16[2,2048,256]{2,1,0:T(8,128)(2,1)}, u32[]{:S(2)}, u32[]{:S(2)}) collective-permute-start(bf16[2,2048,256]{2,1,0:T(8,128)(2,1)} %pad_maximum_fusion.refs_7_), channel_id=1, source_target_pairs={{0,8},{2,10},{4,12},{6,14},{8,16},{10,18},{12,20},{14,22},{16,24},... | collective-permute-start | bytes 6291464 | tf_op jit(solution)/shard_map/ppermute | solution.py:377
  19.0 21.7 %collective-permute-start.4 = (bf16[3,256,512]{2,1,0:T(8,128)(2,1)}, bf16[3,256,512]{2,1,0:T(8,128)(2,1)}, u32[]{:S(2)}, u32[]{:S(2)}) collective-permute-start(bf16[3,256,512]{2,1,0:T(8,128)(2,1)} %get-tuple-element.82), channel_id=1, source_target_pairs={{0,6},{2,4},{4,2},{6,0},{8,14},{10,12},{12,10},{14,8},{16,22},{18,... | collective-permute-start | bytes 2359304 | tf_op jit(solution)/shard_map/ppermute | solution.py:373
  21.5 34.4 %collective-permute-start.2 = (bf16[3,256,512]{2,1,0:T(8,128)(2,1)}, bf16[3,256,512]{2,1,0:T(8,128)(2,1)}, u32[]{:S(2)}, u32[]{:S(2)}) collective-permute-start(bf16[3,256,512]{2,1,0:T(8,128)(2,1)} %get-tuple-element.83), channel_id=1, source_target_pairs={{0,2},{2,0},{4,6},{6,4},{8,10},{10,8},{12,14},{14,12},{16,18},{18,... | collective-permute-start | bytes 2359304 | tf_op jit(solution)/shard_map/ppermute | solution.py:373
  22.0 33.9 %collective-permute-start.3 = (bf16[3,256,512]{2,1,0:T(8,128)(2,1)}, bf16[3,256,512]{2,1,0:T(8,128)(2,1)}, u32[]{:S(2)}, u32[]{:S(2)}) collective-permute-start(bf16[3,256,512]{2,1,0:T(8,128)(2,1)} %get-tuple-element.85), channel_id=1, source_target_pairs={{0,4},{2,6},{4,0},{6,2},{8,12},{10,14},{12,8},{14,10},{16,20},{18,... | collective-permute-start | bytes 2359304 | tf_op jit(solution)/shard_map/ppermute | solution.py:373
  24.9 84.9 %collective-permute-start.15 = (bf16[2,2048,256]{2,1,0:T(8,128)(2,1)}, bf16[2,2048,256]{2,1,0:T(8,128)(2,1)}, u32[]{:S(2)}, u32[]{:S(2)}) collective-permute-start(bf16[2,2048,256]{2,1,0:T(8,128)(2,1)} %pad_maximum_fusion.refs_7_), channel_id=1, source_target_pairs={{8,0},{10,2},{12,4},{14,6},{16,8},{18,10},{20,12},{22,14},{24,16},... | collective-permute-start | bytes 6291464 | tf_op jit(solution)/shard_map/ppermute | solution.py:377
  59.0 36.6 %collective-permute-start.5 = (bf16[4,256,512]{2,1,0:T(8,128)(2,1)S(1)}, bf16[4,256,512]{2,1,0:T(8,128)(2,1)}, u32[]{:S(2)}, u32[]{:S(2)}) collective-permute-start(bf16[4,256,512]{2,1,0:T(8,128)(2,1)S(1)} %pad_maximum_fusion.2.q_ref), channel_id=1, source_target_pairs={{8,0},{10,2},{12,4},{14,6},{16,8},{18,10},{20,12},{22,14},{24,16},... | collective-permute-start | bytes 3145736 | tf_op jit(solution)/shard_map/ppermute | solution.py:377
  63.0 49.4 %collective-permute-start.9 = (bf16[4,2,256,512]{3,2,1,0:T(8,128)(2,1)S(1)}, bf16[4,2,256,512]{3,2,1,0:T(8,128)(2,1)S(1)}, u32[]{:S(2)}, u32[]{:S(2)}) collective-permute-start(bf16[4,2,256,512]{3,2,1,0:T(8,128)(2,1)S(1)} %pad_maximum_fusion.1.k_ref.v_ref), channel_id=1, source_target_pairs={{0,8},{2,10},{4,12},{6,14},{8,16},{10,18},{12,20},{14,22},{1,9},{3... | collective-permute-start | bytes 6291464 | tf_op jit(solution)/shard_map/ppermute | solution.py:377
  78.4 42.2 %collective-permute-start.8 = (bf16[2,2048,256]{2,1,0:T(8,128)(2,1)}, bf16[2,2048,256]{2,1,0:T(8,128)(2,1)S(1)}, u32[]{:S(2)}, u32[]{:S(2)}) collective-permute-start(bf16[2,2048,256]{2,1,0:T(8,128)(2,1)} %collective-permute-done.1.refs_6_), channel_id=1, source_target_pairs={{16,24},{18,26},{20,28},{22,30},{17,25},{19,27},{21,29},{23,31}} | collective-permute-start | bytes 6291464 | tf_op jit(solution)/shard_map/ppermute | solution.py:377
  95.6 25.0 %collective-permute-start.7 = (bf16[256,2048]{1,0:T(8,128)(2,1)}, bf16[256,2048]{1,0:T(8,128)(2,1)}, u32[]{:S(2)}, u32[]{:S(2)}) collective-permute-start(bf16[256,2048]{1,0:T(8,128)(2,1)} %shard_map.105.refs_0_), channel_id=1, source_target_pairs={{0,4},{2,6},{4,0},{6,2},{8,12},{10,14},{12,8},{14,10},{16,20},{18,... | collective-permute-start | bytes 3145736 | tf_op jit(solution)/shard_map/ppermute | solution.py:373
  97.1 23.5 %collective-permute-start.6 = (bf16[256,2048]{1,0:T(8,128)(2,1)}, bf16[256,2048]{1,0:T(8,128)(2,1)}, u32[]{:S(2)}, u32[]{:S(2)}) collective-permute-start(bf16[256,2048]{1,0:T(8,128)(2,1)} %shard_map.105.refs_0_), channel_id=1, source_target_pairs={{0,2},{2,0},{4,6},{6,4},{8,10},{10,8},{12,14},{14,12},{16,18},{18,... | collective-permute-start | bytes 3145736 | tf_op jit(solution)/shard_map/ppermute | solution.py:373
  111.1 30.1 %collective-permute-start.16 = (bf16[2048,256]{1,0:T(8,128)(2,1)S(1)}, bf16[2048,256]{1,0:T(8,128)(2,1)}, u32[]{:S(2)}, u32[]{:S(2)}) collective-permute-start(bf16[2048,256]{1,0:T(8,128)(2,1)S(1)} %slice_bitcast_fusion.2), channel_id=1, source_target_pairs={{8,0},{10,2},{12,4},{14,6},{16,8},{18,10},{20,12},{22,14},{9,1},{1... | collective-permute-start | bytes 3145736 | tf_op jit(solution)/shard_map/ppermute | solution.py:377
  131.5 17.5 %collective-permute-start.13 = (bf16[2048,256]{1,0:T(8,128)(2,1)S(1)}, bf16[2048,256]{1,0:T(8,128)(2,1)S(1)}, u32[]{:S(2)}, u32[]{:S(2)}) collective-permute-start(bf16[2048,256]{1,0:T(8,128)(2,1)S(1)} %slice_bitcast_fusion.3), channel_id=1, source_target_pairs={{8,16},{10,18},{12,20},{14,22},{9,17},{11,19},{13,21},{15,23}} | collective-permute-start | bytes 3145736 | tf_op jit(solution)/shard_map/ppermute | solution.py:377
  137.2 24.1 %collective-permute-start.18 = (bf16[4,256,512]{2,1,0:T(8,128)(2,1)S(1)}, bf16[4,256,512]{2,1,0:T(8,128)(2,1)S(1)}, u32[]{:S(2)}, u32[]{:S(2)}) collective-permute-start(bf16[4,256,512]{2,1,0:T(8,128)(2,1)S(1)} %copy-done.21), channel_id=1, source_target_pairs={{0,8},{2,10},{4,12},{6,14},{8,16},{10,18},{12,20},{14,22},{16,24},... | collective-permute-start | bytes 3145736 | tf_op jit(solution)/shard_map/ppermute | solution.py:377
  142.5 24.4 %collective-permute-start.17 = (bf16[2048,256]{1,0:T(8,128)(2,1)S(1)}, bf16[2048,256]{1,0:T(8,128)(2,1)}, u32[]{:S(2)}, u32[]{:S(2)}) collective-permute-start(bf16[2048,256]{1,0:T(8,128)(2,1)S(1)} %slice_bitcast_fusion.1), channel_id=1, source_target_pairs={{8,0},{10,2},{12,4},{14,6},{16,8},{18,10},{20,12},{22,14},{9,1},{1... | collective-permute-start | bytes 3145736 | tf_op jit(solution)/shard_map/ppermute | solution.py:377
  166.9 40.9 %collective-permute-start.19 = (bf16[2048,256]{1,0:T(8,128)(2,1)}, bf16[2048,256]{1,0:T(8,128)(2,1)}, u32[]{:S(2)}, u32[]{:S(2)}) collective-permute-start(bf16[2048,256]{1,0:T(8,128)(2,1)} %collective-permute-done.16), channel_id=1, source_target_pairs={{8,0},{10,2},{12,4},{14,6},{9,1},{11,3},{13,5},{15,7}} | collective-permute-start | bytes 3145736 | tf_op jit(solution)/shard_map/ppermute | solution.py:377
  172.4 36.7 %collective-permute-start.25 = (bf16[4,256,512]{2,1,0:T(8,128)(2,1)}, bf16[4,256,512]{2,1,0:T(8,128)(2,1)S(1)}, u32[]{:S(2)}, u32[]{:S(2)}) collective-permute-start(bf16[4,256,512]{2,1,0:T(8,128)(2,1)} %shard_map.110.refs_0_), channel_id=1, source_target_pairs={{0,4},{2,6},{4,0},{6,2},{8,12},{10,14},{12,8},{14,10},{16,20},{18,... | collective-permute-start | bytes 3145736 | tf_op jit(solution)/shard_map/ppermute | solution.py:373
  173.7 35.8 %collective-permute-start.24 = (bf16[4,256,512]{2,1,0:T(8,128)(2,1)}, bf16[4,256,512]{2,1,0:T(8,128)(2,1)}, u32[]{:S(2)}, u32[]{:S(2)}) collective-permute-start(bf16[4,256,512]{2,1,0:T(8,128)(2,1)} %shard_map.110.refs_0_), channel_id=1, source_target_pairs={{0,2},{2,0},{4,6},{6,4},{8,10},{10,8},{12,14},{14,12},{16,18},{18,... | collective-permute-start | bytes 3145736 | tf_op jit(solution)/shard_map/ppermute | solution.py:373
  175.4 37.4 %collective-permute-start.14 = (bf16[2048,256]{1,0:T(8,128)(2,1)S(1)}, bf16[2048,256]{1,0:T(8,128)(2,1)}, u32[]{:S(2)}, u32[]{:S(2)}) collective-permute-start(bf16[2048,256]{1,0:T(8,128)(2,1)S(1)} %bitcast_add_fusion.1), channel_id=1, source_target_pairs={{16,24},{18,26},{20,28},{22,30},{17,25},{19,27},{21,29},{23,31}} | collective-permute-start | bytes 3145736 | tf_op jit(solution)/shard_map/ppermute | solution.py:377
  177.2 48.6 %collective-permute-start.29 = (bf16[2048,256]{1,0:T(8,128)(2,1)S(1)}, bf16[2048,256]{1,0:T(8,128)(2,1)}, u32[]{:S(2)}, u32[]{:S(2)}) collective-permute-start(bf16[2048,256]{1,0:T(8,128)(2,1)S(1)} %bitcast_add_fusion), channel_id=1, source_target_pairs={{16,24},{18,26},{20,28},{22,30},{17,25},{19,27},{21,29},{23,31}} | collective-permute-start | bytes 3145736 | tf_op jit(solution)/shard_map/ppermute | solution.py:377
  207.9 24.0 %collective-permute-start.30 = (bf16[2048,256]{1,0:T(8,128)(2,1)}, bf16[2048,256]{1,0:T(8,128)(2,1)}, u32[]{:S(2)}, u32[]{:S(2)}) collective-permute-start(bf16[2048,256]{1,0:T(8,128)(2,1)} %collective-permute-done.17), channel_id=1, source_target_pairs={{8,0},{10,2},{12,4},{14,6},{9,1},{11,3},{13,5},{15,7}} | collective-permute-start | bytes 3145736 | tf_op jit(solution)/shard_map/ppermute | solution.py:377
  224.6 20.3 %collective-permute-start.20 = (bf16[4,2,256,256]{3,2,1,0:T(8,128)(2,1)}, bf16[4,2,256,256]{3,2,1,0:T(8,128)(2,1)S(1)}, u32[]{:S(2)}, u32[]{:S(2)}) collective-permute-start(bf16[4,2,256,256]{3,2,1,0:T(8,128)(2,1)} %bitcast.80), channel_id=1, source_target_pairs={{0,1},{1,0},{2,3},{3,2},{4,5},{5,4},{6,7},{7,6},{8,9},{9,8},{10,11... | collective-permute-start | bytes 3145736 | tf_op jit(solution)/shard_map/ppermute | solution.py:465
  250.6 16.8 %collective-permute-start.34 = (bf16[2,256,256]{2,1,0:T(8,128)(2,1)S(1)}, bf16[2,256,256]{2,1,0:T(8,128)(2,1)S(1)}, u32[]{:S(2)}, u32[]{:S(2)}) collective-permute-start(bf16[2,256,256]{2,1,0:T(8,128)(2,1)S(1)} %get-tuple-element.86), channel_id=1, source_target_pairs={{0,6},{2,4},{4,2},{6,0},{8,14},{10,12},{12,10},{14,8},{16,22},{18,... | collective-permute-start | bytes 786440 | tf_op jit(solution)/shard_map/ppermute | solution.py:373
  252.2 20.3 %collective-permute-start.33 = (bf16[2,256,256]{2,1,0:T(8,128)(2,1)S(1)}, bf16[2,256,256]{2,1,0:T(8,128)(2,1)S(1)}, u32[]{:S(2)}, u32[]{:S(2)}) collective-permute-start(bf16[2,256,256]{2,1,0:T(8,128)(2,1)S(1)} %get-tuple-element.87), channel_id=1, source_target_pairs={{0,4},{2,6},{4,0},{6,2},{8,12},{10,14},{12,8},{14,10},{16,20},{18,... | collective-permute-start | bytes 786440 | tf_op jit(solution)/shard_map/ppermute | solution.py:373
  (33 other events, 359.0 us)

commit v3 on v2

--- a/solution.py
+++ b/solution.py
@@ -14,7 +14,9 @@
 WINDOW = 2048
 PLANE = 4
 MASKED = -1e30
+LEVEL_ROWS = 16
 VMEM = 56 * 1024 * 1024
+CHEAP = pl.CostEstimate(flops=1, bytes_accessed=1, transcendentals=0)
 
 
 def split_bf16(array):
@@ -85,19 +87,33 @@
         out_specs=column(rows),
         out_shape=jax.ShapeDtypeStruct((rows, width), jnp.bfloat16),
         compiler_params=pltpu.CompilerParams(vmem_limit_bytes=VMEM),
-        cost_estimate=pl.CostEstimate(
-            flops=2 * width * (10 * rows * taps + 6 * taps * taps),
-            bytes_accessed=8 * rows * width,
-            transcendentals=0,
-        ),
+        cost_estimate=CHEAP,
     )(rim, product, gate, filters, *mats)
+
+
+def pack_level(level):
+    pieces, rest = [], level
+    for _ in range(3):
+        term = rest.astype(jnp.bfloat16).astype(jnp.float32)
+        pieces += [term[:, c : c + HEAD_DIM] for c in range(0, level.shape[1], HEAD_DIM)]
+        rest = rest - term
+    pieces += [jnp.zeros((LEVEL_ROWS - len(pieces), HEAD_DIM), jnp.float32)]
+    return jnp.concatenate(pieces, 0).astype(jnp.bfloat16)
+
+
+def unpack_level(block, rows):
+    block = block.astype(jnp.float32)
+    count = rows // HEAD_DIM
+    total = block[0:count] + block[count : 2 * count] + block[2 * count : 3 * count]
+    return jnp.concatenate([total[c : c + 1] for c in range(count)], 1)
 
 
 def attend_kernel(kind, first, last, info, q_ref, k_ref, v_ref, *refs):
     refs = list(refs)
     if not first:
         acc_in, stat_in = refs.pop(0), refs.pop(0)
-    out, stat_out = refs
+    packed = len(refs) == 1
+    out, stat_out = refs[0], refs[-1]
     plane, rows = k_ref.shape[0], k_ref.shape[2]
     me = info[0]
     factor = math.log2(math.e) / math.sqrt(HEAD_DIM)
@@ -105,9 +121,12 @@
 
     def write(i, top, total, acc):
         if last:
-            out[me ^ i] = (acc * (1.0 / total)).astype(out.dtype)
-            level = jnp.broadcast_to(top + jnp.log2(total), (rows, HEAD_DIM))
-            stat_out[0, me ^ i] = level.T[0:8]
+            out[me ^ i, :rows] = (acc * (1.0 / total)).astype(out.dtype)
+            level = jnp.broadcast_to(top + jnp.log2(total), (rows, HEAD_DIM)).T[0:1]
+            if packed:
+                out[me ^ i, rows:] = pack_level(level)
+            else:
+                stat_out[0, me ^ i] = jnp.broadcast_to(level, (8, rows))
         else:
             out[me ^ i] = acc
             lane = lax.broadcasted_iota(jnp.int32, (rows, HEAD_DIM), 1)
@@ -174,7 +193,11 @@
     keys = pl.BlockSpec((plane, 1, rows, HEAD_DIM), lambda h, info: (0, 0, 0, h))
     values = pl.BlockSpec((plane, 1, rows, HEAD_DIM), lambda h, info: (0, 1, 0, h))
     state = jax.ShapeDtypeStruct(queries.shape, jnp.float32)
-    if last:
+    if last and dtype == jnp.bfloat16:
+        tall = (plane, rows + LEVEL_ROWS)
+        out_specs = pl.BlockSpec(tall + (HEAD_DIM,), lambda h, info: (0, 0, h))
+        out_shape = jax.ShapeDtypeStruct(tall + (width,), dtype)
+    elif last:
         out_specs = (mine, pl.BlockSpec((1, plane, 8, rows), lambda h, info: (h, 0, 0, 0)))
         out_shape = (
             jax.ShapeDtypeStruct(queries.shape, dtype),
@@ -182,7 +205,6 @@
         )
     else:
         out_specs, out_shape = (mine, mine), (state, state)
-    scores = heads * (plane * rows) ** 2 // (1 if kind == "full" else 2)
     return pl.pallas_call(
         functools.partial(attend_kernel, kind, not carry, last),
         grid_spec=pltpu.PrefetchScalarGridSpec(
@@ -193,26 +215,24 @@
         ),
         out_shape=out_shape,
         compiler_params=pltpu.CompilerParams(vmem_limit_bytes=VMEM),
-        cost_estimate=pl.CostEstimate(
-            flops=4 * scores * HEAD_DIM, bytes_accessed=12 * queries.size, transcendentals=scores
-        ),
+        cost_estimate=CHEAP,
     )(info, queries, pairs, pairs, *carry)
 
 
-def merge_kernel(info, one_ref, level_one, two_ref, level_two, out):
+def merge_kernel(info, one_ref, level_one, two_ref, out):
     rows = one_ref.shape[1]
     for h in range(one_ref.shape[2] // HEAD_DIM):
         span = slice(h * HEAD_DIM, (h + 1) * HEAD_DIM)
-        one, two = level_one[h, 0, 0:1], level_two[h, 0, 0:1]
+        one, two = level_one[h, 0, 0:1], unpack_level(two_ref[0, rows:, span], rows)
         two = jnp.where(info[0] > 0, two, MASKED)
         top = jnp.maximum(one, two)
         one, two = jnp.exp2(one - top), jnp.exp2(two - top)
         share = jnp.broadcast_to(two * (1.0 / (one + two)), (HEAD_DIM, rows)).T
-        first, second = one_ref[0, :, span], two_ref[0, :, span].astype(jnp.float32)
+        first, second = one_ref[0, :, span], two_ref[0, :rows, span].astype(jnp.float32)
         out[0, :, span] = (first + share * (second - first)).astype(out.dtype)
 
 
-def merge(info, one, level_one, two, level_two):
+def merge(info, one, level_one, two):
     plane, rows, width = one.shape
     block = pl.BlockSpec((1, rows, width), lambda i, info: (i, 0, 0))
     level = pl.BlockSpec((level_one.shape[0], 1, 8, rows), lambda i, info: (0, i, 0, 0))
@@ -221,93 +241,96 @@
         grid_spec=pltpu.PrefetchScalarGridSpec(
             num_scalar_prefetch=1,
             grid=(plane,),
-            in_specs=[block, level, block, level],
+            in_specs=[
+                block,
+                level,
+                pl.BlockSpec((1,) + two.shape[1:], lambda i, info: (i, 0, 0)),
+            ],
             out_specs=block,
         ),
         out_shape=jax.ShapeDtypeStruct(one.shape, jnp.bfloat16),
         compiler_params=pltpu.CompilerParams(vmem_limit_bytes=VMEM),
-        cost_estimate=pl.CostEstimate(
-            flops=4 * one.size, bytes_accessed=8 * one.size, transcendentals=0
-        ),
-    )(info, one, level_one, two, level_two)
-
-
-def project_kernel(levels, n_tp, splits, by_rows, info, *refs):
-    parts, weights = refs[:splits], refs[splits:-4]
-    mine, others, a, acc = refs[-4:]
-    level, group, step = info[0], info[1], pl.program_id(0)
-    plane = mine.shape[0]
-    rows = a.shape[0] // plane
+        cost_estimate=CHEAP,
+    )(info, one, level_one, two)
+
+
+def project_kernel(levels, n_tp, part_index, weight_index, info, *refs):
+    splits = len(part_index)
+    parts, weights = refs[:splits], refs[splits:-8]
+    mine, others, a, w, y, sem_a, sem_w, sem_y = refs[-8:]
+    level, group = info[0], info[1]
+    plane, rows, columns = y.shape[1:]
+    depth = a.shape[1] // plane
     share = levels // n_tp
-    if by_rows:
-        for r, part in enumerate(parts):
-            a[r * rows : (r + 1) * rows] = part[...]
-    else:
-        for s, part in enumerate(parts):
-
-            @pl.when(step == s)
-            def _(s=s, part=part):
-                for r in range(plane):
-                    a[r * rows : (r + 1) * rows] = part[r ^ s]
-
-    @pl.when(step == 0)
-    def _():
-        acc[...] = jnp.zeros_like(acc)
-
-    for index, w in enumerate(weights):
-        target = level + (index - (levels - 1))
+
+    loads = []
+    for s, (part, index) in enumerate(zip(parts, part_index)):
+        if index is not None:
+            copy = pltpu.make_async_copy(part.at[index], a.at[pl.ds(s * rows, rows)], sem_a.at[s])
+            loads.append(copy)
+            continue
+        for r in range(plane):
+            loads.append(
+                pltpu.make_async_copy(
+                    part.at[r ^ s],
+                    a.at[pl.ds(r * rows, rows), pl.ds(s * depth, depth)],
+                    sem_a.at[s * plane + r],
+                )
+            )
+    for copy in loads:
+        copy.start()
+    for position, (weight, index) in enumerate(zip(weights, weight_index)):
+        target = level + (position - (levels - 1))
 
         @pl.when((target >= 0) & (target < levels))
-        def _(w=w, target=target):
-            acc[target] += mm(a[...], w[...])
-
-    @pl.when(step == pl.num_programs(0) - 1)
-    def _():
-        for t in range(levels):
-            ahead = (t // share + n_tp - group) % n_tp
-
-            @pl.when(ahead == 0)
-            def _(t=t):
-                for r in range(plane):
-                    mine[r, t % share] = acc[t, r * rows : (r + 1) * rows].astype(mine.dtype)
-
-            @pl.when(ahead > 0)
-            def _(t=t, ahead=ahead):
-                for r in range(plane):
-                    others[ahead - 1, r, t % share] = acc[t, r * rows : (r + 1) * rows].astype(
-                        others.dtype
-                    )
+        def _(weight=weight, index=index, target=target):
+            pltpu.make_async_copy(weight.at[index], w.at[target], sem_w.at[target]).start()
+
+    def store(t, act):
+        ahead = (t // share + n_tp - group) % n_tp
+
+        @pl.when(ahead == 0)
+        def _():
+            act(pltpu.make_async_copy(y.at[t], mine.at[:, t % share], sem_y.at[t]))
+
+        @pl.when(ahead > 0)
+        def _():
+            act(pltpu.make_async_copy(y.at[t], others.at[ahead - 1, :, t % share], sem_y.at[t]))
+
+    for copy in loads:
+        copy.wait()
+    for t in range(levels):
+        pltpu.make_async_copy(weights[0].at[0], w.at[t], sem_w.at[t]).wait()
+        for r in range(plane):
+            y[t, r] = mm(a[r * rows : (r + 1) * rows], w[t]).astype(y.dtype)
+        store(t, lambda copy: copy.start())
+    for t in range(levels):
+        store(t, lambda copy: copy.wait())
 
 
 def project(levels, n_tp, info, parts, weights):
-    by_rows = parts[0].ndim == 2
+    parts = [p if isinstance(p, tuple) else (p, None) for p in parts]
     weights = [w if isinstance(w, tuple) else (w[None], 0) for w in weights]
     width, columns = weights[0][0].shape[1:]
-    rows = parts[0].shape[-2]
-    depth = width // PLANE
-    share = levels // n_tp
-    if by_rows:
-        part_spec = pl.BlockSpec((rows, depth), lambda k, info: (0, k))
-    else:
-        part_spec = pl.BlockSpec((PLANE, rows, depth), lambda k, info: (0, 0, 0))
-    block = (PLANE, share, rows, columns)
+    rows = parts[0][0].shape[1]
+    block = (PLANE, levels // n_tp, rows, columns)
+    anywhere = pl.BlockSpec(memory_space=pl.ANY)
     return pl.pallas_call(
-        functools.partial(project_kernel, levels, n_tp, len(parts), by_rows),
+        functools.partial(
+            project_kernel, levels, n_tp, [i for _, i in parts], [i for _, i in weights]
+        ),
         grid_spec=pltpu.PrefetchScalarGridSpec(
             num_scalar_prefetch=1,
-            grid=(PLANE,),
-            in_specs=[part_spec] * len(parts)
-            + [
-                pl.BlockSpec((pl.squeezed, depth, columns), lambda k, info, i=i: (i, k, 0))
-                for _, i in weights
-            ],
-            out_specs=(
-                pl.BlockSpec(block, lambda k, info: (0,) * 4),
-                pl.BlockSpec((n_tp - 1,) + block, lambda k, info: (0,) * 5),
-            ),
+            grid=(1,),
+            in_specs=[anywhere] * (len(parts) + len(weights)),
+            out_specs=(anywhere, anywhere),
             scratch_shapes=[
-                pltpu.VMEM((PLANE * rows, depth), jnp.bfloat16),
-                pltpu.VMEM((levels, PLANE * rows, columns), jnp.float32),
+                pltpu.VMEM((PLANE * rows, width), jnp.bfloat16),
+                pltpu.VMEM((levels, width, columns), jnp.bfloat16),
+                pltpu.VMEM((levels, PLANE, rows, columns), jnp.bfloat16),
+                pltpu.SemaphoreType.DMA((PLANE * PLANE,)),
+                pltpu.SemaphoreType.DMA((levels,)),
+                pltpu.SemaphoreType.DMA((levels,)),
             ],
         ),
         out_shape=(
@@ -315,12 +338,8 @@
             jax.ShapeDtypeStruct((n_tp - 1,) + block, jnp.bfloat16),
         ),
         compiler_params=pltpu.CompilerParams(vmem_limit_bytes=VMEM),
-        cost_estimate=pl.CostEstimate(
-            flops=2 * PLANE * rows * width * columns * levels,
-            bytes_accessed=16 * 1024 * 1024,
-            transcendentals=0,
-        ),
-    )(info, *parts, *[w for w, _ in weights])
+        cost_estimate=CHEAP,
+    )(info, *[p for p, _ in parts], *[w for w, _ in weights])
 
 
 def assemble_kernel(info, *refs):
@@ -349,6 +368,7 @@
         ),
         out_shape=jax.ShapeDtypeStruct((rows, share * PLANE * columns), jnp.bfloat16),
         compiler_params=pltpu.CompilerParams(vmem_limit_bytes=VMEM),
+        cost_estimate=CHEAP,
     )(info, *pieces)
 
 
@@ -391,88 +411,103 @@
     rim = (last_rows[:, 0].astype(jnp.float32) * last_rows[:, 2].astype(jnp.float32)).astype(
         jnp.bfloat16
     )
+    attn_rows = attn_weight.reshape(PLANE, chunk, -1)
+    attn_weight = jnp.concatenate(
+        [lax.dynamic_index_in_dim(attn_rows, me ^ s, 0, False) for s in range(PLANE)], 0
+    )
+    weights = after(jnp.stack([out_weight, attn_weight]), rim)
+    attn_in = after(attn_in, weights)
     rim = lax.ppermute(rim, "ctx", [(i, i + 1) for i in range(n_ctx - 1)])
 
     def piece(index):
         block = lax.dynamic_slice(attn_in, (0, 0, index * chunk), (rows, 3, chunk))
         return block.transpose(1, 0, 2)
 
-    sent = [piece(me ^ s) for s in range(PLANE)]
+    sent = list(lax.optimization_barrier([piece(me ^ s) for s in range(PLANE)]))
     pieces = [sent[0]] + [swap(sent[s], s) for s in range(1, PLANE)]
-    attn_rows = attn_weight.reshape(PLANE, chunk, -1)
-    attn_weight = jnp.concatenate(
-        [lax.dynamic_index_in_dim(attn_rows, me ^ s, 0, False) for s in range(PLANE)], 0
-    )
-    weights = jnp.stack([out_weight, attn_weight])
     both_up = climb(weights, 1)
     both_down = climb(after(weights, rim), -1)
     product = (hyena_in[:, 0].astype(jnp.float32) * hyena_in[:, 2].astype(jnp.float32)).astype(
         jnp.bfloat16
     )
-    product, gate, *pieces = lax.optimization_barrier((product, hyena_in[:, 1], *pieces))
-
-    queries = jnp.stack([p[0] for p in pieces])
+    hyena_act = fir(rim, product, hyena_in[:, 1], filters)
+    hyena_act, *pieces = lax.optimization_barrier((hyena_act, *pieces))
+
     pairs = jnp.stack([p[1:] for p in pieces])
+    queries = jnp.stack([p[0] for p in lax.optimization_barrier([pairs] + pieces)[1:]])
     lower_pairs = move(pairs, 1, 0, levels - 3)
     upper_queries = climb(queries, -1)
+    hyena_one = swap(after(hyena_act, queries), 1)
     own = attend("causal", True, flags(me, 1), queries, pairs)
     top = levels - 2
     both_up = after(both_up, own[0])
     both_top = move(both_up, 1, top, top)
-    hyena_act = fir(after(rim, both_up), product, gate, filters)
-    upper_queries = after(upper_queries, hyena_act)
-    hyena_one, hyena_two = (swap(after(hyena_act, upper_queries), s) for s in (1, 2))
+    hyena_rest, attn_rest = lax.optimization_barrier((both_up[0], both_up[1]))
+    upper_queries, both_down, hyena_one = lax.optimization_barrier(
+        (after(upper_queries, hyena_rest), both_down, hyena_one)
+    )
+    hyena_rest = move(after(hyena_rest, upper_queries), 1, 1, top - 1)
+    hyena_down2 = climb(both_down[0], -1, 2)
+    hyena_pair = jnp.stack([hyena_act, hyena_one])
+    hyena_other = swap(hyena_pair, 2)
     carry = attend("full", False, flags(me, 1), upper_queries, pairs)
-    both_down = after(both_down, carry[0])
-    hyena_down2 = climb(both_down[0], -1, 2)
-    lower_pairs = after(lower_pairs, carry[0])
-    hyena_rest = move(after(both_up, lower_pairs)[0], 1, 1, top - 1)
-    served, served_level = attend(
+    lower_pairs, attn_down2 = lax.optimization_barrier((after(lower_pairs, carry[0]), both_down[1]))
+    attn_down2 = climb(attn_down2, -1, 2)
+    served = attend(
         "anti", True, flags(me, level > 0), upper_queries, lower_pairs, carry, jnp.bfloat16
     )
-    hyena_one, hyena_two, both_top = lax.optimization_barrier(
-        (hyena_one, hyena_two, after(both_top, served))
-    )
-    partial_up = climb(after(served, both_top), 1)
-    level_up = climb(after(served_level, both_top), 1)
-    half = rows // 2
-    hyena_three = swap(hyena_one[:half], 2), swap(after(hyena_two, level_up)[half:], 1)
-    hyena_down2 = after(hyena_down2, level_up)
-    attn_down2 = climb(after(both_down, hyena_down2)[1], -1, 2)
-    hyena_three = jnp.concatenate(lax.optimization_barrier(hyena_three), 0)
-    hyena_parts = [hyena_act, hyena_one, hyena_two, hyena_three]
-    hyena_up2 = both_top[0] + after(hyena_rest, hyena_three)
+    served, both_top, hyena_down2 = lax.optimization_barrier((served, both_top, hyena_down2))
+    partial_up = climb(served, 1)
+    attn_rest = move(after(attn_rest, served), 1, 1, top - 1)
+    hyena_up2 = both_top[0] + after(hyena_rest, served)
     hyena_ups, hyena_downs = [hyena_up2], [hyena_down2]
     attn_ups, attn_downs = [], [attn_down2]
     for step in range(3, levels):
         hyena_ups.append(climb(hyena_ups[-1], 1, step))
-    partial_up = after(partial_up, hyena_up2)
-    attn_rest = move(after(both_up, partial_up)[1], 1, 1, top - 1)
-    attended = across_plane(merge(flags(level > 0), *own, partial_up, level_up))
-    for step in range(3, levels):
-        hyena_downs.append(climb(after(hyena_downs[-1], attn_downs[0], partial_up), -1, step))
-    attn_ups.append(both_top[1] + attn_rest)
+        hyena_downs.append(climb(after(hyena_downs[-1], attn_down2), -1, step))
+    attended = merge(flags(level > 0), *own, after(partial_up, hyena_up2, hyena_other))
+    attn_ups.append(both_top[1] + after(attn_rest, attended, hyena_ups[-1], hyena_downs[-1]))
     for step in range(3, levels):
         attn_ups.append(climb(attn_ups[-1], 1, step))
         attn_downs.append(climb(after(attn_downs[-1], hyena_downs[-1]), -1, step))
+    hyena_parts = [(hyena_pair, 0), (hyena_pair, 1), (hyena_other, 0), (hyena_other, 1)]
     hyena_weights = hyena_ups[::-1] + [(both_up, 0), (weights, 0), (both_down, 0)] + hyena_downs
+
+    def add_up(mine, others):
+        gots = [
+            lax.ppermute(others[shift - 1], "tp", [(i, (i + shift) % n_tp) for i in range(n_tp)])
+            for shift in range(1, n_tp)
+        ]
+        pieces = []
+        for s in range(PLANE):
+            total = mine[s].astype(jnp.float32)
+            for got in gots:
+                total = total + got[s].astype(jnp.float32)
+            pieces.append(total.astype(jnp.bfloat16))
+        return pieces
+
+    def exchange(pieces):
+        return [pieces[0]] + [swap(pieces[s], s) for s in range(1, PLANE)]
+
+    where = flags(level, group)
+    attn_one, attn_two = swap(attended, 1), swap(attended, 2)
+    hyena_terms = project(levels, n_tp, where, hyena_parts, hyena_weights)
+    attn_one, attn_two, *hyena_terms = lax.optimization_barrier(
+        (after(attn_one, attn_ups[0]), attn_two, *hyena_terms)
+    )
+    half = PLANE // 2
+    attn_three = [swap(attn_one[:half], 2), swap(attn_two[half:], 1)]
+    hyena_pieces = add_up(*hyena_terms)
+    attn_three, attn_ups[-1], attn_downs[-1], *hyena_pieces = lax.optimization_barrier(
+        (jnp.concatenate(attn_three, 0), attn_ups[-1], attn_downs[-1], *hyena_pieces)
+    )
+    hyena_pieces = exchange(hyena_pieces)
     attn_weights = attn_ups[::-1] + [(both_up, 1), (weights, 1), (both_down, 1)] + attn_downs
-
-    def finish(parts, weights):
-        mine, others = project(levels, n_tp, flags(level, group), parts, weights)
-        total = mine.astype(jnp.float32)
-        for shift in range(1, n_tp):
-            got = lax.ppermute(
-                others[shift - 1], "tp", [(i, (i + shift) % n_tp) for i in range(n_tp)]
-            )
-            total = total + got.astype(jnp.float32)
-        total = total.astype(jnp.bfloat16)
-        return assemble(flags(me), [total[0]] + [swap(total[s], s) for s in range(1, PLANE)])
-
-    return (
-        finish(hyena_parts, hyena_weights),
-        finish(attended, attn_weights),
-    )
+    attn_parts = [attended, attn_one, attn_two, attn_three]
+    attn_terms = project(levels, n_tp, where, attn_parts, attn_weights)
+    hyena_pieces = [after(p, *attn_terms) for p in hyena_pieces]
+    attn_pieces = exchange(add_up(*attn_terms))
+    return assemble(flags(me), hyena_pieces), assemble(flags(me), attn_pieces)
 
 
 def solution(mesh):

time: 278 us -> 259 us (0.932)
  waiting for transfers between devices: 110 us -> 96 us
  other arithmetic: 8.65 us -> 16.3 us
  local copies, waits for them, and re-layouts: 25.7 us -> 19 us
  Pallas kernels: 69 us -> 63.7 us
  starting transfers between devices: 60.9 us -> 57.9 us
    ppermute x15 -> x14, waiting for transfers between devices: 59.4 us -> 41.4 us  [move(): lax.ppermute(block, 'ctx', [(i, i + direction * PLANE) for i in sources])]
    pallas_call x2, Pallas kernels: 24.9 us -> 19.5 us  [project(): pl.pallas_call(functools.partial(project_kernel, levels, n_tp, [i for _,...]
    ppermute x17 -> x15, starting transfers between devices: 19.4 us -> 14.5 us  [swap(): return lax.ppermute(block, 'ctx', [(i, i ^ relative) for i in range(n_ctx)])]
    slice x8 -> x9, local copies, waits for them, and re-layouts: 6.26 us -> 1.98 us  [the longest x7 1.91 us: per_device(): p[0]]
    ppermute x17 -> x15, waiting for transfers between devices: 50.9 us -> 54.6 us  [swap(): return lax.ppermute(block, 'ctx', [(i, i ^ relative) for i in range(n_ctx)])]
    add x2, other arithmetic: 0.21 us -> 3.38 us  [the longest x1 1.73 us: per_device(): both_top[1] + after(attn_rest, attended, hyena_ups[-1], hyena_downs[-1])]
    squeeze x6 -> x2, local copies, waits for them, and re-layouts: 6.84 us -> 4.03 us  [the longest x1 2.99 us: per_device(): hyena_rest, attn_rest = lax.optimization_barrier((both_up[0], both_up[1]))]
    ppermute x15 -> x14, starting transfers between devices: 35.8 us -> 38.5 us  [move(): lax.ppermute(block, 'ctx', [(i, i + direction * PLANE) for i in sources])]
  transfers between devices with their start and end apart: 35 -> 32, of which waited for: 13 -> 16; matrix products, arithmetic and copies ran while one was open for 10% -> 10% of each run, Pallas kernels for 24% -> 20%
where the time goes in v3:
time: 259 us; the launch traced here: 254 us
  waiting for transfers between devices  96 us (37%)
  Pallas kernels  63.7 us (25%)
  starting transfers between devices  57.9 us (22%)
  local copies, waits for them, and re-layouts  19 us (7%)
  other arithmetic  16.3 us (6%)
    ppermute x15, waiting for transfers between devices, swap(): return lax.ppermute(block, 'ctx', [(i, i ^ relative) for i in range(n_ctx)])  54.6 us
    ppermute x14, waiting for transfers between devices, move(): lax.ppermute(block, 'ctx', [(i, i + direction * PLANE) for i in sources])  41.4 us
    ppermute x14, starting transfers between devices, move(): lax.ppermute(block, 'ctx', [(i, i + direction * PLANE) for i in sources])  38.5 us
    pallas_call x3, Pallas kernels, attend(): pl.pallas_call(functools.partial(attend_kernel, kind, not carry, last), g...  28.2 us
    pallas_call x2, Pallas kernels, project(): pl.pallas_call(functools.partial(project_kernel, levels, n_tp, [i for _,...  19.5 us
    ppermute x15, starting transfers between devices, swap(): return lax.ppermute(block, 'ctx', [(i, i ^ relative) for i in range(n_ctx)])  14.5 us
    unnamed x58, local copies, waits for them, and re-layouts  7.7 us
    pallas_call x1, Pallas kernels, fir(): pl.pallas_call(fir_kernel, grid=(width // tile,), in_specs=[column(taps),...  7.21 us
  transfers between devices with their start and end apart: 32, of which 16 were waited for; matrix products, arithmetic and copies ran while one was open for 10% of the time, Pallas kernels for 20%

profile of v3, /device:TPU:0, one launch (start us, length us, event | category | flops | bytes accessed | tf_op | source)
XLA Modules:
  0.0 253.9 jit_solution(17017403192462351780)
XLA Ops:
  2.9 4.9 %collective-permute-start = (bf16[128,2048]{1,0:T(8,128)(2,1)}, bf16[128,2048]{1,0:T(8,128)(2,1)S(1)}, u32[]{:S(2)}, u32[]{:S(2)}) collective-permute-start(bf16[128,2048]{1,0:T(8,128)(2,1)} %fusion.1), channel_id=1, source_target_pairs={{0,2},{2,4},{4,6},{6,8},{8,10},{10,12},{12,14},{14,16},{16,18},{18... | collective-permute-start | bytes 1572872 | tf_op jit(solution)/shard_map/ppermute | solution.py:420
  9.2 4.8 %collective-permute-start.5 = (bf16[2,2048,256]{2,1,0:T(8,128)(2,1)S(1)}, bf16[2,2048,256]{2,1,0:T(8,128)(2,1)}, u32[]{:S(2)}, u32[]{:S(2)}) collective-permute-start(bf16[2,2048,256]{2,1,0:T(8,128)(2,1)S(1)} %pad_maximum_fusion.refs_7_), channel_id=1, source_target_pairs={{0,8},{2,10},{4,12},{6,14},{8,16},{10,18},{12,20},{14,22},{16,24},... | collective-permute-start | bytes 6291464 | tf_op jit(solution)/shard_map/ppermute | solution.py:397
  14.0 3.5 %dynamic-slice_bitcast_fusion = (bf16[3,256,512]{2,1,0:T(8,128)(2,1)}, bf16[3,256,512]{2,1,0:T(8,128)(2,1)}, bf16[3,256,512]{2,1,0:T(8,128)(2,1)}, bf16[3,256,512]{2,1,0:T(8,128)(2,1)S(1)}) fusion(bf16[256,3,2048]{2,0,1:T(8,128)(2,1)} %param.11, s32[]{:T(128)S(6)} %select_n.45, s32[]{:T(128)S(6)} %select_n.44, s32[]{:T(128)S(6)} %select_n.43, s32[]{:T(128)S(6)} %select_n.42), kind=kLoop, calls=%fused_computation.16 | loop fusion | bytes 6291472 | tf_op jit(solution)/shard_map/transpose | solution.py:424
  24.7 7.2 %shard_map.104 = bf16[256,2048]{1,0:T(8,128)(2,1)} custom-call(bf16[128,2048]{1,0:T(8,128)(2,1)} %copy-done.21, bf16[256,2048]{1,0:T(8,128)(2,1)} %fusion.product, bf16[256,2048]{1,0:T(8,128)(2,1)} %slice_bitcast_fusion.4.gate, f32[128,2048]{1,0:T(8,128)} %filters.1, bf16[256,256]{1,0:T(8,128)(2,1)} %constant.62.clone.f_hi, ...), custom_call_target="tpu_custom_call" | custom-call | flops 1 | bytes 1 | tf_op jit(solution)/shard_map/pallas_call | solution.py:82
  31.9 7.1 %collective-permute-done.1 = bf16[3,256,512]{2,1,0:T(8,128)(2,1)S(1)} collective-permute-done((bf16[3,256,512]{2,1,0:T(8,128)(2,1)}, bf16[3,256,512]{2,1,0:T(8,128)(2,1)S(1)}, u32[]{:S(2)}, u32[]{:S(2)}) %collective-permute-start.1) | collective-permute-done | bytes 786464 | tf_op jit(solution)/shard_map/ppermute | solution.py:393
  39.0 15.5 %collective-permute-done.2 = bf16[3,256,512]{2,1,0:T(8,128)(2,1)S(1)} collective-permute-done((bf16[3,256,512]{2,1,0:T(8,128)(2,1)}, bf16[3,256,512]{2,1,0:T(8,128)(2,1)S(1)}, u32[]{:S(2)}, u32[]{:S(2)}) %collective-permute-start.2) | collective-permute-done | bytes 786464 | tf_op jit(solution)/shard_map/ppermute | solution.py:393
  62.5 5.9 %collective-permute-start.8 = (bf16[4,2,256,512]{3,2,1,0:T(8,128)(2,1)S(1)}, bf16[4,2,256,512]{3,2,1,0:T(8,128)(2,1)}, u32[]{:S(2)}, u32[]{:S(2)}) collective-permute-start(bf16[4,2,256,512]{3,2,1,0:T(8,128)(2,1)S(1)} %pad_maximum_fusion.1.k_ref.v_ref), channel_id=1, source_target_pairs={{0,8},{2,10},{4,12},{6,14},{8,16},{10,18},{12,20},{14,22},{1,9},{3... | collective-permute-start | bytes 6291464 | tf_op jit(solution)/shard_map/ppermute | solution.py:397
  69.0 10.0 %shard_map.105 = (f32[4,256,512]{2,1,0:T(8,128)}, f32[4,4,8,256]{3,2,1,0:T(8,128)}) custom-call(s32[2]{0:T(128)} %pad_add_fusion.info, bf16[4,256,512]{2,1,0:T(8,128)(2,1)} %pad_maximum_fusion.3.q_ref, bf16[4,2,256,512]{3,2,1,0:T(8,128)(2,1)} %copy-done, bf16[4,2,256,512]{3,2,1,0:T(8,128)(2,1)} %copy-done), custom_call_target="tpu_custom_call" | custom-call | flops 1 | bytes 1 | tf_op jit(solution)/shard_map/pallas_call | solution.py:208
  81.1 3.0 %slice_bitcast_fusion.2 = (bf16[2048,256]{1,0:T(8,128)(2,1)}, bf16[2048,256]{1,0:T(8,128)(2,1)}) fusion(bf16[2,2048,256]{2,1,0:T(8,128)(2,1)} %collective-permute-done.5.refs_6_), kind=kLoop, calls=%fused_computation.12 | loop fusion | bytes 4194304 | tf_op jit(solution)/shard_map/squeeze | solution.py:445
  84.1 8.7 %collective-permute-done.4.q_ref = bf16[4,256,512]{2,1,0:T(8,128)(2,1)} collective-permute-done((bf16[4,256,512]{2,1,0:T(8,128)(2,1)}, bf16[4,256,512]{2,1,0:T(8,128)(2,1)}, u32[]{:S(2)}, u32[]{:S(2)}) %collective-permute-start.4) | collective-permute-done | bytes 1048608 | tf_op jit(solution)/shard_map/ppermute | solution.py:397
  100.9 11.2 %shard_map.106 = (f32[4,256,512]{2,1,0:T(8,128)}, f32[4,256,512]{2,1,0:T(8,128)}) custom-call(s32[2]{0:T(128)} %pad_add_fusion.info, bf16[4,256,512]{2,1,0:T(8,128)(2,1)} %collective-permute-done.4.q_ref, bf16[4,2,256,512]{3,2,1,0:T(8,128)(2,1)} %copy-done, bf16[4,2,256,512]{3,2,1,0:T(8,128)(2,1)} %copy-done), custom_call_target="tpu_custom_call" | custom-call | flops 1 | bytes 1 | tf_op jit(solution)/shard_map/pallas_call | solution.py:208
  114.0 7.0 %shard_map.107 = bf16[4,272,512]{2,1,0:T(8,128)(2,1)} custom-call(s32[2]{0:T(128)} %pad_add_fusion.1.info, bf16[4,256,512]{2,1,0:T(8,128)(2,1)} %collective-permute-done.4.q_ref, bf16[4,2,256,512]{3,2,1,0:T(8,128)(2,1)} %collective-permute-done.8.k_ref.v_ref, bf16[4,2,256,512]{3,2,1,0:T(8,128)(2,1)} %collective-permute-done.8.k_ref.v_ref, ...), custom_call_target="tpu_custom_call" | custom-call | flops 1 | bytes 1 | tf_op jit(solution)/shard_map/pallas_call | solution.py:208
  121.9 12.2 %collective-permute-start.11 = (bf16[4,272,512]{2,1,0:T(8,128)(2,1)}, bf16[4,272,512]{2,1,0:T(8,128)(2,1)S(1)}, u32[]{:S(2)}, u32[]{:S(2)}) collective-permute-start(bf16[4,272,512]{2,1,0:T(8,128)(2,1)} %shard_map.107), channel_id=1, source_target_pairs={{0,8},{2,10},{4,12},{6,14},{8,16},{10,18},{12,20},{14,22},{16,24},... | collective-permute-start | bytes 3342344 | tf_op jit(solution)/shard_map/ppermute | solution.py:397
  137.4 4.4 %collective-permute-done.17 = bf16[2048,256]{1,0:T(8,128)(2,1)} collective-permute-done((bf16[2048,256]{1,0:T(8,128)(2,1)}, bf16[2048,256]{1,0:T(8,128)(2,1)}, u32[]{:S(2)}, u32[]{:S(2)}) %collective-permute-start.17) | collective-permute-done | bytes 1048608 | tf_op jit(solution)/shard_map/ppermute | solution.py:397
  144.8 9.6 %collective-permute-done.11.two_ref = bf16[4,272,512]{2,1,0:T(8,128)(2,1)S(1)} collective-permute-done((bf16[4,272,512]{2,1,0:T(8,128)(2,1)}, bf16[4,272,512]{2,1,0:T(8,128)(2,1)S(1)}, u32[]{:S(2)}, u32[]{:S(2)}) %collective-permute-start.11) | collective-permute-done | bytes 1114144 | tf_op jit(solution)/shard_map/ppermute | solution.py:397
  155.4 4.2 %shard_map.108.refs_0_ = bf16[4,256,512]{2,1,0:T(8,128)(2,1)} custom-call(s32[1]{0:T(128)} %bitcast.1.info, f32[4,256,512]{2,1,0:T(8,128)} %get-tuple-element.77.one_ref, f32[4,4,8,256]{3,2,1,0:T(8,128)} %get-tuple-element.78.level_one, bf16[4,272,512]{2,1,0:T(8,128)(2,1)} %copy-done.11), custom_call_target="tpu_custom_call" | custom-call | flops 1 | bytes 1 | tf_op jit(solution)/shard_map/pallas_call | solution.py:239
  162.3 4.4 %collective-permute-done.18 = bf16[2048,256]{1,0:T(8,128)(2,1)} collective-permute-done((bf16[2048,256]{1,0:T(8,128)(2,1)}, bf16[2048,256]{1,0:T(8,128)(2,1)}, u32[]{:S(2)}, u32[]{:S(2)}) %collective-permute-start.18) | collective-permute-done | bytes 1048608 | tf_op jit(solution)/shard_map/ppermute | solution.py:397
  166.7 9.8 %shard_map.109 = (bf16[4,2,256,256]{3,2,1,0:T(8,128)(2,1)}, bf16[1,4,2,256,256]{4,3,2,1,0:T(8,128)(2,1)}) custom-call(s32[2]{0:T(128)} %pad_add_fusion.2.info, bf16[2,256,2048]{2,1,0:T(8,128)(2,1)} %copy-done.3, bf16[2,256,2048]{2,1,0:T(8,128)(2,1)} %copy-done.3, bf16[2,256,2048]{2,1,0:T(8,128)(2,1)} %collective-permute-done.13.refs_2_.refs_3_, ...), custom_call_target="tpu_custom_call" | custom-call | flops 1 | bytes 1 | tf_op jit(solution)/shard_map/pallas_call | solution.py:318
  185.6 12.7 %collective-permute-done.21 = bf16[2,256,512]{2,1,0:T(8,128)(2,1)S(1)} collective-permute-done((bf16[2,256,512]{2,1,0:T(8,128)(2,1)S(1)}, bf16[2,256,512]{2,1,0:T(8,128)(2,1)S(1)}, u32[]{:S(2)}, u32[]{:S(2)}) %collective-permute-start.21) | collective-permute-done | bytes 524320 | tf_op jit(solution)/shard_map/ppermute | solution.py:393
  200.6 13.4 %collective-permute-done.23 = bf16[2048,256]{1,0:T(8,128)(2,1)S(1)} collective-permute-done((bf16[2048,256]{1,0:T(8,128)(2,1)}, bf16[2048,256]{1,0:T(8,128)(2,1)S(1)}, u32[]{:S(2)}, u32[]{:S(2)}) %collective-permute-start.23) | collective-permute-done | bytes 1048608 | tf_op jit(solution)/shard_map/ppermute | solution.py:397
  215.3 9.8 %shard_map.110 = (bf16[4,2,256,256]{3,2,1,0:T(8,128)(2,1)}, bf16[1,4,2,256,256]{4,3,2,1,0:T(8,128)(2,1)}) custom-call(s32[2]{0:T(128)} %pad_add_fusion.2.info, bf16[4,256,512]{2,1,0:T(8,128)(2,1)} %shard_map.108.refs_0_, bf16[4,256,512]{2,1,0:T(8,128)(2,1)} %copy-done.9, bf16[4,256,512]{2,1,0:T(8,128)(2,1)} %copy-done.10, ...), custom_call_target="tpu_custom_call" | custom-call | flops 1 | bytes 1 | tf_op jit(solution)/shard_map/pallas_call | solution.py:318
  225.8 2.8 %collective-permute-start.27 = (bf16[2,256,256]{2,1,0:T(8,128)(2,1)S(1)}, bf16[2,256,256]{2,1,0:T(8,128)(2,1)S(1)}, u32[]{:S(2)}, u32[]{:S(2)}) collective-permute-start(bf16[2,256,256]{2,1,0:T(8,128)(2,1)S(1)} %get-tuple-element.122), channel_id=1, source_target_pairs={{0,6},{2,4},{4,2},{6,0},{8,14},{10,12},{12,10},{14,8},{16,22},{18,... | collective-permute-start | bytes 786440 | tf_op jit(solution)/shard_map/ppermute | solution.py:393
  234.4 6.0 %collective-permute-done.26.refs_2_ = bf16[2,256,256]{2,1,0:T(8,128)(2,1)S(1)} collective-permute-done((bf16[2,256,256]{2,1,0:T(8,128)(2,1)S(1)}, bf16[2,256,256]{2,1,0:T(8,128)(2,1)S(1)}, u32[]{:S(2)}, u32[]{:S(2)}) %collective-permute-start.26) | collective-permute-done | bytes 262176 | tf_op jit(solution)/shard_map/ppermute | solution.py:393
  245.6 5.2 %collective-permute-done.30.refs_2_ = bf16[2,256,256]{2,1,0:T(8,128)(2,1)S(1)} collective-permute-done((bf16[2,256,256]{2,1,0:T(8,128)(2,1)S(1)}, bf16[2,256,256]{2,1,0:T(8,128)(2,1)S(1)}, u32[]{:S(2)}, u32[]{:S(2)}) %collective-permute-start.30) | collective-permute-done | bytes 262176 | tf_op jit(solution)/shard_map/ppermute | solution.py:393
  (138 shorter events, 69.7 us)
Async XLA Ops:
  2.9 19.5 %collective-permute-start = (bf16[128,2048]{1,0:T(8,128)(2,1)}, bf16[128,2048]{1,0:T(8,128)(2,1)S(1)}, u32[]{:S(2)}, u32[]{:S(2)}) collective-permute-start(bf16[128,2048]{1,0:T(8,128)(2,1)} %fusion.1), channel_id=1, source_target_pairs={{0,2},{2,4},{4,6},{6,8},{8,10},{10,12},{12,14},{14,16},{16,18},{18... | collective-permute-start | bytes 1572872 | tf_op jit(solution)/shard_map/ppermute | solution.py:420
  9.2 69.8 %collective-permute-start.5 = (bf16[2,2048,256]{2,1,0:T(8,128)(2,1)S(1)}, bf16[2,2048,256]{2,1,0:T(8,128)(2,1)}, u32[]{:S(2)}, u32[]{:S(2)}) collective-permute-start(bf16[2,2048,256]{2,1,0:T(8,128)(2,1)S(1)} %pad_maximum_fusion.refs_7_), channel_id=1, source_target_pairs={{0,8},{2,10},{4,12},{6,14},{8,16},{10,18},{12,20},{14,22},{16,24},... | collective-permute-start | bytes 6291464 | tf_op jit(solution)/shard_map/ppermute | solution.py:397
  17.5 21.5 %collective-permute-start.1 = (bf16[3,256,512]{2,1,0:T(8,128)(2,1)}, bf16[3,256,512]{2,1,0:T(8,128)(2,1)S(1)}, u32[]{:S(2)}, u32[]{:S(2)}) collective-permute-start(bf16[3,256,512]{2,1,0:T(8,128)(2,1)} %get-tuple-element.66), channel_id=1, source_target_pairs={{0,2},{2,0},{4,6},{6,4},{8,10},{10,8},{12,14},{14,12},{16,18},{18,... | collective-permute-start | bytes 2359304 | tf_op jit(solution)/shard_map/ppermute | solution.py:393
  19.0 35.5 %collective-permute-start.2 = (bf16[3,256,512]{2,1,0:T(8,128)(2,1)}, bf16[3,256,512]{2,1,0:T(8,128)(2,1)S(1)}, u32[]{:S(2)}, u32[]{:S(2)}) collective-permute-start(bf16[3,256,512]{2,1,0:T(8,128)(2,1)} %get-tuple-element.67), channel_id=1, source_target_pairs={{0,4},{2,6},{4,0},{6,2},{8,12},{10,14},{12,8},{14,10},{16,20},{18,... | collective-permute-start | bytes 2359304 | tf_op jit(solution)/shard_map/ppermute | solution.py:393
  20.5 34.0 %collective-permute-start.3 = (bf16[3,256,512]{2,1,0:T(8,128)(2,1)}, bf16[3,256,512]{2,1,0:T(8,128)(2,1)S(1)}, u32[]{:S(2)}, u32[]{:S(2)}) collective-permute-start(bf16[3,256,512]{2,1,0:T(8,128)(2,1)} %get-tuple-element.68), channel_id=1, source_target_pairs={{0,6},{2,4},{4,2},{6,0},{8,14},{10,12},{12,10},{14,8},{16,22},{18,... | collective-permute-start | bytes 2359304 | tf_op jit(solution)/shard_map/ppermute | solution.py:393
  22.3 70.4 %collective-permute-start.6 = (bf16[2,2048,256]{2,1,0:T(8,128)(2,1)S(1)}, bf16[2,2048,256]{2,1,0:T(8,128)(2,1)S(1)}, u32[]{:S(2)}, u32[]{:S(2)}) collective-permute-start(bf16[2,2048,256]{2,1,0:T(8,128)(2,1)S(1)} %pad_maximum_fusion.refs_7_), channel_id=1, source_target_pairs={{8,0},{10,2},{12,4},{14,6},{16,8},{18,10},{20,12},{22,14},{24,16},... | collective-permute-start | bytes 6291464 | tf_op jit(solution)/shard_map/ppermute | solution.py:397
  59.7 33.1 %collective-permute-start.4 = (bf16[4,256,512]{2,1,0:T(8,128)(2,1)}, bf16[4,256,512]{2,1,0:T(8,128)(2,1)}, u32[]{:S(2)}, u32[]{:S(2)}) collective-permute-start(bf16[4,256,512]{2,1,0:T(8,128)(2,1)} %pad_maximum_fusion.3.q_ref), channel_id=1, source_target_pairs={{8,0},{10,2},{12,4},{14,6},{16,8},{18,10},{20,12},{22,14},{24,16},... | collective-permute-start | bytes 3145736 | tf_op jit(solution)/shard_map/ppermute | solution.py:397
  61.0 31.8 %collective-permute-start.7 = (bf16[256,2048]{1,0:T(8,128)(2,1)S(1)}, bf16[256,2048]{1,0:T(8,128)(2,1)}, u32[]{:S(2)}, u32[]{:S(2)}) collective-permute-start(bf16[256,2048]{1,0:T(8,128)(2,1)S(1)} %copy-done.6), channel_id=1, source_target_pairs={{0,2},{2,0},{4,6},{6,4},{8,10},{10,8},{12,14},{14,12},{16,18},{18,... | collective-permute-start | bytes 3145736 | tf_op jit(solution)/shard_map/ppermute | solution.py:393
  62.5 49.6 %collective-permute-start.8 = (bf16[4,2,256,512]{3,2,1,0:T(8,128)(2,1)S(1)}, bf16[4,2,256,512]{3,2,1,0:T(8,128)(2,1)}, u32[]{:S(2)}, u32[]{:S(2)}) collective-permute-start(bf16[4,2,256,512]{3,2,1,0:T(8,128)(2,1)S(1)} %pad_maximum_fusion.1.k_ref.v_ref), channel_id=1, source_target_pairs={{0,8},{2,10},{4,12},{6,14},{8,16},{10,18},{12,20},{14,22},{1,9},{3... | collective-permute-start | bytes 6291464 | tf_op jit(solution)/shard_map/ppermute | solution.py:397
  79.0 42.8 %collective-permute-start.9 = (bf16[2,2048,256]{2,1,0:T(8,128)(2,1)}, bf16[2,2048,256]{2,1,0:T(8,128)(2,1)}, u32[]{:S(2)}, u32[]{:S(2)}) collective-permute-start(bf16[2,2048,256]{2,1,0:T(8,128)(2,1)} %collective-permute-done.5.refs_6_), channel_id=1, source_target_pairs={{16,24},{18,26},{20,28},{22,30},{17,25},{19,27},{21,29},{23,31}} | collective-permute-start | bytes 6291464 | tf_op jit(solution)/shard_map/ppermute | solution.py:397
  94.8 27.0 %collective-permute-start.10 = (bf16[2048,256]{1,0:T(8,128)(2,1)}, bf16[2048,256]{1,0:T(8,128)(2,1)}, u32[]{:S(2)}, u32[]{:S(2)}) collective-permute-start(bf16[2048,256]{1,0:T(8,128)(2,1)} %get-tuple-element.136), channel_id=1, source_target_pairs={{8,0},{10,2},{12,4},{14,6},{16,8},{18,10},{20,12},{22,14},{9,1},{1... | collective-permute-start | bytes 3145736 | tf_op jit(solution)/shard_map/ppermute | solution.py:397
  96.1 38.0 %collective-permute-start.12 = (bf16[2048,256]{1,0:T(8,128)(2,1)}, bf16[2048,256]{1,0:T(8,128)(2,1)}, u32[]{:S(2)}, u32[]{:S(2)}) collective-permute-start(bf16[2048,256]{1,0:T(8,128)(2,1)} %get-tuple-element.93), channel_id=1, source_target_pairs={{8,16},{10,18},{12,20},{14,22},{9,17},{11,19},{13,21},{15,23}} | collective-permute-start | bytes 3145736 | tf_op jit(solution)/shard_map/ppermute | solution.py:397
  99.3 45.5 %collective-permute-start.13 = (bf16[2,256,2048]{2,1,0:T(8,128)(2,1)S(1)}, bf16[2,256,2048]{2,1,0:T(8,128)(2,1)}, u32[]{:S(2)}, u32[]{:S(2)}) collective-permute-start(bf16[2,256,2048]{2,1,0:T(8,128)(2,1)S(1)} %pad_maximum_fusion.2.refs_0_.refs_1_), channel_id=1, source_target_pairs={{0,4},{2,6},{4,0},{6,2},{8,12},{10,14},{12,8},{14,10},{16,20},{18,... | collective-permute-start | bytes 6291464 | tf_op jit(solution)/shard_map/ppermute | solution.py:393
  112.0 29.8 %collective-permute-start.17 = (bf16[2048,256]{1,0:T(8,128)(2,1)}, bf16[2048,256]{1,0:T(8,128)(2,1)}, u32[]{:S(2)}, u32[]{:S(2)}) collective-permute-start(bf16[2048,256]{1,0:T(8,128)(2,1)} %get-tuple-element.100), channel_id=1, source_target_pairs={{8,0},{10,2},{12,4},{14,6},{16,8},{18,10},{20,12},{22,14},{9,1},{1... | collective-permute-start | bytes 3145736 | tf_op jit(solution)/shard_map/ppermute | solution.py:397
  121.9 32.5 %collective-permute-start.11 = (bf16[4,272,512]{2,1,0:T(8,128)(2,1)}, bf16[4,272,512]{2,1,0:T(8,128)(2,1)S(1)}, u32[]{:S(2)}, u32[]{:S(2)}) collective-permute-start(bf16[4,272,512]{2,1,0:T(8,128)(2,1)} %shard_map.107), channel_id=1, source_target_pairs={{0,8},{2,10},{4,12},{6,14},{8,16},{10,18},{12,20},{14,22},{16,24},... | collective-permute-start | bytes 3342344 | tf_op jit(solution)/shard_map/ppermute | solution.py:397
  135.8 26.6 %collective-permute-start.16 = (bf16[2048,256]{1,0:T(8,128)(2,1)S(1)}, bf16[2048,256]{1,0:T(8,128)(2,1)}, u32[]{:S(2)}, u32[]{:S(2)}) collective-permute-start(bf16[2048,256]{1,0:T(8,128)(2,1)S(1)} %bitcast_add_fusion.1), channel_id=1, source_target_pairs={{16,24},{18,26},{20,28},{22,30},{17,25},{19,27},{21,29},{23,31}} | collective-permute-start | bytes 3145736 | tf_op jit(solution)/shard_map/ppermute | solution.py:397
  141.9 24.9 %collective-permute-start.18 = (bf16[2048,256]{1,0:T(8,128)(2,1)}, bf16[2048,256]{1,0:T(8,128)(2,1)}, u32[]{:S(2)}, u32[]{:S(2)}) collective-permute-start(bf16[2048,256]{1,0:T(8,128)(2,1)} %collective-permute-done.10), channel_id=1, source_target_pairs={{8,0},{10,2},{12,4},{14,6},{9,1},{11,3},{13,5},{15,7}} | collective-permute-start | bytes 3145736 | tf_op jit(solution)/shard_map/ppermute | solution.py:397
  143.1 33.4 %collective-permute-start.15 = (bf16[2048,256]{1,0:T(8,128)(2,1)}, bf16[2048,256]{1,0:T(8,128)(2,1)}, u32[]{:S(2)}, u32[]{:S(2)}) collective-permute-start(bf16[2048,256]{1,0:T(8,128)(2,1)} %get-tuple-element.98), channel_id=1, source_target_pairs={{8,16},{10,18},{12,20},{14,22},{9,17},{11,19},{13,21},{15,23}} | collective-permute-start | bytes 3145736 | tf_op jit(solution)/shard_map/ppermute | solution.py:397
  159.6 20.8 %collective-permute-start.14 = (bf16[4,256,512]{2,1,0:T(8,128)(2,1)}, bf16[4,256,512]{2,1,0:T(8,128)(2,1)S(1)}, u32[]{:S(2)}, u32[]{:S(2)}) collective-permute-start(bf16[4,256,512]{2,1,0:T(8,128)(2,1)} %shard_map.108.refs_0_), channel_id=1, source_target_pairs={{0,2},{2,0},{4,6},{6,4},{8,10},{10,8},{12,14},{14,12},{16,18},{18,... | collective-permute-start | bytes 3145736 | tf_op jit(solution)/shard_map/ppermute | solution.py:393
  161.2 20.6 %collective-permute-start.19 = (bf16[4,256,512]{2,1,0:T(8,128)(2,1)}, bf16[4,256,512]{2,1,0:T(8,128)(2,1)S(1)}, u32[]{:S(2)}, u32[]{:S(2)}) collective-permute-start(bf16[4,256,512]{2,1,0:T(8,128)(2,1)} %shard_map.108.refs_0_), channel_id=1, source_target_pairs={{0,4},{2,6},{4,0},{6,2},{8,12},{10,14},{12,8},{14,10},{16,20},{18,... | collective-permute-start | bytes 3145736 | tf_op jit(solution)/shard_map/ppermute | solution.py:393
  181.8 17.8 %collective-permute-start.24 = (bf16[4,2,256,256]{3,2,1,0:T(8,128)(2,1)S(1)}, bf16[4,2,256,256]{3,2,1,0:T(8,128)(2,1)S(1)}, u32[]{:S(2)}, u32[]{:S(2)}) collective-permute-start(bf16[4,2,256,256]{3,2,1,0:T(8,128)(2,1)S(1)} %bitcast.85), channel_id=1, source_target_pairs={{0,1},{1,0},{2,3},{3,2},{4,5},{5,4},{6,7},{7,6},{8,9},{9,8},{10,11... | collective-permute-start | bytes 3145736 | tf_op jit(solution)/shard_map/ppermute | solution.py:478
  181.8 32.1 %collective-permute-start.23 = (bf16[2048,256]{1,0:T(8,128)(2,1)}, bf16[2048,256]{1,0:T(8,128)(2,1)S(1)}, u32[]{:S(2)}, u32[]{:S(2)}) collective-permute-start(bf16[2048,256]{1,0:T(8,128)(2,1)} %collective-permute-done.17), channel_id=1, source_target_pairs={{8,0},{10,2},{12,4},{14,6},{9,1},{11,3},{13,5},{15,7}} | collective-permute-start | bytes 3145736 | tf_op jit(solution)/shard_map/ppermute | solution.py:397
  183.3 30.7 %collective-permute-start.22 = (bf16[2048,256]{1,0:T(8,128)(2,1)S(1)}, bf16[2048,256]{1,0:T(8,128)(2,1)S(1)}, u32[]{:S(2)}, u32[]{:S(2)}) collective-permute-start(bf16[2048,256]{1,0:T(8,128)(2,1)S(1)} %bitcast_add_fusion), channel_id=1, source_target_pairs={{16,24},{18,26},{20,28},{22,30},{17,25},{19,27},{21,29},{23,31}} | collective-permute-start | bytes 3145736 | tf_op jit(solution)/shard_map/ppermute | solution.py:397
  231.3 19.6 %collective-permute-start.30 = (bf16[2,256,256]{2,1,0:T(8,128)(2,1)S(1)}, bf16[2,256,256]{2,1,0:T(8,128)(2,1)S(1)}, u32[]{:S(2)}, u32[]{:S(2)}) collective-permute-start(bf16[2,256,256]{2,1,0:T(8,128)(2,1)S(1)} %get-tuple-element.129), channel_id=1, source_target_pairs={{0,4},{2,6},{4,0},{6,2},{8,12},{10,14},{12,8},{14,10},{16,20},{18,... | collective-permute-start | bytes 786440 | tf_op jit(solution)/shard_map/ppermute | solution.py:393
  (40 other events, 343.0 us)

commit v4 on v3

--- a/solution.py
+++ b/solution.py
@@ -17,6 +17,9 @@
 LEVEL_ROWS = 16
 VMEM = 56 * 1024 * 1024
 CHEAP = pl.CostEstimate(flops=1, bytes_accessed=1, transcendentals=0)
+MODEST = pl.CostEstimate(flops=2 * 10**9, bytes_accessed=1, transcendentals=0)
+LARGE = pl.CostEstimate(flops=10**10, bytes_accessed=1, transcendentals=0)
+ATTEND_COST = {"causal": LARGE, "full": CHEAP, "anti": LARGE}
 
 
 def split_bf16(array):
@@ -73,6 +76,7 @@
         out[span] = (gate[span].astype(jnp.float32) * filtered).astype(out.dtype)
 
 
+@jax.named_scope('fir')
 def fir(rim, product, gate, filters):
     taps, width = filters.shape
     rows = product.shape[0]
@@ -215,7 +219,7 @@
         ),
         out_shape=out_shape,
         compiler_params=pltpu.CompilerParams(vmem_limit_bytes=VMEM),
-        cost_estimate=CHEAP,
+        cost_estimate=ATTEND_COST[kind],
     )(info, queries, pairs, pairs, *carry)
 
 
@@ -232,6 +236,7 @@
         out[0, :, span] = (first + share * (second - first)).astype(out.dtype)
 
 
+@jax.named_scope('merge')
 def merge(info, one, level_one, two):
     plane, rows, width = one.shape
     block = pl.BlockSpec((1, rows, width), lambda i, info: (i, 0, 0))
@@ -250,7 +255,7 @@
         ),
         out_shape=jax.ShapeDtypeStruct(one.shape, jnp.bfloat16),
         compiler_params=pltpu.CompilerParams(vmem_limit_bytes=VMEM),
-        cost_estimate=CHEAP,
+        cost_estimate=MODEST,
     )(info, one, level_one, two)
 
 
@@ -279,10 +284,10 @@
             )
     for copy in loads:
         copy.start()
-    for position, (weight, index) in enumerate(zip(weights, weight_index)):
-        target = level + (position - (levels - 1))
-
-        @pl.when((target >= 0) & (target < levels))
+    for weight, (index, offset, first, last) in zip(weights, weight_index):
+        target = level + offset
+
+        @pl.when((level >= first) & (level <= last))
         def _(weight=weight, index=index, target=target):
             pltpu.make_async_copy(weight.at[index], w.at[target], sem_w.at[target]).start()
 
@@ -308,16 +313,17 @@
         store(t, lambda copy: copy.wait())
 
 
-def project(levels, n_tp, info, parts, weights):
+@jax.named_scope('project')
+def project(levels, n_tp, info, parts, weights, cost=CHEAP):
     parts = [p if isinstance(p, tuple) else (p, None) for p in parts]
-    weights = [w if isinstance(w, tuple) else (w[None], 0) for w in weights]
+    weights = [(w[0][None], 0, *w[2:]) if w[0].ndim == 2 else w for w in weights]
     width, columns = weights[0][0].shape[1:]
     rows = parts[0][0].shape[1]
     block = (PLANE, levels // n_tp, rows, columns)
     anywhere = pl.BlockSpec(memory_space=pl.ANY)
     return pl.pallas_call(
         functools.partial(
-            project_kernel, levels, n_tp, [i for _, i in parts], [i for _, i in weights]
+            project_kernel, levels, n_tp, [i for _, i in parts], [w[1:] for w in weights]
         ),
         grid_spec=pltpu.PrefetchScalarGridSpec(
             num_scalar_prefetch=1,
@@ -338,8 +344,8 @@
             jax.ShapeDtypeStruct((n_tp - 1,) + block, jnp.bfloat16),
         ),
         compiler_params=pltpu.CompilerParams(vmem_limit_bytes=VMEM),
-        cost_estimate=CHEAP,
-    )(info, *[p for p, _ in parts], *[w for w, _ in weights])
+        cost_estimate=cost,
+    )(info, *[p for p, _ in parts], *[w[0] for w in weights])
 
 
 def assemble_kernel(info, *refs):
@@ -351,6 +357,7 @@
             out[:, pl.ds(start, columns)] = piece[t]
 
 
+@jax.named_scope('assemble')
 def assemble(info, pieces):
     share, rows, columns = pieces[0].shape
     if columns % 128:
@@ -401,12 +408,6 @@
             return move(block, 1, step - 1, levels - 2)
         return move(block, -1, 1, levels - step)
 
-    def across_plane(block):
-        one, two = swap(block, 1), swap(block, 2)
-        half = block.shape[0] // 2
-        three = jnp.concatenate([swap(one[:half], 2), swap(two[half:], 1)], 0)
-        return [block, one, two, three]
-
     last_rows = hyena_in[rows - taps :]
     rim = (last_rows[:, 0].astype(jnp.float32) * last_rows[:, 2].astype(jnp.float32)).astype(
         jnp.bfloat16
@@ -457,21 +458,34 @@
         "anti", True, flags(me, level > 0), upper_queries, lower_pairs, carry, jnp.bfloat16
     )
     served, both_top, hyena_down2 = lax.optimization_barrier((served, both_top, hyena_down2))
+    hyena_rest, served = lax.optimization_barrier((hyena_rest, served))
     partial_up = climb(served, 1)
     attn_rest = move(after(attn_rest, served), 1, 1, top - 1)
-    hyena_up2 = both_top[0] + after(hyena_rest, served)
-    hyena_ups, hyena_downs = [hyena_up2], [hyena_down2]
+    hyena_ups = [both_top[0] + after(hyena_rest, served)]
+    hyena_downs = [hyena_down2]
     attn_ups, attn_downs = [], [attn_down2]
     for step in range(3, levels):
         hyena_ups.append(climb(hyena_ups[-1], 1, step))
         hyena_downs.append(climb(after(hyena_downs[-1], attn_down2), -1, step))
-    attended = merge(flags(level > 0), *own, after(partial_up, hyena_up2, hyena_other))
-    attn_ups.append(both_top[1] + after(attn_rest, attended, hyena_ups[-1], hyena_downs[-1]))
+    attended = merge(flags(level > 0), *own, after(partial_up, hyena_ups[0], hyena_other))
+    dep = [attended, hyena_ups[-1], hyena_downs[-1]]
+    attn_ups.append(after(attn_rest, *dep))
     for step in range(3, levels):
         attn_ups.append(climb(attn_ups[-1], 1, step))
-        attn_downs.append(climb(after(attn_downs[-1], hyena_downs[-1]), -1, step))
+        attn_downs.append(climb(after(attn_downs[-1], hyena_downs[-1], attended), -1, step))
     hyena_parts = [(hyena_pair, 0), (hyena_pair, 1), (hyena_other, 0), (hyena_other, 1)]
-    hyena_weights = hyena_ups[::-1] + [(both_up, 0), (weights, 0), (both_down, 0)] + hyena_downs
+
+    def blocks(layer, ups, downs, direct):
+        found = [
+            (weights, layer, 0, 0, levels - 1),
+            (both_up, layer, -1, 1, levels - 1),
+            (both_down, layer, 1, 0, levels - 2),
+            (ups[0], 0, -2, 2, levels - 2 if direct else levels - 1),
+        ]
+        if direct:
+            found.append((both_top, layer, -2, levels - 1, levels - 1))
+        found += [(w, 0, -k, k, levels - 1) for k, w in enumerate(ups[1:], 3)]
+        return found + [(w, 0, k, 0, levels - 1 - k) for k, w in enumerate(downs, 2)]
 
     def add_up(mine, others):
         gots = [
@@ -491,22 +505,22 @@
 
     where = flags(level, group)
     attn_one, attn_two = swap(attended, 1), swap(attended, 2)
-    hyena_terms = project(levels, n_tp, where, hyena_parts, hyena_weights)
-    attn_one, attn_two, *hyena_terms = lax.optimization_barrier(
-        (after(attn_one, attn_ups[0]), attn_two, *hyena_terms)
-    )
+    hyena_parts[0] = (after(hyena_parts[0][0], attn_ups[0]), 0)
+    hyena_blocks = blocks(0, hyena_ups, hyena_downs, False)
+    hyena_terms = project(levels, n_tp, where, hyena_parts, hyena_blocks, CHEAP)
+    attn_one, attn_two, attn_ups[0] = lax.optimization_barrier((attn_one, attn_two, attn_ups[0]))
+    hyena_pieces = add_up(*hyena_terms)
     half = PLANE // 2
     attn_three = [swap(attn_one[:half], 2), swap(attn_two[half:], 1)]
-    hyena_pieces = add_up(*hyena_terms)
-    attn_three, attn_ups[-1], attn_downs[-1], *hyena_pieces = lax.optimization_barrier(
-        (jnp.concatenate(attn_three, 0), attn_ups[-1], attn_downs[-1], *hyena_pieces)
-    )
+    hyena_pieces = [after(p, *attn_three) for p in hyena_pieces]
+    attn_three = jnp.concatenate(attn_three, 0)
     hyena_pieces = exchange(hyena_pieces)
-    attn_weights = attn_ups[::-1] + [(both_up, 1), (weights, 1), (both_down, 1)] + attn_downs
     attn_parts = [attended, attn_one, attn_two, attn_three]
-    attn_terms = project(levels, n_tp, where, attn_parts, attn_weights)
+    attn_blocks = blocks(1, attn_ups, attn_downs, True)
+    attn_terms = project(levels, n_tp, where, attn_parts, attn_blocks, CHEAP)
     hyena_pieces = [after(p, *attn_terms) for p in hyena_pieces]
-    attn_pieces = exchange(add_up(*attn_terms))
+    attn_pieces = add_up(*attn_terms)
+    attn_pieces = exchange(attn_pieces)
     return assemble(flags(me), hyena_pieces), assemble(flags(me), attn_pieces)
 
 

time: 259 us -> 249 us (0.961); the launches traced: 254 us -> 248 us
  waiting for transfers between devices: 96 us -> 85.8 us
  starting transfers between devices: 57.9 us -> 62.4 us
    ppermute x15, waiting for transfers between devices: 54.6 us -> 44.8 us  [swap(): return lax.ppermute(block, 'ctx', [(i, i ^ relative) for i in range(n_ctx)])]
    ppermute x15, starting transfers between devices: 14.5 us -> 23.6 us  [swap(): return lax.ppermute(block, 'ctx', [(i, i ^ relative) for i in range(n_ctx)])]
    ppermute x14, starting transfers between devices: 38.5 us -> 33.8 us  [move(): lax.ppermute(block, 'ctx', [(i, i + direction * PLANE) for i in sources])]
    unnamed x58 -> x48, local copies, waits for them, and re-layouts: 7.7 us -> 3.31 us
  transfers between devices with their start and end apart: 32 -> 32, of which waited for: 16 -> 13; matrix products, arithmetic and copies ran while one was open for 10% -> 12% of each run, Pallas kernels for 20% -> 25%
where the time goes in v4:
time: 249 us; the launch traced here: 248 us
  waiting for transfers between devices  85.8 us (34%)
  Pallas kernels  64 us (26%)
  starting transfers between devices  62.4 us (25%)
  local copies, waits for them, and re-layouts  20.4 us (8%)
  other arithmetic  14.3 us (6%)
    ppermute x15, waiting for transfers between devices, swap(): return lax.ppermute(block, 'ctx', [(i, i ^ relative) for i in range(n_ctx)])  44.8 us
    ppermute x14, waiting for transfers between devices, move(): lax.ppermute(block, 'ctx', [(i, i + direction * PLANE) for i in sources])  41 us
    ppermute x14, starting transfers between devices, move(): lax.ppermute(block, 'ctx', [(i, i + direction * PLANE) for i in sources])  33.8 us
    pallas_call x3, Pallas kernels, attend(): pl.pallas_call(functools.partial(attend_kernel, kind, not carry, last), g...  28.3 us
    ppermute x15, starting transfers between devices, swap(): return lax.ppermute(block, 'ctx', [(i, i ^ relative) for i in range(n_ctx)])  23.6 us
    pallas_call x2, Pallas kernels, project(): pl.pallas_call(functools.partial(project_kernel, levels, n_tp, [i for _,...  19.7 us
    pallas_call x1, Pallas kernels, fir(): pl.pallas_call(fir_kernel, grid=(width // tile,), in_specs=[column(taps),...  7.21 us
  transfers between devices with their start and end apart: 32, of which 13 were waited for; matrix products, arithmetic and copies ran while one was open for 12% of the time, Pallas kernels for 25%

profile of v4, /device:TPU:0, one launch (start us, length us, event | category | flops | bytes accessed | tf_op | source)
XLA Modules:
  0.0 248.0 jit_solution(2191232337992785070)
XLA Ops:
  2.8 4.9 %collective-permute-start = (bf16[128,2048]{1,0:T(8,128)(2,1)}, bf16[128,2048]{1,0:T(8,128)(2,1)S(1)}, u32[]{:S(2)}, u32[]{:S(2)}) collective-permute-start(bf16[128,2048]{1,0:T(8,128)(2,1)} %fusion.1), channel_id=1, source_target_pairs={{0,2},{2,4},{4,6},{6,8},{8,10},{10,12},{12,14},{14,16},{16,18},{18... | collective-permute-start | bytes 1572872 | tf_op jit(solution)/shard_map/ppermute | solution.py:421
  9.2 4.8 %collective-permute-start.5 = (bf16[2,2048,256]{2,1,0:T(8,128)(2,1)S(1)}, bf16[2,2048,256]{2,1,0:T(8,128)(2,1)}, u32[]{:S(2)}, u32[]{:S(2)}) collective-permute-start(bf16[2,2048,256]{2,1,0:T(8,128)(2,1)S(1)} %pad_maximum_fusion.refs_4_), channel_id=1, source_target_pairs={{0,8},{2,10},{4,12},{6,14},{8,16},{10,18},{12,20},{14,22},{16,24},... | collective-permute-start | bytes 6291464 | tf_op jit(solution)/shard_map/ppermute | solution.py:404
  25.3 7.2 %fir.1 = bf16[256,2048]{1,0:T(8,128)(2,1)} custom-call(bf16[128,2048]{1,0:T(8,128)(2,1)} %copy-done.17, bf16[256,2048]{1,0:T(8,128)(2,1)} %fusion.product, bf16[256,2048]{1,0:T(8,128)(2,1)} %slice_bitcast_fusion.4.gate, f32[128,2048]{1,0:T(8,128)} %filters.1, bf16[256,256]{1,0:T(8,128)(2,1)} %constant.62.clone.f_hi, bf16[256,256]{1,0:T(8,128)(2,1)} %constant.63.clone.f_lo, ...), custom_call_target="tpu_custom_call" | custom-call | flops 1 | bytes 1 | tf_op jit(solution)/shard_map/fir/pallas_call | solution.py:86
  32.5 6.6 %collective-permute-done.1 = bf16[3,256,512]{2,1,0:T(8,128)(2,1)} collective-permute-done((bf16[3,256,512]{2,1,0:T(8,128)(2,1)}, bf16[3,256,512]{2,1,0:T(8,128)(2,1)}, u32[]{:S(2)}, u32[]{:S(2)}) %collective-permute-start.1) | collective-permute-done | bytes 786464 | tf_op jit(solution)/shard_map/ppermute | solution.py:400
  39.1 15.5 %collective-permute-done.2 = bf16[3,256,512]{2,1,0:T(8,128)(2,1)} collective-permute-done((bf16[3,256,512]{2,1,0:T(8,128)(2,1)}, bf16[3,256,512]{2,1,0:T(8,128)(2,1)}, u32[]{:S(2)}, u32[]{:S(2)}) %collective-permute-start.2) | collective-permute-done | bytes 786464 | tf_op jit(solution)/shard_map/ppermute | solution.py:400
  57.3 6.1 %collective-permute-start.9 = (bf16[4,2,256,512]{3,2,1,0:T(8,128)(2,1)S(1)}, bf16[4,2,256,512]{3,2,1,0:T(8,128)(2,1)}, u32[]{:S(2)}, u32[]{:S(2)}) collective-permute-start(bf16[4,2,256,512]{3,2,1,0:T(8,128)(2,1)S(1)} %pad_maximum_fusion.1.k_ref.v_ref), channel_id=1, source_target_pairs={{0,8},{2,10},{4,12},{6,14},{8,16},{10,18},{12,20},{14,22},{1,9},{3... | collective-permute-start | bytes 6291464 | tf_op jit(solution)/shard_map/ppermute | solution.py:404
  70.4 10.0 %shard_map.104 = (f32[4,256,512]{2,1,0:T(8,128)}, f32[4,4,8,256]{3,2,1,0:T(8,128)}) custom-call(s32[2]{0:T(128)} %pad_add_fusion.1.info, bf16[4,256,512]{2,1,0:T(8,128)(2,1)} %pad_maximum_fusion.3.q_ref, bf16[4,2,256,512]{3,2,1,0:T(8,128)(2,1)} %copy-done, bf16[4,2,256,512]{3,2,1,0:T(8,128)(2,1)} %copy-done), custom_call_target="tpu_custom_call" | custom-call | flops 10000000000 | bytes 1 | tf_op jit(solution)/shard_map/pallas_call | solution.py:212
  85.5 9.9 %collective-permute-done.4.q_ref = bf16[4,256,512]{2,1,0:T(8,128)(2,1)} collective-permute-done((bf16[4,256,512]{2,1,0:T(8,128)(2,1)}, bf16[4,256,512]{2,1,0:T(8,128)(2,1)}, u32[]{:S(2)}, u32[]{:S(2)}) %collective-permute-start.4) | collective-permute-done | bytes 1048608 | tf_op jit(solution)/shard_map/ppermute | solution.py:404
  102.6 11.2 %shard_map.105 = (f32[4,256,512]{2,1,0:T(8,128)}, f32[4,256,512]{2,1,0:T(8,128)}) custom-call(s32[2]{0:T(128)} %pad_add_fusion.1.info, bf16[4,256,512]{2,1,0:T(8,128)(2,1)} %collective-permute-done.4.q_ref, bf16[4,2,256,512]{3,2,1,0:T(8,128)(2,1)} %copy-done, bf16[4,2,256,512]{3,2,1,0:T(8,128)(2,1)} %copy-done), custom_call_target="tpu_custom_call" | custom-call | flops 1 | bytes 1 | tf_op jit(solution)/shard_map/pallas_call | solution.py:212
  115.1 7.1 %shard_map.106 = bf16[4,272,512]{2,1,0:T(8,128)(2,1)} custom-call(s32[2]{0:T(128)} %pad_add_fusion.2.info, bf16[4,256,512]{2,1,0:T(8,128)(2,1)} %collective-permute-done.4.q_ref, bf16[4,2,256,512]{3,2,1,0:T(8,128)(2,1)} %collective-permute-done.9.k_ref.v_ref, bf16[4,2,256,512]{3,2,1,0:T(8,128)(2,1)} %collective-permute-done.9.k_ref.v_ref, ...), custom_call_target="tpu_custom_call" | custom-call | flops 10000000000 | bytes 1 | tf_op jit(solution)/shard_map/pallas_call | solution.py:212
  122.2 5.8 %collective-permute-done.11 = bf16[2048,256]{1,0:T(8,128)(2,1)} collective-permute-done((bf16[2048,256]{1,0:T(8,128)(2,1)}, bf16[2048,256]{1,0:T(8,128)(2,1)}, u32[]{:S(2)}, u32[]{:S(2)}) %collective-permute-start.11) | collective-permute-done | bytes 1048608 | tf_op jit(solution)/shard_map/ppermute | solution.py:404
  128.0 6.3 %collective-permute-start.13 = (bf16[4,272,512]{2,1,0:T(8,128)(2,1)}, bf16[4,272,512]{2,1,0:T(8,128)(2,1)}, u32[]{:S(2)}, u32[]{:S(2)}) collective-permute-start(bf16[4,272,512]{2,1,0:T(8,128)(2,1)} %shard_map.106), channel_id=1, source_target_pairs={{0,8},{2,10},{4,12},{6,14},{8,16},{10,18},{12,20},{14,22},{16,24},... | collective-permute-start | bytes 3342344 | tf_op jit(solution)/shard_map/ppermute | solution.py:404
  139.3 8.6 %collective-permute-done.16 = bf16[2048,256]{1,0:T(8,128)(2,1)S(1)} collective-permute-done((bf16[2048,256]{1,0:T(8,128)(2,1)}, bf16[2048,256]{1,0:T(8,128)(2,1)S(1)}, u32[]{:S(2)}, u32[]{:S(2)}) %collective-permute-start.16) | collective-permute-done | bytes 1048608 | tf_op jit(solution)/shard_map/ppermute | solution.py:404
  149.3 7.3 %collective-permute-done.13.two_ref = bf16[4,272,512]{2,1,0:T(8,128)(2,1)} collective-permute-done((bf16[4,272,512]{2,1,0:T(8,128)(2,1)}, bf16[4,272,512]{2,1,0:T(8,128)(2,1)}, u32[]{:S(2)}, u32[]{:S(2)}) %collective-permute-start.13) | collective-permute-done | bytes 1114144 | tf_op jit(solution)/shard_map/ppermute | solution.py:404
  156.6 4.2 %merge.1.refs_0_ = bf16[4,256,512]{2,1,0:T(8,128)(2,1)} custom-call(s32[1]{0:T(128)} %bitcast.25.info, f32[4,256,512]{2,1,0:T(8,128)} %get-tuple-element.76.one_ref, f32[4,4,8,256]{3,2,1,0:T(8,128)} %get-tuple-element.94.level_one, bf16[4,272,512]{2,1,0:T(8,128)(2,1)} %collective-permute-done.13.two_ref), custom_call_target="tpu_custom_call" | custom-call | flops 2000000000 | bytes 1 | tf_op jit(solution)/shard_map/merge/pallas_call | solution.py:244
  160.9 4.6 %collective-permute-start.20 = (bf16[4,256,512]{2,1,0:T(8,128)(2,1)}, bf16[4,256,512]{2,1,0:T(8,128)(2,1)S(1)}, u32[]{:S(2)}, u32[]{:S(2)}) collective-permute-start(bf16[4,256,512]{2,1,0:T(8,128)(2,1)} %merge.1.refs_0_), channel_id=1, source_target_pairs={{0,4},{2,6},{4,0},{6,2},{8,12},{10,14},{12,8},{14,10},{16,20},{18,... | collective-permute-start | bytes 3145736 | tf_op jit(solution)/shard_map/ppermute | solution.py:400
  165.6 7.1 %collective-permute-done.17 = bf16[2048,256]{1,0:T(8,128)(2,1)} collective-permute-done((bf16[2048,256]{1,0:T(8,128)(2,1)}, bf16[2048,256]{1,0:T(8,128)(2,1)}, u32[]{:S(2)}, u32[]{:S(2)}) %collective-permute-start.17) | collective-permute-done | bytes 1048608 | tf_op jit(solution)/shard_map/ppermute | solution.py:404
  175.6 8.7 %collective-permute-done.19.refs_1_ = bf16[4,256,512]{2,1,0:T(8,128)(2,1)S(1)} collective-permute-done((bf16[4,256,512]{2,1,0:T(8,128)(2,1)}, bf16[4,256,512]{2,1,0:T(8,128)(2,1)S(1)}, u32[]{:S(2)}, u32[]{:S(2)}) %collective-permute-start.19) | collective-permute-done | bytes 1048608 | tf_op jit(solution)/shard_map/ppermute | solution.py:400
  191.4 9.8 %project.2 = (bf16[4,2,256,256]{3,2,1,0:T(8,128)(2,1)}, bf16[1,4,2,256,256]{4,3,2,1,0:T(8,128)(2,1)}) custom-call(s32[2]{0:T(128)} %pad_add_fusion.info, bf16[2,256,2048]{2,1,0:T(8,128)(2,1)} %copy-done.3, bf16[2,256,2048]{2,1,0:T(8,128)(2,1)} %copy-done.3, bf16[2,256,2048]{2,1,0:T(8,128)(2,1)} %copy-done.4, bf16[2,256,2048]{2,1,0:T(8,128)(2,1)} %copy-done.4, ...), custom_call_target="tpu_custom_call" | custom-call | flops 1 | bytes 1 | tf_op jit(solution)/shard_map/project/pallas_call | solution.py:324
  206.0 9.9 %project.3 = (bf16[4,2,256,256]{3,2,1,0:T(8,128)(2,1)}, bf16[1,4,2,256,256]{4,3,2,1,0:T(8,128)(2,1)}) custom-call(s32[2]{0:T(128)} %pad_add_fusion.info, bf16[4,256,512]{2,1,0:T(8,128)(2,1)} %merge.1.refs_0_, bf16[4,256,512]{2,1,0:T(8,128)(2,1)} %copy-done.9, bf16[4,256,512]{2,1,0:T(8,128)(2,1)} %copy-done.10, ...), custom_call_target="tpu_custom_call" | custom-call | flops 1 | bytes 1 | tf_op jit(solution)/shard_map/project/pallas_call | solution.py:324
  216.9 4.5 %collective-permute-start.26 = (bf16[2,256,256]{2,1,0:T(8,128)(2,1)S(1)}, bf16[2,256,256]{2,1,0:T(8,128)(2,1)S(1)}, u32[]{:S(2)}, u32[]{:S(2)}) collective-permute-start(bf16[2,256,256]{2,1,0:T(8,128)(2,1)S(1)} %get-tuple-element.115), channel_id=1, source_target_pairs={{0,4},{2,6},{4,0},{6,2},{8,12},{10,14},{12,8},{14,10},{16,20},{18,... | collective-permute-start | bytes 786440 | tf_op jit(solution)/shard_map/ppermute | solution.py:400
  226.0 4.0 %collective-permute-start.31 = (bf16[2,256,256]{2,1,0:T(8,128)(2,1)S(1)}, bf16[2,256,256]{2,1,0:T(8,128)(2,1)S(1)}, u32[]{:S(2)}, u32[]{:S(2)}) collective-permute-start(bf16[2,256,256]{2,1,0:T(8,128)(2,1)S(1)} %get-tuple-element.123), channel_id=1, source_target_pairs={{0,6},{2,4},{4,2},{6,0},{8,14},{10,12},{12,10},{14,8},{16,22},{18,... | collective-permute-start | bytes 786440 | tf_op jit(solution)/shard_map/ppermute | solution.py:400
  230.0 4.2 %collective-permute-done.26.refs_2_ = bf16[2,256,256]{2,1,0:T(8,128)(2,1)S(1)} collective-permute-done((bf16[2,256,256]{2,1,0:T(8,128)(2,1)S(1)}, bf16[2,256,256]{2,1,0:T(8,128)(2,1)S(1)}, u32[]{:S(2)}, u32[]{:S(2)}) %collective-permute-start.26) | collective-permute-done | bytes 262176 | tf_op jit(solution)/shard_map/ppermute | solution.py:400
  237.8 7.1 %collective-permute-done.30.refs_2_ = bf16[2,256,256]{2,1,0:T(8,128)(2,1)S(1)} collective-permute-done((bf16[2,256,256]{2,1,0:T(8,128)(2,1)S(1)}, bf16[2,256,256]{2,1,0:T(8,128)(2,1)S(1)}, u32[]{:S(2)}, u32[]{:S(2)}) %collective-permute-start.30) | collective-permute-done | bytes 262176 | tf_op jit(solution)/shard_map/ppermute | solution.py:400
  (124 shorter events, 71.6 us)
Async XLA Ops:
  2.8 21.1 %collective-permute-start = (bf16[128,2048]{1,0:T(8,128)(2,1)}, bf16[128,2048]{1,0:T(8,128)(2,1)S(1)}, u32[]{:S(2)}, u32[]{:S(2)}) collective-permute-start(bf16[128,2048]{1,0:T(8,128)(2,1)} %fusion.1), channel_id=1, source_target_pairs={{0,2},{2,4},{4,6},{6,8},{8,10},{10,12},{12,14},{14,16},{16,18},{18... | collective-permute-start | bytes 1572872 | tf_op jit(solution)/shard_map/ppermute | solution.py:421
  9.2 71.3 %collective-permute-start.5 = (bf16[2,2048,256]{2,1,0:T(8,128)(2,1)S(1)}, bf16[2,2048,256]{2,1,0:T(8,128)(2,1)}, u32[]{:S(2)}, u32[]{:S(2)}) collective-permute-start(bf16[2,2048,256]{2,1,0:T(8,128)(2,1)S(1)} %pad_maximum_fusion.refs_4_), channel_id=1, source_target_pairs={{0,8},{2,10},{4,12},{6,14},{8,16},{10,18},{12,20},{14,22},{16,24},... | collective-permute-start | bytes 6291464 | tf_op jit(solution)/shard_map/ppermute | solution.py:404
  17.5 21.6 %collective-permute-start.1 = (bf16[3,256,512]{2,1,0:T(8,128)(2,1)}, bf16[3,256,512]{2,1,0:T(8,128)(2,1)}, u32[]{:S(2)}, u32[]{:S(2)}) collective-permute-start(bf16[3,256,512]{2,1,0:T(8,128)(2,1)} %get-tuple-element.64), channel_id=1, source_target_pairs={{0,2},{2,0},{4,6},{6,4},{8,10},{10,8},{12,14},{14,12},{16,18},{18,... | collective-permute-start | bytes 2359304 | tf_op jit(solution)/shard_map/ppermute | solution.py:400
  19.0 35.6 %collective-permute-start.2 = (bf16[3,256,512]{2,1,0:T(8,128)(2,1)}, bf16[3,256,512]{2,1,0:T(8,128)(2,1)}, u32[]{:S(2)}, u32[]{:S(2)}) collective-permute-start(bf16[3,256,512]{2,1,0:T(8,128)(2,1)} %get-tuple-element.65), channel_id=1, source_target_pairs={{0,4},{2,6},{4,0},{6,2},{8,12},{10,14},{12,8},{14,10},{16,20},{18,... | collective-permute-start | bytes 2359304 | tf_op jit(solution)/shard_map/ppermute | solution.py:400
  20.5 34.1 %collective-permute-start.3 = (bf16[3,256,512]{2,1,0:T(8,128)(2,1)}, bf16[3,256,512]{2,1,0:T(8,128)(2,1)}, u32[]{:S(2)}, u32[]{:S(2)}) collective-permute-start(bf16[3,256,512]{2,1,0:T(8,128)(2,1)} %get-tuple-element.66), channel_id=1, source_target_pairs={{0,6},{2,4},{4,2},{6,0},{8,14},{10,12},{12,10},{14,8},{16,22},{18,... | collective-permute-start | bytes 2359304 | tf_op jit(solution)/shard_map/ppermute | solution.py:400
  24.0 71.4 %collective-permute-start.6 = (bf16[2,2048,256]{2,1,0:T(8,128)(2,1)S(1)}, bf16[2,2048,256]{2,1,0:T(8,128)(2,1)S(1)}, u32[]{:S(2)}, u32[]{:S(2)}) collective-permute-start(bf16[2,2048,256]{2,1,0:T(8,128)(2,1)S(1)} %pad_maximum_fusion.refs_4_), channel_id=1, source_target_pairs={{8,0},{10,2},{12,4},{14,6},{16,8},{18,10},{20,12},{22,14},{24,16},... | collective-permute-start | bytes 6291464 | tf_op jit(solution)/shard_map/ppermute | solution.py:404
  57.3 56.4 %collective-permute-start.9 = (bf16[4,2,256,512]{3,2,1,0:T(8,128)(2,1)S(1)}, bf16[4,2,256,512]{3,2,1,0:T(8,128)(2,1)}, u32[]{:S(2)}, u32[]{:S(2)}) collective-permute-start(bf16[4,2,256,512]{3,2,1,0:T(8,128)(2,1)S(1)} %pad_maximum_fusion.1.k_ref.v_ref), channel_id=1, source_target_pairs={{0,8},{2,10},{4,12},{6,14},{8,16},{10,18},{12,20},{14,22},{1,9},{3... | collective-permute-start | bytes 6291464 | tf_op jit(solution)/shard_map/ppermute | solution.py:404
  68.5 27.0 %collective-permute-start.4 = (bf16[4,256,512]{2,1,0:T(8,128)(2,1)}, bf16[4,256,512]{2,1,0:T(8,128)(2,1)}, u32[]{:S(2)}, u32[]{:S(2)}) collective-permute-start(bf16[4,256,512]{2,1,0:T(8,128)(2,1)} %pad_maximum_fusion.3.q_ref), channel_id=1, source_target_pairs={{8,0},{10,2},{12,4},{14,6},{16,8},{18,10},{20,12},{22,14},{24,16},... | collective-permute-start | bytes 3145736 | tf_op jit(solution)/shard_map/ppermute | solution.py:404
  69.8 25.7 %collective-permute-start.7 = (bf16[256,2048]{1,0:T(8,128)(2,1)S(1)}, bf16[256,2048]{1,0:T(8,128)(2,1)}, u32[]{:S(2)}, u32[]{:S(2)}) collective-permute-start(bf16[256,2048]{1,0:T(8,128)(2,1)S(1)} %copy-done.6), channel_id=1, source_target_pairs={{0,2},{2,0},{4,6},{6,4},{8,10},{10,8},{12,14},{14,12},{16,18},{18,... | collective-permute-start | bytes 3145736 | tf_op jit(solution)/shard_map/ppermute | solution.py:400
  80.5 47.5 %collective-permute-start.10 = (bf16[2,2048,256]{2,1,0:T(8,128)(2,1)}, bf16[2,2048,256]{2,1,0:T(8,128)(2,1)}, u32[]{:S(2)}, u32[]{:S(2)}) collective-permute-start(bf16[2,2048,256]{2,1,0:T(8,128)(2,1)} %collective-permute-done.5.refs_5_), channel_id=1, source_target_pairs={{16,24},{18,26},{20,28},{22,30},{17,25},{19,27},{21,29},{23,31}} | collective-permute-start | bytes 6291464 | tf_op jit(solution)/shard_map/ppermute | solution.py:404
  95.4 32.6 %collective-permute-start.8 = (bf16[2048,256]{1,0:T(8,128)(2,1)}, bf16[2048,256]{1,0:T(8,128)(2,1)}, u32[]{:S(2)}, u32[]{:S(2)}) collective-permute-start(bf16[2048,256]{1,0:T(8,128)(2,1)} %get-tuple-element.85), channel_id=1, source_target_pairs={{8,16},{10,18},{12,20},{14,22},{9,17},{11,19},{13,21},{15,23}} | collective-permute-start | bytes 3145736 | tf_op jit(solution)/shard_map/ppermute | solution.py:404
  98.7 29.3 %collective-permute-start.11 = (bf16[2048,256]{1,0:T(8,128)(2,1)}, bf16[2048,256]{1,0:T(8,128)(2,1)}, u32[]{:S(2)}, u32[]{:S(2)}) collective-permute-start(bf16[2048,256]{1,0:T(8,128)(2,1)} %get-tuple-element.131), channel_id=1, source_target_pairs={{8,0},{10,2},{12,4},{14,6},{16,8},{18,10},{20,12},{22,14},{9,1},{1... | collective-permute-start | bytes 3145736 | tf_op jit(solution)/shard_map/ppermute | solution.py:404
  101.4 47.9 %collective-permute-start.14 = (bf16[2,256,2048]{2,1,0:T(8,128)(2,1)S(1)}, bf16[2,256,2048]{2,1,0:T(8,128)(2,1)S(1)}, u32[]{:S(2)}, u32[]{:S(2)}) collective-permute-start(bf16[2,256,2048]{2,1,0:T(8,128)(2,1)S(1)} %pad_maximum_fusion.2.refs_0_.refs_1_), channel_id=1, source_target_pairs={{0,4},{2,6},{4,0},{6,2},{8,12},{10,14},{12,8},{14,10},{16,20},{18,... | collective-permute-start | bytes 6291464 | tf_op jit(solution)/shard_map/ppermute | solution.py:400
  113.8 34.1 %collective-permute-start.16 = (bf16[2048,256]{1,0:T(8,128)(2,1)}, bf16[2048,256]{1,0:T(8,128)(2,1)S(1)}, u32[]{:S(2)}, u32[]{:S(2)}) collective-permute-start(bf16[2048,256]{1,0:T(8,128)(2,1)} %get-tuple-element.99), channel_id=1, source_target_pairs={{8,0},{10,2},{12,4},{14,6},{16,8},{18,10},{20,12},{22,14},{9,1},{1... | collective-permute-start | bytes 3145736 | tf_op jit(solution)/shard_map/ppermute | solution.py:404
  128.0 28.6 %collective-permute-start.13 = (bf16[4,272,512]{2,1,0:T(8,128)(2,1)}, bf16[4,272,512]{2,1,0:T(8,128)(2,1)}, u32[]{:S(2)}, u32[]{:S(2)}) collective-permute-start(bf16[4,272,512]{2,1,0:T(8,128)(2,1)} %shard_map.106), channel_id=1, source_target_pairs={{0,8},{2,10},{4,12},{6,14},{8,16},{10,18},{12,20},{14,22},{16,24},... | collective-permute-start | bytes 3342344 | tf_op jit(solution)/shard_map/ppermute | solution.py:404
  134.3 31.3 %collective-permute-start.12 = (bf16[2048,256]{1,0:T(8,128)(2,1)S(1)}, bf16[2048,256]{1,0:T(8,128)(2,1)}, u32[]{:S(2)}, u32[]{:S(2)}) collective-permute-start(bf16[2048,256]{1,0:T(8,128)(2,1)S(1)} %copy-done.16), channel_id=1, source_target_pairs={{8,16},{10,18},{12,20},{14,22},{9,17},{11,19},{13,21},{15,23}} | collective-permute-start | bytes 3145736 | tf_op jit(solution)/shard_map/ppermute | solution.py:404
  137.6 28.0 %collective-permute-start.15 = (bf16[2048,256]{1,0:T(8,128)(2,1)S(1)}, bf16[2048,256]{1,0:T(8,128)(2,1)}, u32[]{:S(2)}, u32[]{:S(2)}) collective-permute-start(bf16[2048,256]{1,0:T(8,128)(2,1)S(1)} %bitcast_add_fusion), channel_id=1, source_target_pairs={{16,24},{18,26},{20,28},{22,30},{17,25},{19,27},{21,29},{23,31}} | collective-permute-start | bytes 3145736 | tf_op jit(solution)/shard_map/ppermute | solution.py:404
  147.8 24.8 %collective-permute-start.17 = (bf16[2048,256]{1,0:T(8,128)(2,1)}, bf16[2048,256]{1,0:T(8,128)(2,1)}, u32[]{:S(2)}, u32[]{:S(2)}) collective-permute-start(bf16[2048,256]{1,0:T(8,128)(2,1)} %collective-permute-done.11), channel_id=1, source_target_pairs={{8,0},{10,2},{12,4},{14,6},{9,1},{11,3},{13,5},{15,7}} | collective-permute-start | bytes 3145736 | tf_op jit(solution)/shard_map/ppermute | solution.py:404
  160.8 23.5 %collective-permute-start.19 = (bf16[4,256,512]{2,1,0:T(8,128)(2,1)}, bf16[4,256,512]{2,1,0:T(8,128)(2,1)S(1)}, u32[]{:S(2)}, u32[]{:S(2)}) collective-permute-start(bf16[4,256,512]{2,1,0:T(8,128)(2,1)} %merge.1.refs_0_), channel_id=1, source_target_pairs={{0,2},{2,0},{4,6},{6,4},{8,10},{10,8},{12,14},{14,12},{16,18},{18,... | collective-permute-start | bytes 3145736 | tf_op jit(solution)/shard_map/ppermute | solution.py:400
  160.9 26.0 %collective-permute-start.20 = (bf16[4,256,512]{2,1,0:T(8,128)(2,1)}, bf16[4,256,512]{2,1,0:T(8,128)(2,1)S(1)}, u32[]{:S(2)}, u32[]{:S(2)}) collective-permute-start(bf16[4,256,512]{2,1,0:T(8,128)(2,1)} %merge.1.refs_0_), channel_id=1, source_target_pairs={{0,4},{2,6},{4,0},{6,2},{8,12},{10,14},{12,8},{14,10},{16,20},{18,... | collective-permute-start | bytes 3145736 | tf_op jit(solution)/shard_map/ppermute | solution.py:400
  172.7 31.0 %collective-permute-start.23 = (bf16[2048,256]{1,0:T(8,128)(2,1)}, bf16[2048,256]{1,0:T(8,128)(2,1)}, u32[]{:S(2)}, u32[]{:S(2)}) collective-permute-start(bf16[2048,256]{1,0:T(8,128)(2,1)} %collective-permute-done.12), channel_id=1, source_target_pairs={{16,24},{18,26},{20,28},{22,30},{17,25},{19,27},{21,29},{23,31}} | collective-permute-start | bytes 3145736 | tf_op jit(solution)/shard_map/ppermute | solution.py:404
  174.3 31.6 %collective-permute-start.24 = (bf16[2048,256]{1,0:T(8,128)(2,1)S(1)}, bf16[2048,256]{1,0:T(8,128)(2,1)}, u32[]{:S(2)}, u32[]{:S(2)}) collective-permute-start(bf16[2048,256]{1,0:T(8,128)(2,1)S(1)} %collective-permute-done.16), channel_id=1, source_target_pairs={{8,0},{10,2},{12,4},{14,6},{9,1},{11,3},{13,5},{15,7}} | collective-permute-start | bytes 3145736 | tf_op jit(solution)/shard_map/ppermute | solution.py:404
  223.9 21.0 %collective-permute-start.30 = (bf16[2,256,256]{2,1,0:T(8,128)(2,1)S(1)}, bf16[2,256,256]{2,1,0:T(8,128)(2,1)S(1)}, u32[]{:S(2)}, u32[]{:S(2)}) collective-permute-start(bf16[2,256,256]{2,1,0:T(8,128)(2,1)S(1)} %get-tuple-element.124), channel_id=1, source_target_pairs={{0,4},{2,6},{4,0},{6,2},{8,12},{10,14},{12,8},{14,10},{16,20},{18,... | collective-permute-start | bytes 786440 | tf_op jit(solution)/shard_map/ppermute | solution.py:400
  226.0 18.9 %collective-permute-start.31 = (bf16[2,256,256]{2,1,0:T(8,128)(2,1)S(1)}, bf16[2,256,256]{2,1,0:T(8,128)(2,1)S(1)}, u32[]{:S(2)}, u32[]{:S(2)}) collective-permute-start(bf16[2,256,256]{2,1,0:T(8,128)(2,1)S(1)} %get-tuple-element.123), channel_id=1, source_target_pairs={{0,6},{2,4},{4,2},{6,0},{8,14},{10,12},{12,10},{14,8},{16,22},{18,... | collective-permute-start | bytes 786440 | tf_op jit(solution)/shard_map/ppermute | solution.py:400
  (32 other events, 353.8 us)

commit v5 on v4

--- a/solution.py
+++ b/solution.py
@@ -269,15 +269,17 @@
     share = levels // n_tp
 
     loads = []
-    for s, (part, index) in enumerate(zip(parts, part_index)):
+    for part, (s, index, base) in zip(parts, part_index):
         if index is not None:
             copy = pltpu.make_async_copy(part.at[index], a.at[pl.ds(s * rows, rows)], sem_a.at[s])
             loads.append(copy)
             continue
         for r in range(plane):
+            if not base <= r ^ s < base + part.shape[0]:
+                continue
             loads.append(
                 pltpu.make_async_copy(
-                    part.at[r ^ s],
+                    part.at[(r ^ s) - base],
                     a.at[pl.ds(r * rows, rows), pl.ds(s * depth, depth)],
                     sem_a.at[s * plane + r],
                 )
@@ -315,7 +317,15 @@
 
 @jax.named_scope('project')
 def project(levels, n_tp, info, parts, weights, cost=CHEAP):
-    parts = [p if isinstance(p, tuple) else (p, None) for p in parts]
+    pieces = []
+    for s, part in enumerate(parts):
+        if isinstance(part, list):
+            pieces += [(p, s, None, i * p.shape[0]) for i, p in enumerate(part)]
+        elif isinstance(part, tuple):
+            pieces.append((part[0], s, part[1], 0))
+        else:
+            pieces.append((part, s, None, 0))
+    parts = pieces
     weights = [(w[0][None], 0, *w[2:]) if w[0].ndim == 2 else w for w in weights]
     width, columns = weights[0][0].shape[1:]
     rows = parts[0][0].shape[1]
@@ -323,7 +333,7 @@
     anywhere = pl.BlockSpec(memory_space=pl.ANY)
     return pl.pallas_call(
         functools.partial(
-            project_kernel, levels, n_tp, [i for _, i in parts], [w[1:] for w in weights]
+            project_kernel, levels, n_tp, [p[1:] for p in parts], [w[1:] for w in weights]
         ),
         grid_spec=pltpu.PrefetchScalarGridSpec(
             num_scalar_prefetch=1,
@@ -345,7 +355,7 @@
         ),
         compiler_params=pltpu.CompilerParams(vmem_limit_bytes=VMEM),
         cost_estimate=cost,
-    )(info, *[p for p, _ in parts], *[w[0] for w in weights])
+    )(info, *[p[0] for p in parts], *[w[0] for w in weights])
 
 
 def assemble_kernel(info, *refs):
@@ -513,7 +523,6 @@
     half = PLANE // 2
     attn_three = [swap(attn_one[:half], 2), swap(attn_two[half:], 1)]
     hyena_pieces = [after(p, *attn_three) for p in hyena_pieces]
-    attn_three = jnp.concatenate(attn_three, 0)
     hyena_pieces = exchange(hyena_pieces)
     attn_parts = [attended, attn_one, attn_two, attn_three]
     attn_blocks = blocks(1, attn_ups, attn_downs, True)

time: 249 us -> 249 us (level)
  transfers between devices with their start and end apart: 32 -> 32, of which waited for: 13 -> 13; matrix products, arithmetic and copies ran while one was open for 12% -> 11% of each run, Pallas kernels for 25% -> 25%
where the time goes in v5:
time: 249 us; the launch traced here: 248 us
  waiting for transfers between devices  88.1 us (35%)
  Pallas kernels  64.1 us (26%)
  starting transfers between devices  62.4 us (25%)
  local copies, waits for them, and re-layouts  20.4 us (8%)
  other arithmetic  12.1 us (5%)
    ppermute x15, waiting for transfers between devices, swap(): return lax.ppermute(block, 'ctx', [(i, i ^ relative) for i in range(n_ctx)])  44.8 us
    ppermute x14, waiting for transfers between devices, move(): lax.ppermute(block, 'ctx', [(i, i + direction * PLANE) for i in sources])  43.3 us
    ppermute x14, starting transfers between devices, move(): lax.ppermute(block, 'ctx', [(i, i + direction * PLANE) for i in sources])  33.8 us
    pallas_call x3, Pallas kernels, attend(): pl.pallas_call(functools.partial(attend_kernel, kind, not carry, last), g...  28.3 us
    ppermute x15, starting transfers between devices, swap(): return lax.ppermute(block, 'ctx', [(i, i ^ relative) for i in range(n_ctx)])  23.6 us
    pallas_call x2, Pallas kernels, project(): pl.pallas_call(functools.partial(project_kernel, levels, n_tp, [p[1:] for...  19.7 us
    pallas_call x1, Pallas kernels, fir(): pl.pallas_call(fir_kernel, grid=(width // tile,), in_specs=[column(taps),...  7.21 us
  transfers between devices with their start and end apart: 32, of which 13 were waited for; matrix products, arithmetic and copies ran while one was open for 11% of the time, Pallas kernels for 25%

profile of v5, /device:TPU:0, one launch (start us, length us, event | category | flops | bytes accessed | tf_op | source)
XLA Modules:
  0.0 248.1 jit_solution(8921599424735262782)
XLA Ops:
  2.8 4.9 %collective-permute-start = (bf16[128,2048]{1,0:T(8,128)(2,1)}, bf16[128,2048]{1,0:T(8,128)(2,1)S(1)}, u32[]{:S(2)}, u32[]{:S(2)}) collective-permute-start(bf16[128,2048]{1,0:T(8,128)(2,1)} %fusion.1), channel_id=1, source_target_pairs={{0,2},{2,4},{4,6},{6,8},{8,10},{10,12},{12,14},{14,16},{16,18},{18... | collective-permute-start | bytes 1572872 | tf_op jit(solution)/shard_map/ppermute | solution.py:431
  9.2 4.8 %collective-permute-start.5 = (bf16[2,2048,256]{2,1,0:T(8,128)(2,1)S(1)}, bf16[2,2048,256]{2,1,0:T(8,128)(2,1)}, u32[]{:S(2)}, u32[]{:S(2)}) collective-permute-start(bf16[2,2048,256]{2,1,0:T(8,128)(2,1)S(1)} %pad_maximum_fusion.refs_4_.refs_5_), channel_id=1, source_target_pairs={{0,8},{2,10},{4,12},{6,14},{8,16},{10,18},{12,20},{14,22},{16,24},... | collective-permute-start | bytes 6291464 | tf_op jit(solution)/shard_map/ppermute | solution.py:414
  25.3 7.2 %fir.1 = bf16[256,2048]{1,0:T(8,128)(2,1)} custom-call(bf16[128,2048]{1,0:T(8,128)(2,1)} %copy-done.17, bf16[256,2048]{1,0:T(8,128)(2,1)} %fusion.product, bf16[256,2048]{1,0:T(8,128)(2,1)} %slice_bitcast_fusion.4.gate, f32[128,2048]{1,0:T(8,128)} %filters.1, bf16[256,256]{1,0:T(8,128)(2,1)} %constant.62.clone.f_hi, bf16[256,256]{1,0:T(8,128)(2,1)} %constant.63.clone.f_lo, ...), custom_call_target="tpu_custom_call" | custom-call | flops 1 | bytes 1 | tf_op jit(solution)/shard_map/fir/pallas_call | solution.py:86
  32.5 6.6 %collective-permute-done.1 = bf16[3,256,512]{2,1,0:T(8,128)(2,1)} collective-permute-done((bf16[3,256,512]{2,1,0:T(8,128)(2,1)}, bf16[3,256,512]{2,1,0:T(8,128)(2,1)}, u32[]{:S(2)}, u32[]{:S(2)}) %collective-permute-start.1) | collective-permute-done | bytes 786464 | tf_op jit(solution)/shard_map/ppermute | solution.py:410
  39.1 15.5 %collective-permute-done.2 = bf16[3,256,512]{2,1,0:T(8,128)(2,1)} collective-permute-done((bf16[3,256,512]{2,1,0:T(8,128)(2,1)}, bf16[3,256,512]{2,1,0:T(8,128)(2,1)}, u32[]{:S(2)}, u32[]{:S(2)}) %collective-permute-start.2) | collective-permute-done | bytes 786464 | tf_op jit(solution)/shard_map/ppermute | solution.py:410
  57.3 6.1 %collective-permute-start.9 = (bf16[4,2,256,512]{3,2,1,0:T(8,128)(2,1)S(1)}, bf16[4,2,256,512]{3,2,1,0:T(8,128)(2,1)}, u32[]{:S(2)}, u32[]{:S(2)}) collective-permute-start(bf16[4,2,256,512]{3,2,1,0:T(8,128)(2,1)S(1)} %pad_maximum_fusion.1.k_ref.v_ref), channel_id=1, source_target_pairs={{0,8},{2,10},{4,12},{6,14},{8,16},{10,18},{12,20},{14,22},{1,9},{3... | collective-permute-start | bytes 6291464 | tf_op jit(solution)/shard_map/ppermute | solution.py:414
  70.4 10.0 %shard_map.104 = (f32[4,256,512]{2,1,0:T(8,128)}, f32[4,4,8,256]{3,2,1,0:T(8,128)}) custom-call(s32[2]{0:T(128)} %pad_add_fusion.1.info, bf16[4,256,512]{2,1,0:T(8,128)(2,1)} %pad_maximum_fusion.3.q_ref, bf16[4,2,256,512]{3,2,1,0:T(8,128)(2,1)} %copy-done, bf16[4,2,256,512]{3,2,1,0:T(8,128)(2,1)} %copy-done), custom_call_target="tpu_custom_call" | custom-call | flops 10000000000 | bytes 1 | tf_op jit(solution)/shard_map/pallas_call | solution.py:212
  85.5 9.9 %collective-permute-done.4.q_ref = bf16[4,256,512]{2,1,0:T(8,128)(2,1)} collective-permute-done((bf16[4,256,512]{2,1,0:T(8,128)(2,1)}, bf16[4,256,512]{2,1,0:T(8,128)(2,1)}, u32[]{:S(2)}, u32[]{:S(2)}) %collective-permute-start.4) | collective-permute-done | bytes 1048608 | tf_op jit(solution)/shard_map/ppermute | solution.py:414
  102.6 11.2 %shard_map.105 = (f32[4,256,512]{2,1,0:T(8,128)}, f32[4,256,512]{2,1,0:T(8,128)}) custom-call(s32[2]{0:T(128)} %pad_add_fusion.1.info, bf16[4,256,512]{2,1,0:T(8,128)(2,1)} %collective-permute-done.4.q_ref, bf16[4,2,256,512]{3,2,1,0:T(8,128)(2,1)} %copy-done, bf16[4,2,256,512]{3,2,1,0:T(8,128)(2,1)} %copy-done), custom_call_target="tpu_custom_call" | custom-call | flops 1 | bytes 1 | tf_op jit(solution)/shard_map/pallas_call | solution.py:212
  115.1 7.1 %shard_map.106 = bf16[4,272,512]{2,1,0:T(8,128)(2,1)} custom-call(s32[2]{0:T(128)} %pad_add_fusion.2.info, bf16[4,256,512]{2,1,0:T(8,128)(2,1)} %collective-permute-done.4.q_ref, bf16[4,2,256,512]{3,2,1,0:T(8,128)(2,1)} %collective-permute-done.9.k_ref.v_ref, bf16[4,2,256,512]{3,2,1,0:T(8,128)(2,1)} %collective-permute-done.9.k_ref.v_ref, ...), custom_call_target="tpu_custom_call" | custom-call | flops 10000000000 | bytes 1 | tf_op jit(solution)/shard_map/pallas_call | solution.py:212
  122.2 5.8 %collective-permute-done.11 = bf16[2048,256]{1,0:T(8,128)(2,1)} collective-permute-done((bf16[2048,256]{1,0:T(8,128)(2,1)}, bf16[2048,256]{1,0:T(8,128)(2,1)}, u32[]{:S(2)}, u32[]{:S(2)}) %collective-permute-start.11) | collective-permute-done | bytes 1048608 | tf_op jit(solution)/shard_map/ppermute | solution.py:414
  128.0 6.3 %collective-permute-start.13 = (bf16[4,272,512]{2,1,0:T(8,128)(2,1)}, bf16[4,272,512]{2,1,0:T(8,128)(2,1)}, u32[]{:S(2)}, u32[]{:S(2)}) collective-permute-start(bf16[4,272,512]{2,1,0:T(8,128)(2,1)} %shard_map.106), channel_id=1, source_target_pairs={{0,8},{2,10},{4,12},{6,14},{8,16},{10,18},{12,20},{14,22},{16,24},... | collective-permute-start | bytes 3342344 | tf_op jit(solution)/shard_map/ppermute | solution.py:414
  139.3 8.6 %collective-permute-done.16 = bf16[2048,256]{1,0:T(8,128)(2,1)S(1)} collective-permute-done((bf16[2048,256]{1,0:T(8,128)(2,1)}, bf16[2048,256]{1,0:T(8,128)(2,1)S(1)}, u32[]{:S(2)}, u32[]{:S(2)}) %collective-permute-start.16) | collective-permute-done | bytes 1048608 | tf_op jit(solution)/shard_map/ppermute | solution.py:414
  149.3 7.3 %collective-permute-done.13.two_ref = bf16[4,272,512]{2,1,0:T(8,128)(2,1)} collective-permute-done((bf16[4,272,512]{2,1,0:T(8,128)(2,1)}, bf16[4,272,512]{2,1,0:T(8,128)(2,1)}, u32[]{:S(2)}, u32[]{:S(2)}) %collective-permute-start.13) | collective-permute-done | bytes 1114144 | tf_op jit(solution)/shard_map/ppermute | solution.py:414
  156.6 4.2 %merge.1.refs_0_ = bf16[4,256,512]{2,1,0:T(8,128)(2,1)} custom-call(s32[1]{0:T(128)} %bitcast.25.info, f32[4,256,512]{2,1,0:T(8,128)} %get-tuple-element.76.one_ref, f32[4,4,8,256]{3,2,1,0:T(8,128)} %get-tuple-element.94.level_one, bf16[4,272,512]{2,1,0:T(8,128)(2,1)} %collective-permute-done.13.two_ref), custom_call_target="tpu_custom_call" | custom-call | flops 2000000000 | bytes 1 | tf_op jit(solution)/shard_map/merge/pallas_call | solution.py:244
  160.9 4.6 %collective-permute-start.20 = (bf16[4,256,512]{2,1,0:T(8,128)(2,1)}, bf16[4,256,512]{2,1,0:T(8,128)(2,1)S(1)}, u32[]{:S(2)}, u32[]{:S(2)}) collective-permute-start(bf16[4,256,512]{2,1,0:T(8,128)(2,1)} %merge.1.refs_0_), channel_id=1, source_target_pairs={{0,4},{2,6},{4,0},{6,2},{8,12},{10,14},{12,8},{14,10},{16,20},{18,... | collective-permute-start | bytes 3145736 | tf_op jit(solution)/shard_map/ppermute | solution.py:410
  165.6 7.1 %collective-permute-done.17 = bf16[2048,256]{1,0:T(8,128)(2,1)} collective-permute-done((bf16[2048,256]{1,0:T(8,128)(2,1)}, bf16[2048,256]{1,0:T(8,128)(2,1)}, u32[]{:S(2)}, u32[]{:S(2)}) %collective-permute-start.17) | collective-permute-done | bytes 1048608 | tf_op jit(solution)/shard_map/ppermute | solution.py:414
  175.6 8.7 %collective-permute-done.19.refs_1_ = bf16[4,256,512]{2,1,0:T(8,128)(2,1)S(1)} collective-permute-done((bf16[4,256,512]{2,1,0:T(8,128)(2,1)}, bf16[4,256,512]{2,1,0:T(8,128)(2,1)S(1)}, u32[]{:S(2)}, u32[]{:S(2)}) %collective-permute-start.19) | collective-permute-done | bytes 1048608 | tf_op jit(solution)/shard_map/ppermute | solution.py:410
  191.4 9.8 %project.2 = (bf16[4,2,256,256]{3,2,1,0:T(8,128)(2,1)}, bf16[1,4,2,256,256]{4,3,2,1,0:T(8,128)(2,1)}) custom-call(s32[2]{0:T(128)} %pad_add_fusion.info, bf16[2,256,2048]{2,1,0:T(8,128)(2,1)} %copy-done.3, bf16[2,256,2048]{2,1,0:T(8,128)(2,1)} %copy-done.3, bf16[2,256,2048]{2,1,0:T(8,128)(2,1)} %copy-done.4, bf16[2,256,2048]{2,1,0:T(8,128)(2,1)} %copy-done.4, ...), custom_call_target="tpu_custom_call" | custom-call | flops 1 | bytes 1 | tf_op jit(solution)/shard_map/project/pallas_call | solution.py:334
  201.4 4.6 %collective-permute-done.24 = bf16[2048,256]{1,0:T(8,128)(2,1)} collective-permute-done((bf16[2048,256]{1,0:T(8,128)(2,1)S(1)}, bf16[2048,256]{1,0:T(8,128)(2,1)}, u32[]{:S(2)}, u32[]{:S(2)}) %collective-permute-start.24) | collective-permute-done | bytes 1048608 | tf_op jit(solution)/shard_map/ppermute | solution.py:414
  206.0 9.9 %project.3 = (bf16[4,2,256,256]{3,2,1,0:T(8,128)(2,1)}, bf16[1,4,2,256,256]{4,3,2,1,0:T(8,128)(2,1)}) custom-call(s32[2]{0:T(128)} %pad_add_fusion.info, bf16[4,256,512]{2,1,0:T(8,128)(2,1)} %merge.1.refs_0_, bf16[4,256,512]{2,1,0:T(8,128)(2,1)} %copy-done.9, bf16[4,256,512]{2,1,0:T(8,128)(2,1)} %copy-done.10, ...), custom_call_target="tpu_custom_call" | custom-call | flops 1 | bytes 1 | tf_op jit(solution)/shard_map/project/pallas_call | solution.py:334
  217.0 4.5 %collective-permute-start.26 = (bf16[2,256,256]{2,1,0:T(8,128)(2,1)S(1)}, bf16[2,256,256]{2,1,0:T(8,128)(2,1)S(1)}, u32[]{:S(2)}, u32[]{:S(2)}) collective-permute-start(bf16[2,256,256]{2,1,0:T(8,128)(2,1)S(1)} %get-tuple-element.115), channel_id=1, source_target_pairs={{0,4},{2,6},{4,0},{6,2},{8,12},{10,14},{12,8},{14,10},{16,20},{18,... | collective-permute-start | bytes 786440 | tf_op jit(solution)/shard_map/ppermute | solution.py:410
  230.0 4.2 %collective-permute-done.26.refs_2_ = bf16[2,256,256]{2,1,0:T(8,128)(2,1)S(1)} collective-permute-done((bf16[2,256,256]{2,1,0:T(8,128)(2,1)S(1)}, bf16[2,256,256]{2,1,0:T(8,128)(2,1)S(1)}, u32[]{:S(2)}, u32[]{:S(2)}) %collective-permute-start.26) | collective-permute-done | bytes 262176 | tf_op jit(solution)/shard_map/ppermute | solution.py:410
  237.9 7.1 %collective-permute-done.30.refs_2_ = bf16[2,256,256]{2,1,0:T(8,128)(2,1)S(1)} collective-permute-done((bf16[2,256,256]{2,1,0:T(8,128)(2,1)S(1)}, bf16[2,256,256]{2,1,0:T(8,128)(2,1)S(1)}, u32[]{:S(2)}, u32[]{:S(2)}) %collective-permute-start.30) | collective-permute-done | bytes 262176 | tf_op jit(solution)/shard_map/ppermute | solution.py:410
  (123 shorter events, 71.0 us)
Async XLA Ops:
  2.8 21.1 %collective-permute-start = (bf16[128,2048]{1,0:T(8,128)(2,1)}, bf16[128,2048]{1,0:T(8,128)(2,1)S(1)}, u32[]{:S(2)}, u32[]{:S(2)}) collective-permute-start(bf16[128,2048]{1,0:T(8,128)(2,1)} %fusion.1), channel_id=1, source_target_pairs={{0,2},{2,4},{4,6},{6,8},{8,10},{10,12},{12,14},{14,16},{16,18},{18... | collective-permute-start | bytes 1572872 | tf_op jit(solution)/shard_map/ppermute | solution.py:431
  9.2 71.3 %collective-permute-start.5 = (bf16[2,2048,256]{2,1,0:T(8,128)(2,1)S(1)}, bf16[2,2048,256]{2,1,0:T(8,128)(2,1)}, u32[]{:S(2)}, u32[]{:S(2)}) collective-permute-start(bf16[2,2048,256]{2,1,0:T(8,128)(2,1)S(1)} %pad_maximum_fusion.refs_4_.refs_5_), channel_id=1, source_target_pairs={{0,8},{2,10},{4,12},{6,14},{8,16},{10,18},{12,20},{14,22},{16,24},... | collective-permute-start | bytes 6291464 | tf_op jit(solution)/shard_map/ppermute | solution.py:414
  17.5 21.6 %collective-permute-start.1 = (bf16[3,256,512]{2,1,0:T(8,128)(2,1)}, bf16[3,256,512]{2,1,0:T(8,128)(2,1)}, u32[]{:S(2)}, u32[]{:S(2)}) collective-permute-start(bf16[3,256,512]{2,1,0:T(8,128)(2,1)} %get-tuple-element.64), channel_id=1, source_target_pairs={{0,2},{2,0},{4,6},{6,4},{8,10},{10,8},{12,14},{14,12},{16,18},{18,... | collective-permute-start | bytes 2359304 | tf_op jit(solution)/shard_map/ppermute | solution.py:410
  19.0 35.6 %collective-permute-start.2 = (bf16[3,256,512]{2,1,0:T(8,128)(2,1)}, bf16[3,256,512]{2,1,0:T(8,128)(2,1)}, u32[]{:S(2)}, u32[]{:S(2)}) collective-permute-start(bf16[3,256,512]{2,1,0:T(8,128)(2,1)} %get-tuple-element.65), channel_id=1, source_target_pairs={{0,4},{2,6},{4,0},{6,2},{8,12},{10,14},{12,8},{14,10},{16,20},{18,... | collective-permute-start | bytes 2359304 | tf_op jit(solution)/shard_map/ppermute | solution.py:410
  20.5 34.1 %collective-permute-start.3 = (bf16[3,256,512]{2,1,0:T(8,128)(2,1)}, bf16[3,256,512]{2,1,0:T(8,128)(2,1)}, u32[]{:S(2)}, u32[]{:S(2)}) collective-permute-start(bf16[3,256,512]{2,1,0:T(8,128)(2,1)} %get-tuple-element.66), channel_id=1, source_target_pairs={{0,6},{2,4},{4,2},{6,0},{8,14},{10,12},{12,10},{14,8},{16,22},{18,... | collective-permute-start | bytes 2359304 | tf_op jit(solution)/shard_map/ppermute | solution.py:410
  24.0 71.4 %collective-permute-start.6 = (bf16[2,2048,256]{2,1,0:T(8,128)(2,1)S(1)}, bf16[2,2048,256]{2,1,0:T(8,128)(2,1)S(1)}, u32[]{:S(2)}, u32[]{:S(2)}) collective-permute-start(bf16[2,2048,256]{2,1,0:T(8,128)(2,1)S(1)} %pad_maximum_fusion.refs_4_.refs_5_), channel_id=1, source_target_pairs={{8,0},{10,2},{12,4},{14,6},{16,8},{18,10},{20,12},{22,14},{24,16},... | collective-permute-start | bytes 6291464 | tf_op jit(solution)/shard_map/ppermute | solution.py:414
  57.3 56.4 %collective-permute-start.9 = (bf16[4,2,256,512]{3,2,1,0:T(8,128)(2,1)S(1)}, bf16[4,2,256,512]{3,2,1,0:T(8,128)(2,1)}, u32[]{:S(2)}, u32[]{:S(2)}) collective-permute-start(bf16[4,2,256,512]{3,2,1,0:T(8,128)(2,1)S(1)} %pad_maximum_fusion.1.k_ref.v_ref), channel_id=1, source_target_pairs={{0,8},{2,10},{4,12},{6,14},{8,16},{10,18},{12,20},{14,22},{1,9},{3... | collective-permute-start | bytes 6291464 | tf_op jit(solution)/shard_map/ppermute | solution.py:414
  68.5 27.0 %collective-permute-start.4 = (bf16[4,256,512]{2,1,0:T(8,128)(2,1)}, bf16[4,256,512]{2,1,0:T(8,128)(2,1)}, u32[]{:S(2)}, u32[]{:S(2)}) collective-permute-start(bf16[4,256,512]{2,1,0:T(8,128)(2,1)} %pad_maximum_fusion.3.q_ref), channel_id=1, source_target_pairs={{8,0},{10,2},{12,4},{14,6},{16,8},{18,10},{20,12},{22,14},{24,16},... | collective-permute-start | bytes 3145736 | tf_op jit(solution)/shard_map/ppermute | solution.py:414
  69.8 25.7 %collective-permute-start.7 = (bf16[256,2048]{1,0:T(8,128)(2,1)S(1)}, bf16[256,2048]{1,0:T(8,128)(2,1)}, u32[]{:S(2)}, u32[]{:S(2)}) collective-permute-start(bf16[256,2048]{1,0:T(8,128)(2,1)S(1)} %copy-done.6), channel_id=1, source_target_pairs={{0,2},{2,0},{4,6},{6,4},{8,10},{10,8},{12,14},{14,12},{16,18},{18,... | collective-permute-start | bytes 3145736 | tf_op jit(solution)/shard_map/ppermute | solution.py:410
  80.5 47.5 %collective-permute-start.10 = (bf16[2,2048,256]{2,1,0:T(8,128)(2,1)}, bf16[2,2048,256]{2,1,0:T(8,128)(2,1)}, u32[]{:S(2)}, u32[]{:S(2)}) collective-permute-start(bf16[2,2048,256]{2,1,0:T(8,128)(2,1)} %collective-permute-done.5.refs_5_.refs_6_), channel_id=1, source_target_pairs={{16,24},{18,26},{20,28},{22,30},{17,25},{19,27},{21,29},{23,31}} | collective-permute-start | bytes 6291464 | tf_op jit(solution)/shard_map/ppermute | solution.py:414
  95.4 32.6 %collective-permute-start.8 = (bf16[2048,256]{1,0:T(8,128)(2,1)}, bf16[2048,256]{1,0:T(8,128)(2,1)}, u32[]{:S(2)}, u32[]{:S(2)}) collective-permute-start(bf16[2048,256]{1,0:T(8,128)(2,1)} %get-tuple-element.85), channel_id=1, source_target_pairs={{8,16},{10,18},{12,20},{14,22},{9,17},{11,19},{13,21},{15,23}} | collective-permute-start | bytes 3145736 | tf_op jit(solution)/shard_map/ppermute | solution.py:414
  98.7 29.3 %collective-permute-start.11 = (bf16[2048,256]{1,0:T(8,128)(2,1)}, bf16[2048,256]{1,0:T(8,128)(2,1)}, u32[]{:S(2)}, u32[]{:S(2)}) collective-permute-start(bf16[2048,256]{1,0:T(8,128)(2,1)} %get-tuple-element.131), channel_id=1, source_target_pairs={{8,0},{10,2},{12,4},{14,6},{16,8},{18,10},{20,12},{22,14},{9,1},{1... | collective-permute-start | bytes 3145736 | tf_op jit(solution)/shard_map/ppermute | solution.py:414
  101.4 47.9 %collective-permute-start.14 = (bf16[2,256,2048]{2,1,0:T(8,128)(2,1)S(1)}, bf16[2,256,2048]{2,1,0:T(8,128)(2,1)S(1)}, u32[]{:S(2)}, u32[]{:S(2)}) collective-permute-start(bf16[2,256,2048]{2,1,0:T(8,128)(2,1)S(1)} %pad_maximum_fusion.2.refs_0_.refs_1_), channel_id=1, source_target_pairs={{0,4},{2,6},{4,0},{6,2},{8,12},{10,14},{12,8},{14,10},{16,20},{18,... | collective-permute-start | bytes 6291464 | tf_op jit(solution)/shard_map/ppermute | solution.py:410
  113.8 34.1 %collective-permute-start.16 = (bf16[2048,256]{1,0:T(8,128)(2,1)}, bf16[2048,256]{1,0:T(8,128)(2,1)S(1)}, u32[]{:S(2)}, u32[]{:S(2)}) collective-permute-start(bf16[2048,256]{1,0:T(8,128)(2,1)} %get-tuple-element.99), channel_id=1, source_target_pairs={{8,0},{10,2},{12,4},{14,6},{16,8},{18,10},{20,12},{22,14},{9,1},{1... | collective-permute-start | bytes 3145736 | tf_op jit(solution)/shard_map/ppermute | solution.py:414
  128.0 28.6 %collective-permute-start.13 = (bf16[4,272,512]{2,1,0:T(8,128)(2,1)}, bf16[4,272,512]{2,1,0:T(8,128)(2,1)}, u32[]{:S(2)}, u32[]{:S(2)}) collective-permute-start(bf16[4,272,512]{2,1,0:T(8,128)(2,1)} %shard_map.106), channel_id=1, source_target_pairs={{0,8},{2,10},{4,12},{6,14},{8,16},{10,18},{12,20},{14,22},{16,24},... | collective-permute-start | bytes 3342344 | tf_op jit(solution)/shard_map/ppermute | solution.py:414
  134.3 31.3 %collective-permute-start.12 = (bf16[2048,256]{1,0:T(8,128)(2,1)S(1)}, bf16[2048,256]{1,0:T(8,128)(2,1)}, u32[]{:S(2)}, u32[]{:S(2)}) collective-permute-start(bf16[2048,256]{1,0:T(8,128)(2,1)S(1)} %copy-done.16), channel_id=1, source_target_pairs={{8,16},{10,18},{12,20},{14,22},{9,17},{11,19},{13,21},{15,23}} | collective-permute-start | bytes 3145736 | tf_op jit(solution)/shard_map/ppermute | solution.py:414
  137.6 28.0 %collective-permute-start.15 = (bf16[2048,256]{1,0:T(8,128)(2,1)S(1)}, bf16[2048,256]{1,0:T(8,128)(2,1)}, u32[]{:S(2)}, u32[]{:S(2)}) collective-permute-start(bf16[2048,256]{1,0:T(8,128)(2,1)S(1)} %bitcast_add_fusion), channel_id=1, source_target_pairs={{16,24},{18,26},{20,28},{22,30},{17,25},{19,27},{21,29},{23,31}} | collective-permute-start | bytes 3145736 | tf_op jit(solution)/shard_map/ppermute | solution.py:414
  147.8 24.8 %collective-permute-start.17 = (bf16[2048,256]{1,0:T(8,128)(2,1)}, bf16[2048,256]{1,0:T(8,128)(2,1)}, u32[]{:S(2)}, u32[]{:S(2)}) collective-permute-start(bf16[2048,256]{1,0:T(8,128)(2,1)} %collective-permute-done.11), channel_id=1, source_target_pairs={{8,0},{10,2},{12,4},{14,6},{9,1},{11,3},{13,5},{15,7}} | collective-permute-start | bytes 3145736 | tf_op jit(solution)/shard_map/ppermute | solution.py:414
  160.8 23.5 %collective-permute-start.19 = (bf16[4,256,512]{2,1,0:T(8,128)(2,1)}, bf16[4,256,512]{2,1,0:T(8,128)(2,1)S(1)}, u32[]{:S(2)}, u32[]{:S(2)}) collective-permute-start(bf16[4,256,512]{2,1,0:T(8,128)(2,1)} %merge.1.refs_0_), channel_id=1, source_target_pairs={{0,2},{2,0},{4,6},{6,4},{8,10},{10,8},{12,14},{14,12},{16,18},{18,... | collective-permute-start | bytes 3145736 | tf_op jit(solution)/shard_map/ppermute | solution.py:410
  160.9 26.0 %collective-permute-start.20 = (bf16[4,256,512]{2,1,0:T(8,128)(2,1)}, bf16[4,256,512]{2,1,0:T(8,128)(2,1)S(1)}, u32[]{:S(2)}, u32[]{:S(2)}) collective-permute-start(bf16[4,256,512]{2,1,0:T(8,128)(2,1)} %merge.1.refs_0_), channel_id=1, source_target_pairs={{0,4},{2,6},{4,0},{6,2},{8,12},{10,14},{12,8},{14,10},{16,20},{18,... | collective-permute-start | bytes 3145736 | tf_op jit(solution)/shard_map/ppermute | solution.py:410
  172.7 28.7 %collective-permute-start.23 = (bf16[2048,256]{1,0:T(8,128)(2,1)}, bf16[2048,256]{1,0:T(8,128)(2,1)}, u32[]{:S(2)}, u32[]{:S(2)}) collective-permute-start(bf16[2048,256]{1,0:T(8,128)(2,1)} %collective-permute-done.12), channel_id=1, source_target_pairs={{16,24},{18,26},{20,28},{22,30},{17,25},{19,27},{21,29},{23,31}} | collective-permute-start | bytes 3145736 | tf_op jit(solution)/shard_map/ppermute | solution.py:414
  174.3 31.6 %collective-permute-start.24 = (bf16[2048,256]{1,0:T(8,128)(2,1)S(1)}, bf16[2048,256]{1,0:T(8,128)(2,1)}, u32[]{:S(2)}, u32[]{:S(2)}) collective-permute-start(bf16[2048,256]{1,0:T(8,128)(2,1)S(1)} %collective-permute-done.16), channel_id=1, source_target_pairs={{8,0},{10,2},{12,4},{14,6},{9,1},{11,3},{13,5},{15,7}} | collective-permute-start | bytes 3145736 | tf_op jit(solution)/shard_map/ppermute | solution.py:414
  224.0 21.0 %collective-permute-start.30 = (bf16[2,256,256]{2,1,0:T(8,128)(2,1)S(1)}, bf16[2,256,256]{2,1,0:T(8,128)(2,1)S(1)}, u32[]{:S(2)}, u32[]{:S(2)}) collective-permute-start(bf16[2,256,256]{2,1,0:T(8,128)(2,1)S(1)} %get-tuple-element.124), channel_id=1, source_target_pairs={{0,4},{2,6},{4,0},{6,2},{8,12},{10,14},{12,8},{14,10},{16,20},{18,... | collective-permute-start | bytes 786440 | tf_op jit(solution)/shard_map/ppermute | solution.py:410
  226.1 18.9 %collective-permute-start.31 = (bf16[2,256,256]{2,1,0:T(8,128)(2,1)S(1)}, bf16[2,256,256]{2,1,0:T(8,128)(2,1)S(1)}, u32[]{:S(2)}, u32[]{:S(2)}) collective-permute-start(bf16[2,256,256]{2,1,0:T(8,128)(2,1)S(1)} %get-tuple-element.123), channel_id=1, source_target_pairs={{0,6},{2,4},{4,2},{6,0},{8,14},{10,12},{12,10},{14,8},{16,22},{18,... | collective-permute-start | bytes 786440 | tf_op jit(solution)/shard_map/ppermute | solution.py:410
  (32 other events, 363.2 us)
